TPU v7x, 128 devices: a whole 4x4x4 slice. The times are simulated.
128 devices in a mesh: rows: 32 (over z, x, core), cols: 4 (over y).
Axes of the slice: x: 4, y: 4, z: 4, core: 2. Of those that a mesh axis runs over, the one named last changes fastest.
Arguments:
- panel_cols: float32 [262144, 256], P(('rows', 'cols')), may hold values from -10000 to 10000, as said below
- trailing: float32 [262144, 1024], P('rows', 'cols'), may hold values from -200000 to 200000
Outputs:
- r_factor: float32 [256, 256], replicated
- r_cross: float32 [256, 1024], P(None, 'cols')
- updated: float32 [262144, 1024], P('rows', 'cols')
Inputs may be any that keep to these rules, and one draw needn't show every extreme that they name: panel_cols has full column rank.
All inputs are finite; a program needn't handle non-finite values.
Results may differ from a plain program's by a relative error of at most 0.0003.
Values sent between devices are 32-bit elements; how exact they have to be, the bound alone decides.
No kernel may reach another device: no remote copies, remote signals or barrier semaphores. Data moves between devices by JAX's collectives and lax.ppermute only.
A program may use at most 128 MiB of HBM per device.

v0:
```python
import math

import jax
import jax.numpy as jnp
from jax import lax
from jax.sharding import PartitionSpec as P


def matmul(left, right):
    return jnp.dot(left, right, precision=lax.Precision.HIGHEST)


def lower_factor(gram_sum):
    return jnp.linalg.cholesky(gram_sum)


def lower_inverse(lower):
    identity = jnp.eye(lower.shape[0], dtype=jnp.float32)
    return jax.scipy.linalg.solve_triangular(lower, identity, lower=True)


def local(panel_cols, trailing):
    rows_total = trailing.shape[0] * lax.axis_size("rows")
    shrink = 1.0 / math.sqrt(rows_total)
    gram_sum = lax.psum(matmul(panel_cols.T, panel_cols), ("rows", "cols"))
    lower = lower_factor(gram_sum)
    inverse = lower_inverse(lower)
    basis_part = matmul(panel_cols, inverse.T)
    orthonormal = lax.all_gather(basis_part, "cols", axis=0, tiled=True)
    coupling = lax.psum(matmul(orthonormal.T, trailing), "rows")
    updated = trailing - matmul(orthonormal, coupling)
    return (lower.T * shrink, coupling * shrink, updated)


def solution(mesh):
    in_specs = (P(("rows", "cols"), None), P("rows", "cols"))
    out_specs = (P(), P(None, "cols"), P("rows", "cols"))
    return jax.shard_map(local, mesh=mesh, in_specs=in_specs, out_specs=out_specs, check_vma=False)
```

profile of v0, /device:TPU:1, one launch (start us, length us, event | category | flops | bytes accessed | tf_op | source)
XLA Modules:
  0.0 447.2 jit_solution(1440533770498955808)
XLA Ops:
  7.2 0.0 all-reduce.4.cloned.1.call-start
  7.2 1.5 copy-done
  8.8 4.2 fusion.14
  12.9 0.0 all-reduce.4.cloned.1.call-update
  12.9 0.2 all-gather.2.cloned.1.call-start
  13.2 145.0 %all-reduce.4.cloned.1.call-done = f32[256,256]{0,1:T(8,128)} async-done(((f32[256,256]{0,1:T(8,128)}), f32[256,256]{0,1:T(8,128)}) %all-reduce.4.cloned.1.call-update) | async-done | bytes 262160 | tf_op jit(solution)/shard_map/psum | solution.py:25
  158.2 1.1 copy.6
  159.3 1.0 fusion.3
  160.3 11.7 %cholesky.50 = f32[128,128]{1,0:T(8,128)S(1)} custom-call(f32[128,128]{1,0:T(8,128)S(1)} %cholesky.118), custom_call_target="Cholesky" | custom-call | tf_op jit(solution)/shard_map/jit(cholesky)/cholesky | solution.py:14
  172.0 9.8 %custom-call.15 = f32[1,128,128]{1,2,0:T(8,128)S(1)} custom-call(f32[1,128,128]{2,1,0:T(8,128)S(1)} %get-tuple-element.29), custom_call_target="InvertDiagBlocksLowerTriangular" | custom-call | tf_op jit(solution)/shard_map/jit(cholesky)/cholesky | solution.py:14
  181.9 0.2 constant_dynamic-update-slice_fusion.1
  182.1 0.3 convolution_subtract_fusion.2
  182.3 11.7 %cholesky.105 = f32[128,128]{1,0:T(8,128)S(1)} custom-call(f32[128,128]{1,0:T(8,128)S(1)} %convolution_subtract_fusion.2), custom_call_target="Cholesky" | custom-call | tf_op jit(solution)/shard_map/jit(cholesky)/cholesky | solution.py:14
  194.1 0.6 compare_reduce_fusion
  196.1 0.1 triangular_solve.44
  196.2 4.2 while.1
  196.3 0.6 fusion.28
  196.9 1.4 bitcast_dynamic-update-slice_fusion.2
  198.3 0.6 fusion.28
  198.9 1.4 bitcast_dynamic-update-slice_fusion.2
  200.3 19.7 %custom-call.16 = f32[2,128,128]{1,2,0:T(8,128)S(1)} custom-call(f32[2,128,128]{2,1,0:T(8,128)S(1)} %get-tuple-element.10), custom_call_target="InvertDiagBlocksLowerTriangular" | custom-call | tf_op jit(solution)/shard_map/jit(_solve_triangular)/triangular_solve | solution.py:19
  220.0 0.3 fusion.5
  220.3 0.3 convolution_subtract_fusion.1
  220.6 0.3 fusion.8
  220.9 3.3 convolution_bitcast_fusion
  224.2 0.0 all-reduce.6.cloned.1.call-start
  224.2 80.6 %all-gather.2.cloned.1.call-done = f32[8192,256]{0,1:T(8,128)} async-done(((f32[2048,256]{0,1:T(8,128)}), f32[8192,256]{0,1:T(8,128)}) %all-gather.2.cloned.1.call-update) | async-done | bytes 8388624 | tf_op jit(solution)/shard_map/all_gather | solution.py:29
  304.8 11.4 %fusion.15 = f32[256,256]{1,0:T(8,128)} fusion(f32[8192,256]{0,1:T(8,128)} %all-gather.2.cloned.1.call-done, f32[8192,256]{1,0:T(8,128)} %param.3), kind=kOutput, calls=%fused_computation.39 | convolution fusion | flops 6442450944 | bytes 17039360 | tf_op jit(solution)/shard_map/dot_general | solution.py:10
  316.2 0.8 copy.7
  317.1 101.8 %all-reduce.6.cloned.1.call-done = f32[256,256]{1,0:T(8,128)} async-done(((f32[256,256]{1,0:T(8,128)}), f32[256,256]{1,0:T(8,128)}) %all-reduce.6.cloned.1.call-update) | async-done | bytes 262160 | tf_op jit(solution)/shard_map/psum | solution.py:30
  418.9 21.1 %convolution_subtract_fusion = f32[8192,256]{1,0:T(8,128)} fusion(f32[8192,256]{1,0:T(8,128)} %param.3, f32[8192,256]{0,1:T(8,128)} %all-gather.2.cloned.1.call-done, f32[256,256]{1,0:T(8,128)} %all-reduce.6.cloned.1.call-done), kind=kOutput, calls=%fused_computation.2 | convolution fusion | flops 6444548096 | bytes 25427968 | tf_op jit(solution)/shard_map/dot_general | solution.py:10
  440.0 0.7 broadcast_multiply_fusion
  (15 shorter events, 0.2 us)
Async XLA Ops:
  7.2 1.6 copy-start
  7.2 151.0 %all-reduce.4.cloned.1.call-start = ((), (), s32[]{:S(2)}) async-start(), calls=%async_computation | async-start | bytes 524288 | tf_op jit(solution)/shard_map/psum | solution.py:25
  12.9 291.9 %all-gather.2.cloned.1.call-start = ((), (), s32[]{:S(2)}) async-start(), calls=%async_computation.1 | async-start | bytes 10485760 | tf_op jit(solution)/shard_map/all_gather | solution.py:29
  224.2 194.7 %all-reduce.6.cloned.1.call-start = ((), (), s32[]{:S(2)}) async-start(), calls=%async_computation.2 | async-start | bytes 524288 | tf_op jit(solution)/shard_map/psum | solution.py:30
  418.9 21.1 %copy-start.1 = (f32[256,256]{1,0:T(8,128)S(1)}, f32[256,256]{1,0:T(8,128)}, u32[]{:S(2)}) copy-start(f32[256,256]{1,0:T(8,128)} %all-reduce.6.cloned.1.call-done) | copy-start | bytes 786436
Sparse Core Ops, SparseCore 0:
  13.3 144.8 all-reduce.3
  224.3 80.4 all-gather.1
  316.4 102.4 all-reduce.5
where the time goes:
time: 447 us
  waiting for transfers between devices  327 us (73%)
  other arithmetic  55.4 us (12%)
  matrix products  41.2 us (9%)
  between operations  15.2 us (3%)
  local copies, waits for them, and re-layouts  7.51 us (2%)
    psum x1, waiting for transfers between devices, local(): gram_sum = lax.psum(matmul(panel_cols.T, panel_cols), ('rows', 'cols'))  145 us
    psum x1, waiting for transfers between devices, local(): coupling = lax.psum(matmul(orthonormal.T, trailing), 'rows')  102 us
    all_gather x1, waiting for transfers between devices, local(): orthonormal = lax.all_gather(basis_part, 'cols', axis=0, tiled=True)  80.6 us
    dot_general x4, matrix products, matmul(): return jnp.dot(left, right, precision=lax.Precision.HIGHEST)  39.9 us
    another operation x6, other arithmetic, lower_factor(): return jnp.linalg.cholesky(gram_sum)  34 us
    another operation x3, other arithmetic, lower_inverse(): return jax.scipy.linalg.solve_triangular(lower, identity, lower=True)  19.7 us
  transfers between devices with their start and end apart: 3, of which 3 were waited for; matrix products, arithmetic and copies ran while one was open for 0% of the time, Pallas kernels for 0%

commit v1 on v0

v1 whole, which is shorter than its diff:
```python
import math

import jax
import jax.numpy as jnp
from jax import lax
from jax.experimental import pallas as pl
from jax.experimental.pallas import tpu as pltpu
from jax.sharding import PartitionSpec as P

F32, BF16 = jnp.float32, jnp.bfloat16
HIGHEST = lax.Precision.HIGHEST
CBLOCK = 1024
UBLOCK = 1024

def split(value):
    high = value.astype(BF16)
    return high, (value - high.astype(F32)).astype(BF16)

def contract(left, right, dims, precision=None):
    return lax.dot_general(left, right, (dims, ((), ())), precision=precision, preferred_element_type=F32)

def factor_block(block, group):
    size = block.shape[0]
    lane = lax.broadcasted_iota(jnp.int32, (size, 2 * size), 1)
    row = lax.broadcasted_iota(jnp.int32, (size, 2 * size), 0)
    wide = jnp.concatenate([block, jnp.zeros((size, size), F32)], axis=1)
    wide = jnp.where(lane == row + size, 1.0, wide)
    for first in range(0, size, group):
        columns = [jnp.broadcast_to(wide[:, first + g : first + g + 1], wide.shape) for g in range(group)]
        rows = [wide[first + g : first + g + 1, :] for g in range(group)]
        small = [[columns[j][first + i : first + i + 1, :] for j in range(group)] for i in range(group)]
        change = None
        for g in range(group):
            inv = 1.0 / small[g][g]
            scaled = rows[g] * inv
            for i in range(g + 1, group):
                ratio = small[i][g] * inv
                rows[i] = rows[i] - ratio * rows[g]
                for j in range(g + 1, group):
                    small[i][j] = small[i][j] - ratio * small[g][j]
            for j in range(g + 1, group):
                columns[j] = columns[j] - columns[g] * (small[g][j] * inv)
            term = jnp.where(row > first + g, columns[g] * scaled, 0.0)
            change = term if change is None else change + term
        wide = wide - change
    diagonal = jnp.sum(jnp.where(lane == row, wide, 0.0), axis=1, keepdims=True)
    wide = wide * lax.rsqrt(diagonal)
    return wide

def factor_kernel(shrink, size, group, core, mine, other, r_factor, inverse, work):
    @pl.when(core[0] == 0)
    def _():
        work[:128, :256] = mine[...]
        work[128:, :256] = other[...]
    @pl.when(core[0] != 0)
    def _():
        work[:128, :256] = other[...]
        work[128:, :256] = mine[...]
    rows = lax.broadcasted_iota(jnp.int32, (256, 256), 0)
    lanes = lax.broadcasted_iota(jnp.int32, (256, 256), 1)
    work[:, 256:] = (rows == lanes).astype(F32)
    for first in range(0, 256, size):
        last = first + size
        both = factor_block(work[first:last, first:last], group)
        done = contract(both[:, size:], work[first:last, :], ((1,), (0,)), HIGHEST)
        work[first:last, :] = done
        if last < 256:
            work[last:, :] -= contract(done[:, last:256], done, ((0,), (0,)), HIGHEST)
    r_factor[...] = jnp.where(rows <= lanes, work[:, :256], 0.0) * shrink
    inverse[...] = jnp.where(rows >= lanes, work[:, 256:], 0.0)

def factor(core, mine, other, shrink, size=64, group=4):
    full = jax.ShapeDtypeStruct((256, 256), F32)
    return pl.pallas_call(
        lambda *refs: factor_kernel(shrink, size, group, *refs),
        out_shape=[full, full],
        in_specs=[pl.BlockSpec(memory_space=pltpu.SMEM), pl.BlockSpec(memory_space=pltpu.VMEM), pl.BlockSpec(memory_space=pltpu.VMEM)],
        out_specs=[pl.BlockSpec(memory_space=pltpu.VMEM)] * 2,
        scratch_shapes=[pltpu.VMEM((256, 512), F32)],
        compiler_params=pltpu.CompilerParams(vmem_limit_bytes=16 << 20),
    )(core, mine, other)

def product3(piece, w):
    high, low = split(piece)
    return contract(jnp.concatenate([high, low, high], axis=1), w[...], ((1,), (0,)))

def update_kernel(shrink, block, piece_rows, place, mine, other, inverse, *refs):
    *pieces, trailing, updated, r_cross, w = refs
    step = pl.program_id(0)

    @pl.when(step == 0)
    def _():
        first = place[1] == 0
        top = jnp.where(first, mine[...], other[...])
        bottom = jnp.where(first, other[...], mine[...])
        cross = jnp.concatenate([top, bottom], axis=0)
        coupling = contract(inverse[...], cross, ((1,), (0,)), HIGHEST)
        r_cross[...] = coupling * shrink
        weights = contract(inverse[...], coupling, ((0,), (0,)), HIGHEST)
        high, low = split(weights)
        w[:256, :] = high
        w[256:512, :] = high
        w[512:, :] = low

    at = at_piece = 0
    for piece in pieces:
        count = piece_rows[at_piece] // block
        at_piece += 1
        @pl.when((step >= at) & (step < at + count))
        def _(piece=piece):
            updated[...] = trailing[...] - product3(piece[...], w)
        at += count

def update(mine, other, inverse, pieces, rows, trailing, place, shrink, block):
    full = pl.BlockSpec((256, 256), lambda i, place: (0, 0))
    half = pl.BlockSpec((128, 256), lambda i, place: (0, 0))
    specs, at = [], 0
    for count in rows:
        count //= block
        specs.append(pl.BlockSpec((block, 256), lambda i, place, at=at, count=count: (jnp.clip(i - at, 0, count - 1), 0)))
        at += count
    chunk = 2048 // block

    def row(i, place):
        which = i // chunk
        offset = jnp.where(which == 0, 0, jnp.where(which == 1, 3, jnp.where(which == 2, 1, 2)))
        return ((place[0] + offset) % 4 * chunk + i % chunk, 0)

    wide = pl.BlockSpec((block, 256), row)
    return pl.pallas_call(
        lambda *refs: update_kernel(shrink, block, rows, *refs),
        out_shape=[jax.ShapeDtypeStruct(trailing.shape, F32), jax.ShapeDtypeStruct((256, 256), F32)],
        grid_spec=pltpu.PrefetchScalarGridSpec(
            num_scalar_prefetch=1, grid=(4 * chunk,),
            in_specs=[half, half, full, *specs, wide], out_specs=[wide, full],
            scratch_shapes=[pltpu.VMEM((768, 256), BF16)]),
        compiler_params=pltpu.CompilerParams(vmem_limit_bytes=48 << 20),
    )(place, mine, other, inverse, *pieces, trailing)

def cross_kernel(counts, initial, halves, place, *refs):
    refs = list(refs)
    start = refs.pop(0) if initial else None
    pieces, refs = refs[:len(counts)], refs[len(counts):]
    trailing, *outs, acc = refs
    step = pl.program_id(0)
    @pl.when(step == 0)
    def _():
        acc[...] = start[...] if initial else jnp.zeros_like(acc)
    at = 0
    for piece, count in zip(pieces, counts):
        @pl.when((step >= at) & (step < at + count))
        def _(piece=piece):
            ph, pb = split(piece[...])
            th, tb = split(trailing[...])
            left = jnp.concatenate([ph, pb, ph], axis=0)
            right = jnp.concatenate([th, th, tb], axis=0)
            acc[...] += contract(left, right, ((0,), (0,)))

        at += count
    @pl.when(step == at - 1)
    def _():
        if halves:
            keep, send = outs
            @pl.when(place[1] == 0)
            def _():
                keep[...] = acc[:128, :]
                send[...] = acc[128:, :]
            @pl.when(place[1] != 0)
            def _():
                keep[...] = acc[128:, :]
                send[...] = acc[:128, :]
        else:
            outs[0][...] = acc[...]

def cross_part(place, initial, pieces, spots, trailing, halves, block, rows):
    counts = [r // block for r in rows]
    full = pl.BlockSpec((256, 256), lambda i, place: (0, 0))
    half = pl.BlockSpec((128, 256), lambda i, place: (0, 0))
    specs, at, table = [], 0, []
    for piece, count, (offset, low) in zip(pieces, counts, spots):
        specs.append(pl.BlockSpec((block, 256), lambda i, place, at=at, count=count: (jnp.clip(i - at, 0, count - 1), 0)))
        table += [(offset, low // block + n) for n in range(count)]
        at += count
    def row(i, place):
        offset, low = table[-1]
        off, lo = jnp.int32(offset), jnp.int32(low)
        for n in range(at - 1):
            off = jnp.where(i == n, table[n][0], off)
            lo = jnp.where(i == n, table[n][1], lo)
        return ((place[0] + off) % 4 * (2048 // block) + lo, 0)
    out = [jax.ShapeDtypeStruct((128, 256), F32)] * 2 if halves else [jax.ShapeDtypeStruct((256, 256), F32)]
    return pl.pallas_call(
        lambda *refs: cross_kernel(counts, initial is not None, halves, *refs),
        out_shape=out,
        grid_spec=pltpu.PrefetchScalarGridSpec(
            num_scalar_prefetch=1, grid=(at,),
            in_specs=([full] if initial is not None else []) + specs + [pl.BlockSpec((block, 256), row)],
            out_specs=[half, half] if halves else [full],
            scratch_shapes=[pltpu.VMEM((256, 256), F32)]),
        compiler_params=pltpu.CompilerParams(vmem_limit_bytes=48 << 20),
    )(place, *([initial] if initial is not None else []), *pieces, trailing)


def gram_kernel(place, panel, keep, send):
    @pl.when(pl.program_id(0) == 0)
    def _():
        keep[...] = jnp.zeros_like(keep)
        send[...] = jnp.zeros_like(send)
    part = contract(panel[...], panel[...], ((0,), (0,)), HIGHEST)
    @pl.when(place[1] == 0)
    def _():
        keep[...] += part[:128, :]
        send[...] += part[128:, :]
    @pl.when(place[1] != 0)
    def _():
        keep[...] += part[128:, :]
        send[...] += part[:128, :]

def gram_part(place, panel, block=1024):
    half = pl.BlockSpec((128, 256), lambda i, place: (0, 0))
    return pl.pallas_call(
        gram_kernel,
        out_shape=[jax.ShapeDtypeStruct((128, 256), F32)] * 2,
        grid_spec=pltpu.PrefetchScalarGridSpec(
            num_scalar_prefetch=1, grid=(panel.shape[0] // block,),
            in_specs=[pl.BlockSpec((block, 256), lambda i, place: (i, 0))],
            out_specs=[half, half]),
        compiler_params=pltpu.CompilerParams(vmem_limit_bytes=32 << 20),
    )(place, panel)


def over_rows(move):
    pairs = []
    for z in range(4):
        for x in range(4):
            for core in range(2):
                z2, x2, core2 = move(z, x, core)
                pairs.append(((z * 4 + x) * 2 + core, (z2 % 4 * 4 + x2 % 4) * 2 + core2))
    return pairs


PARTNER = over_rows(lambda z, x, core: (z, x, 1 - core))
FIRST = [over_rows(lambda z, x, core, k=k: (z, x + k, core) if core == 0 else (z + k, x, core)) for k in (2, 1, 3)]
SECOND = [over_rows(lambda z, x, core, k=k: (z + k, x, core) if core == 0 else (z, x + k, core)) for k in (2, 1, 3)]


def around(k):
    return [(i, (i + k) % 4) for i in range(4)]


def exchange_sum(part, axis, moves):
    others = [lax.ppermute(part, axis, move) for move in moves]
    return part + others[0] + others[1] + others[2]


def partner(part):
    return lax.ppermute(part, "rows", PARTNER)


def local(panel_cols, trailing):
    rows_total = trailing.shape[0] * lax.axis_size("rows")
    shrink = 1.0 / math.sqrt(rows_total)
    core = lax.axis_index("rows") % 2
    place = jnp.stack([lax.axis_index("cols"), core]).astype(jnp.int32)
    size = panel_cols.shape[0]
    half = size // 2
    barrier = lax.optimization_barrier
    left1 = lax.ppermute(panel_cols[:half], "cols", around(1))
    right1 = lax.ppermute(panel_cols[half:], "cols", around(-1))

    keep, send = gram_part(place, panel_cols)
    gram = keep + partner(send)
    left1, right1, _, rest = barrier((left1, right1, gram, panel_cols))
    gram = exchange_sum(gram, "cols", [around(k) for k in (2, 1, 3)])
    left2 = lax.ppermute(rest[half:], "cols", around(1))
    right2 = lax.ppermute(rest[:half], "cols", around(-1))
    far1 = lax.ppermute(left1, "cols", around(1))
    far2 = lax.ppermute(right1, "cols", around(-1))
    gram = exchange_sum(gram, "rows", FIRST)
    gram = exchange_sum(gram, "rows", SECOND)
    r_factor, inverse = factor(place[1:], gram, partner(gram), shrink, 64, 8)

    rows = (size, half, half)
    (cross,) = cross_part(place, None, (panel_cols, left1, right1), ((0, 0), (3, 0), (1, half)), trailing, False, CBLOCK, rows=rows)
    (cross,) = cross_part(place, cross, (left2, right2), ((3, half), (1, 0)), trailing, False, CBLOCK, rows=(half, half))
    inverse, far1, far2 = barrier((inverse, far1, far2))
    keep, send = cross_part(place, cross, (far1, far2), ((2, 0), (2, half)), trailing, True, CBLOCK, rows=(half, half))
    cross = keep + partner(send)
    cross = exchange_sum(cross, "rows", FIRST)
    cross = exchange_sum(cross, "rows", SECOND)
    pieces = (panel_cols, left1, left2, right2, right1, far1, far2)
    rows = (size, half, half, half, half, half, half)
    updated, r_cross = update(cross, partner(cross), inverse, pieces, rows, trailing, place, shrink, UBLOCK)
    return (r_factor, r_cross, updated)


def solution(mesh):
    in_specs = (P(("rows", "cols"), None), P("rows", "cols"))
    out_specs = (P(), P(None, "cols"), P("rows", "cols"))
    return jax.shard_map(local, mesh=mesh, in_specs=in_specs, out_specs=out_specs, check_vma=False)
```

time: 447 us -> 134 us (0.30)
  waiting for transfers between devices: 327 us -> 47.6 us
  other arithmetic: 55.4 us -> 0.28 us
  starting transfers between devices: 0.3 us -> 43.5 us
  matrix products: 41.2 us -> 0 us
  Pallas kernels: 0 us -> 38.2 us
  between operations: 15.2 us -> 0.78 us
    psum x2 -> x0, waiting for transfers between devices: 247 us -> none  [the longest x1 145 us: local(): gram_sum = lax.psum(matmul(panel_cols.T, panel_cols), ('rows', 'cols'))]
    all_gather x1 -> x0, waiting for transfers between devices: 80.6 us -> none  [local(): orthonormal = lax.all_gather(basis_part, 'cols', axis=0, tiled=True)]
    another operation x9 -> x1, other arithmetic: 53.7 us -> 0.07 us  [local(): place = jnp.stack([lax.axis_index('cols'), core]).astype(jnp.int32)]
    ppermute x0 -> x25, waiting for transfers between devices: none -> 47.6 us  [the longest x15 43.5 us: exchange_sum(): others = [lax.ppermute(part, axis, move) for move in moves]]
    ppermute x0 -> x25, starting transfers between devices: none -> 43.5 us  [the longest x15 21.3 us: exchange_sum(): others = [lax.ppermute(part, axis, move) for move in moves]]
    dot_general x4 -> x0, matrix products: 39.9 us -> none  [matmul(): return jnp.dot(left, right, precision=lax.Precision.HIGHEST)]
    pallas_call x0 -> x6, Pallas kernels: none -> 38.2 us  [the longest x1 13.1 us: update(): pl.pallas_call(lambda *refs: update_kernel(shrink, block, rows, *refs), o...]
  transfers between devices with their start and end apart: 3 -> 25, of which waited for: 3 -> 16; matrix products, arithmetic and copies ran while one was open for 0% -> 0% of each run, Pallas kernels for 0% -> 14%
where the time goes in v1:
time: 134 us
  waiting for transfers between devices  47.6 us (36%)
  starting transfers between devices  43.5 us (32%)
  Pallas kernels  38.2 us (29%)
  local copies, waits for them, and re-layouts  3.29 us (2%)
    ppermute x15, waiting for transfers between devices, exchange_sum(): others = [lax.ppermute(part, axis, move) for move in moves]  43.5 us
    ppermute x15, starting transfers between devices, exchange_sum(): others = [lax.ppermute(part, axis, move) for move in moves]  21.3 us
    ppermute x4, starting transfers between devices, partner(): return lax.ppermute(part, 'rows', PARTNER)  15.4 us
    pallas_call x1, Pallas kernels, update(): pl.pallas_call(lambda *refs: update_kernel(shrink, block, rows, *refs), o...  13.1 us
    pallas_call x3, Pallas kernels, cross_part(): pl.pallas_call(lambda *refs: cross_kernel(counts, initial is not None, ha...  11.9 us
    pallas_call x1, Pallas kernels, factor(): pl.pallas_call(lambda *refs: factor_kernel(shrink, size, group, *refs), o...  10.2 us
    ppermute x4, waiting for transfers between devices, partner(): return lax.ppermute(part, 'rows', PARTNER)  3.95 us
    ppermute x1, starting transfers between devices, local(): right1 = lax.ppermute(panel_cols[half:], 'cols', around(-1))  3.56 us
  transfers between devices with their start and end apart: 25, of which 16 were waited for; matrix products, arithmetic and copies ran while one was open for 0% of the time, Pallas kernels for 14%

profile of v1, /device:TPU:1, one launch (start us, length us, event | category | flops | bytes accessed | tf_op | source)
XLA Modules:
  0.0 133.6 jit_solution(4384483279903780592)
XLA Ops:
  0.6 3.1 %fusion.1 = (f32[1024,256]{1,0:T(8,128)}, f32[1024,256]{1,0:T(8,128)}) fusion(f32[2048,256]{1,0:T(8,128)} %refs_4_.7), kind=kLoop, calls=%fused_computation.7 | loop fusion | bytes 4194304 | tf_op jit(solution)/shard_map/slice | solution.py:269
  3.8 3.6 %collective-permute-start.12 = (f32[1024,256]{1,0:T(8,128)}, f32[1024,256]{1,0:T(8,128)S(1)}, u32[]{:S(2)}, u32[]{:S(2)}) collective-permute-start(f32[1024,256]{1,0:T(8,128)} %get-tuple-element.33), channel_id=1, source_target_pairs={{0,3},{1,0},{2,1},{3,2},{4,7},{5,4},{6,5},{7,6},{8,11},{9,8},{10,9... | collective-permute-start | bytes 3145736 | tf_op jit(solution)/shard_map/ppermute | solution.py:269
  7.4 3.0 %shard_map.49 = (f32[128,256]{1,0:T(8,128)S(1)}, f32[128,256]{1,0:T(8,128)S(1)}) custom-call(s32[2]{0:T(128)S(1)} %pad_add_fusion.place.refs_0_, f32[2048,256]{1,0:T(8,128)S(1)} %copy-done), custom_call_target="tpu_custom_call" | custom-call | tf_op jit(solution)/shard_map/pallas_call | solution.py:221
  10.4 1.0 collective-permute-start
  11.5 1.0 collective-permute-done
  12.5 3.0 %collective-permute-start.3 = (f32[128,256]{1,0:T(8,128)S(1)}, f32[128,256]{1,0:T(8,128)S(1)}, u32[]{:S(2)}, u32[]{:S(2)}) collective-permute-start(f32[128,256]{1,0:T(8,128)S(1)} %add.56), channel_id=1, source_target_pairs={{0,3},{1,0},{2,1},{3,2},{4,7},{5,4},{6,5},{7,6},{8,11},{9,8},{10,9... | collective-permute-start | bytes 393224 | tf_op jit(solution)/shard_map/ppermute | solution.py:252
  15.5 1.3 collective-permute-start.1
  16.8 18.1 %collective-permute-done.3 = f32[128,256]{1,0:T(8,128)S(1)} collective-permute-done((f32[128,256]{1,0:T(8,128)S(1)}, f32[128,256]{1,0:T(8,128)S(1)}, u32[]{:S(2)}, u32[]{:S(2)}) %collective-permute-start.3) | collective-permute-done | bytes 131104 | tf_op jit(solution)/shard_map/ppermute | solution.py:252
  34.9 1.6 %collective-permute-done.2 = f32[128,256]{1,0:T(8,128)S(1)} collective-permute-done((f32[128,256]{1,0:T(8,128)S(1)}, f32[128,256]{1,0:T(8,128)S(1)}, u32[]{:S(2)}, u32[]{:S(2)}) %collective-permute-start.2) | collective-permute-done | bytes 131104 | tf_op jit(solution)/shard_map/ppermute | solution.py:252
  36.8 3.8 %collective-permute-start.6 = (f32[128,256]{1,0:T(8,128)S(1)}, f32[128,256]{1,0:T(8,128)S(1)}, u32[]{:S(2)}, u32[]{:S(2)}) collective-permute-start(f32[128,256]{1,0:T(8,128)S(1)} %add_add_fusion.4), channel_id=1, source_target_pairs={{0,24},{4,100},{8,0},{12,108},{16,8},{20,116},{24,16},{28,124},{32... | collective-permute-start | bytes 393224 | tf_op jit(solution)/shard_map/ppermute | solution.py:252
  40.6 1.3 collective-permute-start.4
  42.0 2.7 %collective-permute-start.16 = (f32[1024,256]{1,0:T(8,128)S(1)}, f32[1024,256]{1,0:T(8,128)S(1)}, u32[]{:S(2)}, u32[]{:S(2)}) collective-permute-start(f32[1024,256]{1,0:T(8,128)S(1)} %collective-permute-done.12.refs_3_.refs_8_), channel_id=1, source_target_pairs={{0,3},{1,0},{2,1},{3,2},{4,7},{5,4},{6,5},{7,6},{8,11},{9,8},{10,9... | collective-permute-start | bytes 3145736 | tf_op jit(solution)/shard_map/ppermute | solution.py:278
  45.3 2.1 %collective-permute-done.5 = f32[128,256]{1,0:T(8,128)S(1)} collective-permute-done((f32[128,256]{1,0:T(8,128)S(1)}, f32[128,256]{1,0:T(8,128)S(1)}, u32[]{:S(2)}, u32[]{:S(2)}) %collective-permute-start.5) | collective-permute-done | bytes 131104 | tf_op jit(solution)/shard_map/ppermute | solution.py:252
  47.4 2.5 %collective-permute-start.9 = (f32[128,256]{1,0:T(8,128)S(1)}, f32[128,256]{1,0:T(8,128)S(1)}, u32[]{:S(2)}, u32[]{:S(2)}) collective-permute-start(f32[128,256]{1,0:T(8,128)S(1)} %add_add_fusion.3), channel_id=1, source_target_pairs={{0,96},{4,28},{8,104},{12,4},{16,112},{20,12},{24,120},{28,20},{32... | collective-permute-start | bytes 393224 | tf_op jit(solution)/shard_map/ppermute | solution.py:252
  50.0 1.9 %collective-permute-done.9 = f32[128,256]{1,0:T(8,128)S(1)} collective-permute-done((f32[128,256]{1,0:T(8,128)S(1)}, f32[128,256]{1,0:T(8,128)S(1)}, u32[]{:S(2)}, u32[]{:S(2)}) %collective-permute-start.9) | collective-permute-done | bytes 131104 | tf_op jit(solution)/shard_map/ppermute | solution.py:252
  52.7 5.3 %collective-permute-done.8 = f32[128,256]{1,0:T(8,128)S(1)} collective-permute-done((f32[128,256]{1,0:T(8,128)S(1)}, f32[128,256]{1,0:T(8,128)S(1)}, u32[]{:S(2)}, u32[]{:S(2)}) %collective-permute-start.8) | collective-permute-done | bytes 131104 | tf_op jit(solution)/shard_map/ppermute | solution.py:252
  58.4 4.8 %collective-permute-done.7 = f32[128,256]{1,0:T(8,128)S(1)} collective-permute-done((f32[128,256]{1,0:T(8,128)S(1)}, f32[128,256]{1,0:T(8,128)S(1)}, u32[]{:S(2)}, u32[]{:S(2)}) %collective-permute-start.7) | collective-permute-done | bytes 131104 | tf_op jit(solution)/shard_map/ppermute | solution.py:252
  63.3 7.2 %collective-permute-start.10 = (f32[128,256]{1,0:T(8,128)S(1)}, f32[128,256]{1,0:T(8,128)S(1)}, u32[]{:S(2)}, u32[]{:S(2)}) collective-permute-start(f32[128,256]{1,0:T(8,128)S(1)} %add_add_fusion.2.refs_1_), channel_id=1, source_target_pairs={{0,4},{4,0},{8,12},{12,8},{16,20},{20,16},{24,28},{28,24},{32,36},... | collective-permute-start | bytes 393224 | tf_op jit(solution)/shard_map/ppermute | solution.py:257
  70.5 1.0 collective-permute-done.10.refs_2_
  71.5 10.2 %shard_map.50 = (f32[256,256]{1,0:T(8,128)}, f32[256,256]{1,0:T(8,128)S(1)}) custom-call(s32[1]{0:T(128)} %bitcast.refs_0_, f32[128,256]{1,0:T(8,128)S(1)} %add_add_fusion.2.refs_1_, f32[128,256]{1,0:T(8,128)S(1)} %collective-permute-done.10.refs_2_), custom_call_target="tpu_custom_call" | custom-call | tf_op jit(solution)/shard_map/pallas_call | solution.py:74
  81.7 5.4 %shard_map.51.refs_1_ = f32[256,256]{1,0:T(8,128)S(1)} custom-call(s32[2]{0:T(128)S(1)} %pad_add_fusion.place.refs_0_, f32[2048,256]{1,0:T(8,128)S(1)} %copy-done, f32[1024,256]{1,0:T(8,128)} %collective-permute-done.11.refs_2_.refs_5_, f32[1024,256]{1,0:T(8,128)S(1)} %collective-permute-done.12.refs_3_.refs_8_, f32[8192,256]{1,0:T(8,128)} %refs_11_.1), custom_call_target="tpu_custom_call" | custom-call | tf_op jit(solution)/shard_map/pallas_call | solution.py:192
  87.3 3.2 %shard_map.52.refs_1_ = f32[256,256]{1,0:T(8,128)S(1)} custom-call(s32[2]{0:T(128)S(1)} %pad_add_fusion.place.refs_0_, f32[256,256]{1,0:T(8,128)S(1)} %shard_map.51.refs_1_, f32[1024,256]{1,0:T(8,128)S(1)} %collective-permute-done.13.refs_2_.refs_6_, f32[1024,256]{1,0:T(8,128)S(1)} %collective-permute-done.14.refs_3_.refs_7_, f32[8192,256]{1,0:T(8,128)} %refs_11_.1), custom_call_target="tpu_custom_call" | custom-call | tf_op jit(solution)/shard_map/pallas_call | solution.py:192
  90.6 3.2 %shard_map.53 = (f32[128,256]{1,0:T(8,128)S(1)}, f32[128,256]{1,0:T(8,128)S(1)}) custom-call(s32[2]{0:T(128)S(1)} %pad_add_fusion.place.refs_0_, f32[256,256]{1,0:T(8,128)S(1)} %shard_map.52.refs_1_, f32[1024,256]{1,0:T(8,128)S(1)} %collective-permute-done.15.refs_2_.refs_9_, f32[1024,256]{1,0:T(8,128)S(1)} %collective-permute-done.16.refs_3_.refs_10_, ...), custom_call_target="tpu_custom_call" | custom-call | tf_op jit(solution)/shard_map/pallas_call | solution.py:192
  93.8 4.2 %collective-permute-start.17 = (f32[128,256]{1,0:T(8,128)S(1)}, f32[128,256]{1,0:T(8,128)S(1)}, u32[]{:S(2)}, u32[]{:S(2)}) collective-permute-start(f32[128,256]{1,0:T(8,128)S(1)} %get-tuple-element.27), channel_id=1, source_target_pairs={{0,4},{4,0},{8,12},{12,8},{16,20},{20,16},{24,28},{28,24},{32,36},... | collective-permute-start | bytes 393224 | tf_op jit(solution)/shard_map/ppermute | solution.py:257
  99.0 1.5 %collective-permute-start.20 = (f32[128,256]{1,0:T(8,128)S(1)}, f32[128,256]{1,0:T(8,128)S(1)}, u32[]{:S(2)}, u32[]{:S(2)}) collective-permute-start(f32[128,256]{1,0:T(8,128)S(1)} %add.66), channel_id=1, source_target_pairs={{0,24},{4,100},{8,0},{12,108},{16,8},{20,116},{24,16},{28,124},{32... | collective-permute-start | bytes 393224 | tf_op jit(solution)/shard_map/ppermute | solution.py:252
  101.1 1.7 %collective-permute-start.18 = (f32[128,256]{1,0:T(8,128)S(1)}, f32[128,256]{1,0:T(8,128)S(1)}, u32[]{:S(2)}, u32[]{:S(2)}) collective-permute-start(f32[128,256]{1,0:T(8,128)S(1)} %add.66), channel_id=1, source_target_pairs={{0,16},{4,68},{8,24},{12,76},{16,0},{20,84},{24,8},{28,92},{32,48}... | collective-permute-start | bytes 393224 | tf_op jit(solution)/shard_map/ppermute | solution.py:252
  103.7 3.6 %collective-permute-done.19 = f32[128,256]{1,0:T(8,128)S(1)} collective-permute-done((f32[128,256]{1,0:T(8,128)S(1)}, f32[128,256]{1,0:T(8,128)S(1)}, u32[]{:S(2)}, u32[]{:S(2)}) %collective-permute-start.19) | collective-permute-done | bytes 131104 | tf_op jit(solution)/shard_map/ppermute | solution.py:252
  107.3 2.5 %collective-permute-start.23 = (f32[128,256]{1,0:T(8,128)S(1)}, f32[128,256]{1,0:T(8,128)S(1)}, u32[]{:S(2)}, u32[]{:S(2)}) collective-permute-start(f32[128,256]{1,0:T(8,128)S(1)} %add_add_fusion.1), channel_id=1, source_target_pairs={{0,96},{4,28},{8,104},{12,4},{16,112},{20,12},{24,120},{28,20},{32... | collective-permute-start | bytes 393224 | tf_op jit(solution)/shard_map/ppermute | solution.py:252
  109.8 1.9 %collective-permute-start.21 = (f32[128,256]{1,0:T(8,128)S(1)}, f32[128,256]{1,0:T(8,128)S(1)}, u32[]{:S(2)}, u32[]{:S(2)}) collective-permute-start(f32[128,256]{1,0:T(8,128)S(1)} %add_add_fusion.1), channel_id=1, source_target_pairs={{0,64},{4,20},{8,72},{12,28},{16,80},{20,4},{24,88},{28,12},{32,96... | collective-permute-start | bytes 393224 | tf_op jit(solution)/shard_map/ppermute | solution.py:252
  111.7 4.8 %collective-permute-done.22 = f32[128,256]{1,0:T(8,128)S(1)} collective-permute-done((f32[128,256]{1,0:T(8,128)S(1)}, f32[128,256]{1,0:T(8,128)S(1)}, u32[]{:S(2)}, u32[]{:S(2)}) %collective-permute-start.22) | collective-permute-done | bytes 131104 | tf_op jit(solution)/shard_map/ppermute | solution.py:252
  116.5 3.0 %collective-permute-start.24 = (f32[128,256]{1,0:T(8,128)S(1)}, f32[128,256]{1,0:T(8,128)S(1)}, u32[]{:S(2)}, u32[]{:S(2)}) collective-permute-start(f32[128,256]{1,0:T(8,128)S(1)} %add_add_fusion.refs_1_), channel_id=1, source_target_pairs={{0,4},{4,0},{8,12},{12,8},{16,20},{20,16},{24,28},{28,24},{32,36},... | collective-permute-start | bytes 393224 | tf_op jit(solution)/shard_map/ppermute | solution.py:257
  120.5 13.1 %shard_map.54 = (f32[8192,256]{1,0:T(8,128)}, f32[256,256]{1,0:T(8,128)}) custom-call(s32[2]{0:T(128)S(1)} %pad_add_fusion.place.refs_0_, f32[128,256]{1,0:T(8,128)S(1)} %add_add_fusion.refs_1_, f32[128,256]{1,0:T(8,128)S(1)} %collective-permute-done.24.refs_2_, f32[256,256]{1,0:T(8,128)S(1)} %get-tuple-element.28.refs_3_, f32[2048,256]{1,0:T(8,128)} %refs_4_.7, ...), custom_call_target="tpu_custom_call" | custom-call | tf_op jit(solution)/shard_map/pallas_call | solution.py:130
  (38 shorter events, 6.2 us)
Async XLA Ops:
  0.6 6.8 %copy-start = (f32[2048,256]{1,0:T(8,128)S(1)}, f32[2048,256]{1,0:T(8,128)}, u32[]{:S(2)}) copy-start(f32[2048,256]{1,0:T(8,128)} %refs_4_.7) | copy-start | bytes 6291460
  3.8 38.2 %collective-permute-start.12 = (f32[1024,256]{1,0:T(8,128)}, f32[1024,256]{1,0:T(8,128)S(1)}, u32[]{:S(2)}, u32[]{:S(2)}) collective-permute-start(f32[1024,256]{1,0:T(8,128)} %get-tuple-element.33), channel_id=1, source_target_pairs={{0,3},{1,0},{2,1},{3,2},{4,7},{5,4},{6,5},{7,6},{8,11},{9,8},{10,9... | collective-permute-start | bytes 3145736 | tf_op jit(solution)/shard_map/ppermute | solution.py:269
  7.4 34.6 %collective-permute-start.11 = (f32[1024,256]{1,0:T(8,128)}, f32[1024,256]{1,0:T(8,128)}, u32[]{:S(2)}, u32[]{:S(2)}) collective-permute-start(f32[1024,256]{1,0:T(8,128)} %get-tuple-element.34), channel_id=1, source_target_pairs={{0,1},{1,2},{2,3},{3,0},{4,5},{5,6},{6,7},{7,4},{8,9},{9,10},{10,1... | collective-permute-start | bytes 3145736 | tf_op jit(solution)/shard_map/ppermute | solution.py:268
  10.4 2.0 %collective-permute-start = (f32[128,256]{1,0:T(8,128)S(1)}, f32[128,256]{1,0:T(8,128)S(1)}, u32[]{:S(2)}, u32[]{:S(2)}) collective-permute-start(f32[128,256]{1,0:T(8,128)S(1)} %get-tuple-element.18), channel_id=1, source_target_pairs={{0,4},{4,0},{8,12},{12,8},{16,20},{20,16},{24,28},{28,24},{32,36},... | collective-permute-start | bytes 393224 | tf_op jit(solution)/shard_map/ppermute | solution.py:257
  12.5 22.4 %collective-permute-start.3 = (f32[128,256]{1,0:T(8,128)S(1)}, f32[128,256]{1,0:T(8,128)S(1)}, u32[]{:S(2)}, u32[]{:S(2)}) collective-permute-start(f32[128,256]{1,0:T(8,128)S(1)} %add.56), channel_id=1, source_target_pairs={{0,3},{1,0},{2,1},{3,2},{4,7},{5,4},{6,5},{7,6},{8,11},{9,8},{10,9... | collective-permute-start | bytes 393224 | tf_op jit(solution)/shard_map/ppermute | solution.py:252
  15.5 20.9 %collective-permute-start.2 = (f32[128,256]{1,0:T(8,128)S(1)}, f32[128,256]{1,0:T(8,128)S(1)}, u32[]{:S(2)}, u32[]{:S(2)}) collective-permute-start(f32[128,256]{1,0:T(8,128)S(1)} %add.56), channel_id=1, source_target_pairs={{0,1},{1,2},{2,3},{3,0},{4,5},{5,6},{6,7},{7,4},{8,9},{9,10},{10,1... | collective-permute-start | bytes 393224 | tf_op jit(solution)/shard_map/ppermute | solution.py:252
  15.5 21.3 %collective-permute-start.1 = (f32[128,256]{1,0:T(8,128)S(1)}, f32[128,256]{1,0:T(8,128)S(1)}, u32[]{:S(2)}, u32[]{:S(2)}) collective-permute-start(f32[128,256]{1,0:T(8,128)S(1)} %add.56), channel_id=1, source_target_pairs={{0,2},{1,3},{2,0},{3,1},{4,6},{5,7},{6,4},{7,5},{8,10},{9,11},{10,... | collective-permute-start | bytes 393224 | tf_op jit(solution)/shard_map/ppermute | solution.py:252
  36.8 8.0 %collective-permute-start.6 = (f32[128,256]{1,0:T(8,128)S(1)}, f32[128,256]{1,0:T(8,128)S(1)}, u32[]{:S(2)}, u32[]{:S(2)}) collective-permute-start(f32[128,256]{1,0:T(8,128)S(1)} %add_add_fusion.4), channel_id=1, source_target_pairs={{0,24},{4,100},{8,0},{12,108},{16,8},{20,116},{24,16},{28,124},{32... | collective-permute-start | bytes 393224 | tf_op jit(solution)/shard_map/ppermute | solution.py:252
  40.6 6.7 %collective-permute-start.5 = (f32[128,256]{1,0:T(8,128)S(1)}, f32[128,256]{1,0:T(8,128)S(1)}, u32[]{:S(2)}, u32[]{:S(2)}) collective-permute-start(f32[128,256]{1,0:T(8,128)S(1)} %add_add_fusion.4), channel_id=1, source_target_pairs={{0,8},{4,36},{8,16},{12,44},{16,24},{20,52},{24,0},{28,60},{32,40}... | collective-permute-start | bytes 393224 | tf_op jit(solution)/shard_map/ppermute | solution.py:252
  40.6 6.7 %collective-permute-start.4 = (f32[128,256]{1,0:T(8,128)S(1)}, f32[128,256]{1,0:T(8,128)S(1)}, u32[]{:S(2)}, u32[]{:S(2)}) collective-permute-start(f32[128,256]{1,0:T(8,128)S(1)} %add_add_fusion.4), channel_id=1, source_target_pairs={{0,16},{4,68},{8,24},{12,76},{16,0},{20,84},{24,8},{28,92},{32,48}... | collective-permute-start | bytes 393224 | tf_op jit(solution)/shard_map/ppermute | solution.py:252
  42.0 45.2 %collective-permute-start.15 = (f32[1024,256]{1,0:T(8,128)}, f32[1024,256]{1,0:T(8,128)S(1)}, u32[]{:S(2)}, u32[]{:S(2)}) collective-permute-start(f32[1024,256]{1,0:T(8,128)} %collective-permute-done.11.refs_2_.refs_5_), channel_id=1, source_target_pairs={{0,1},{1,2},{2,3},{3,0},{4,5},{5,6},{6,7},{7,4},{8,9},{9,10},{10,1... | collective-permute-start | bytes 3145736 | tf_op jit(solution)/shard_map/ppermute | solution.py:277
  42.0 45.2 %collective-permute-start.16 = (f32[1024,256]{1,0:T(8,128)S(1)}, f32[1024,256]{1,0:T(8,128)S(1)}, u32[]{:S(2)}, u32[]{:S(2)}) collective-permute-start(f32[1024,256]{1,0:T(8,128)S(1)} %collective-permute-done.12.refs_3_.refs_8_), channel_id=1, source_target_pairs={{0,3},{1,0},{2,1},{3,2},{4,7},{5,4},{6,5},{7,6},{8,11},{9,8},{10,9... | collective-permute-start | bytes 3145736 | tf_op jit(solution)/shard_map/ppermute | solution.py:278
  44.8 42.4 %collective-permute-start.14 = (f32[1024,256]{1,0:T(8,128)S(1)}, f32[1024,256]{1,0:T(8,128)S(1)}, u32[]{:S(2)}, u32[]{:S(2)}) collective-permute-start(f32[1024,256]{1,0:T(8,128)S(1)} %get-tuple-element.31), channel_id=1, source_target_pairs={{0,3},{1,0},{2,1},{3,2},{4,7},{5,4},{6,5},{7,6},{8,11},{9,8},{10,9... | collective-permute-start | bytes 3145736 | tf_op jit(solution)/shard_map/ppermute | solution.py:276
  47.4 40.0 %collective-permute-start.13 = (f32[1024,256]{1,0:T(8,128)S(1)}, f32[1024,256]{1,0:T(8,128)S(1)}, u32[]{:S(2)}, u32[]{:S(2)}) collective-permute-start(f32[1024,256]{1,0:T(8,128)S(1)} %get-tuple-element.32), channel_id=1, source_target_pairs={{0,1},{1,2},{2,3},{3,0},{4,5},{5,6},{6,7},{7,4},{8,9},{9,10},{10,1... | collective-permute-start | bytes 3145736 | tf_op jit(solution)/shard_map/ppermute | solution.py:275
  47.4 4.5 %collective-permute-start.9 = (f32[128,256]{1,0:T(8,128)S(1)}, f32[128,256]{1,0:T(8,128)S(1)}, u32[]{:S(2)}, u32[]{:S(2)}) collective-permute-start(f32[128,256]{1,0:T(8,128)S(1)} %add_add_fusion.3), channel_id=1, source_target_pairs={{0,96},{4,28},{8,104},{12,4},{16,112},{20,12},{24,120},{28,20},{32... | collective-permute-start | bytes 393224 | tf_op jit(solution)/shard_map/ppermute | solution.py:252
  51.9 6.0 %collective-permute-start.8 = (f32[128,256]{1,0:T(8,128)S(1)}, f32[128,256]{1,0:T(8,128)S(1)}, u32[]{:S(2)}, u32[]{:S(2)}) collective-permute-start(f32[128,256]{1,0:T(8,128)S(1)} %add_add_fusion.3), channel_id=1, source_target_pairs={{0,32},{4,12},{8,40},{12,20},{16,48},{20,28},{24,56},{28,4},{32,64... | collective-permute-start | bytes 393224 | tf_op jit(solution)/shard_map/ppermute | solution.py:252
  57.9 5.3 %collective-permute-start.7 = (f32[128,256]{1,0:T(8,128)S(1)}, f32[128,256]{1,0:T(8,128)S(1)}, u32[]{:S(2)}, u32[]{:S(2)}) collective-permute-start(f32[128,256]{1,0:T(8,128)S(1)} %add_add_fusion.3), channel_id=1, source_target_pairs={{0,64},{4,20},{8,72},{12,28},{16,80},{20,4},{24,88},{28,12},{32,96... | collective-permute-start | bytes 393224 | tf_op jit(solution)/shard_map/ppermute | solution.py:252
  63.3 8.2 %collective-permute-start.10 = (f32[128,256]{1,0:T(8,128)S(1)}, f32[128,256]{1,0:T(8,128)S(1)}, u32[]{:S(2)}, u32[]{:S(2)}) collective-permute-start(f32[128,256]{1,0:T(8,128)S(1)} %add_add_fusion.2.refs_1_), channel_id=1, source_target_pairs={{0,4},{4,0},{8,12},{12,8},{16,20},{20,16},{24,28},{28,24},{32,36},... | collective-permute-start | bytes 393224 | tf_op jit(solution)/shard_map/ppermute | solution.py:257
  87.1 3.4 %copy-start.1 = (f32[1024,256]{1,0:T(8,128)}, f32[1024,256]{1,0:T(8,128)S(1)}, u32[]{:S(2)}) copy-start(f32[1024,256]{1,0:T(8,128)S(1)} %collective-permute-done.16.refs_3_.refs_10_) | copy-start | bytes 3145732
  93.8 5.2 %collective-permute-start.17 = (f32[128,256]{1,0:T(8,128)S(1)}, f32[128,256]{1,0:T(8,128)S(1)}, u32[]{:S(2)}, u32[]{:S(2)}) collective-permute-start(f32[128,256]{1,0:T(8,128)S(1)} %get-tuple-element.27), channel_id=1, source_target_pairs={{0,4},{4,0},{8,12},{12,8},{16,20},{20,16},{24,28},{28,24},{32,36},... | collective-permute-start | bytes 393224 | tf_op jit(solution)/shard_map/ppermute | solution.py:257
  99.0 4.7 %collective-permute-start.20 = (f32[128,256]{1,0:T(8,128)S(1)}, f32[128,256]{1,0:T(8,128)S(1)}, u32[]{:S(2)}, u32[]{:S(2)}) collective-permute-start(f32[128,256]{1,0:T(8,128)S(1)} %add.66), channel_id=1, source_target_pairs={{0,24},{4,100},{8,0},{12,108},{16,8},{20,116},{24,16},{28,124},{32... | collective-permute-start | bytes 393224 | tf_op jit(solution)/shard_map/ppermute | solution.py:252
  100.5 6.7 %collective-permute-start.19 = (f32[128,256]{1,0:T(8,128)S(1)}, f32[128,256]{1,0:T(8,128)S(1)}, u32[]{:S(2)}, u32[]{:S(2)}) collective-permute-start(f32[128,256]{1,0:T(8,128)S(1)} %add.66), channel_id=1, source_target_pairs={{0,8},{4,36},{8,16},{12,44},{16,24},{20,52},{24,0},{28,60},{32,40}... | collective-permute-start | bytes 393224 | tf_op jit(solution)/shard_map/ppermute | solution.py:252
  101.1 6.1 %collective-permute-start.18 = (f32[128,256]{1,0:T(8,128)S(1)}, f32[128,256]{1,0:T(8,128)S(1)}, u32[]{:S(2)}, u32[]{:S(2)}) collective-permute-start(f32[128,256]{1,0:T(8,128)S(1)} %add.66), channel_id=1, source_target_pairs={{0,16},{4,68},{8,24},{12,76},{16,0},{20,84},{24,8},{28,92},{32,48}... | collective-permute-start | bytes 393224 | tf_op jit(solution)/shard_map/ppermute | solution.py:252
  107.3 4.4 %collective-permute-start.23 = (f32[128,256]{1,0:T(8,128)S(1)}, f32[128,256]{1,0:T(8,128)S(1)}, u32[]{:S(2)}, u32[]{:S(2)}) collective-permute-start(f32[128,256]{1,0:T(8,128)S(1)} %add_add_fusion.1), channel_id=1, source_target_pairs={{0,96},{4,28},{8,104},{12,4},{16,112},{20,12},{24,120},{28,20},{32... | collective-permute-start | bytes 393224 | tf_op jit(solution)/shard_map/ppermute | solution.py:252
  109.8 6.7 %collective-permute-start.22 = (f32[128,256]{1,0:T(8,128)S(1)}, f32[128,256]{1,0:T(8,128)S(1)}, u32[]{:S(2)}, u32[]{:S(2)}) collective-permute-start(f32[128,256]{1,0:T(8,128)S(1)} %add_add_fusion.1), channel_id=1, source_target_pairs={{0,32},{4,12},{8,40},{12,20},{16,48},{20,28},{24,56},{28,4},{32,64... | collective-permute-start | bytes 393224 | tf_op jit(solution)/shard_map/ppermute | solution.py:252
  109.8 6.7 %collective-permute-start.21 = (f32[128,256]{1,0:T(8,128)S(1)}, f32[128,256]{1,0:T(8,128)S(1)}, u32[]{:S(2)}, u32[]{:S(2)}) collective-permute-start(f32[128,256]{1,0:T(8,128)S(1)} %add_add_fusion.1), channel_id=1, source_target_pairs={{0,64},{4,20},{8,72},{12,28},{16,80},{20,4},{24,88},{28,12},{32,96... | collective-permute-start | bytes 393224 | tf_op jit(solution)/shard_map/ppermute | solution.py:252
  116.5 4.0 %collective-permute-start.24 = (f32[128,256]{1,0:T(8,128)S(1)}, f32[128,256]{1,0:T(8,128)S(1)}, u32[]{:S(2)}, u32[]{:S(2)}) collective-permute-start(f32[128,256]{1,0:T(8,128)S(1)} %add_add_fusion.refs_1_), channel_id=1, source_target_pairs={{0,4},{4,0},{8,12},{12,8},{16,20},{20,16},{24,28},{28,24},{32,36},... | collective-permute-start | bytes 393224 | tf_op jit(solution)/shard_map/ppermute | solution.py:257

commit v2 on v0

v2 whole, which is shorter than its diff:
```python
import math

import jax
import jax.numpy as jnp
from jax import lax
from jax.experimental import pallas as pl
from jax.experimental.pallas import tpu as pltpu
from jax.sharding import PartitionSpec as P

F32, BF16 = jnp.float32, jnp.bfloat16
HIGHEST = lax.Precision.HIGHEST
BLOCK = 512
UPDATE_VMEM = 28 << 20
CROSS_VMEM = 16 << 20

def split(value):
    high = value.astype(BF16)
    return high, (value - high.astype(F32)).astype(BF16)

def contract(left, right, dims, precision=None):
    return lax.dot_general(left, right, (dims, ((), ())), precision=precision, preferred_element_type=F32)

def factor_block(block, group):
    size = block.shape[0]
    lane = lax.broadcasted_iota(jnp.int32, (size, 2 * size), 1)
    row = lax.broadcasted_iota(jnp.int32, (size, 2 * size), 0)
    wide = jnp.concatenate([block, jnp.zeros((size, size), F32)], axis=1)
    wide = jnp.where(lane == row + size, 1.0, wide)
    for first in range(0, size, group):
        columns = [jnp.broadcast_to(wide[:, first + g : first + g + 1], wide.shape) for g in range(group)]
        rows = [wide[first + g : first + g + 1, :] for g in range(group)]
        small = [[columns[j][first + i : first + i + 1, :] for j in range(group)] for i in range(group)]
        change = None
        for g in range(group):
            inv = 1.0 / small[g][g]
            scaled = rows[g] * inv
            for i in range(g + 1, group):
                ratio = small[i][g] * inv
                rows[i] = rows[i] - ratio * rows[g]
                for j in range(g + 1, group):
                    small[i][j] = small[i][j] - ratio * small[g][j]
            for j in range(g + 1, group):
                columns[j] = columns[j] - columns[g] * (small[g][j] * inv)
            term = jnp.where(row > first + g, columns[g] * scaled, 0.0)
            change = term if change is None else change + term
        wide = wide - change
    diagonal = jnp.sum(jnp.where(lane == row, wide, 0.0), axis=1, keepdims=True)
    wide = wide * lax.rsqrt(diagonal)
    return wide

def factor_kernel(shrink, size, group, core, mine, other, r_factor, inverse, work):
    @pl.when(core[0] == 0)
    def _():
        work[:128, :256] = mine[...]
        work[128:, :256] = other[...]
    @pl.when(core[0] != 0)
    def _():
        work[:128, :256] = other[...]
        work[128:, :256] = mine[...]
    rows = lax.broadcasted_iota(jnp.int32, (256, 256), 0)
    lanes = lax.broadcasted_iota(jnp.int32, (256, 256), 1)
    work[:, 256:] = (rows == lanes).astype(F32)
    for first in range(0, 256, size):
        last = first + size
        both = factor_block(work[first:last, first:last], group)
        done = contract(both[:, size:], work[first:last, :], ((1,), (0,)), HIGHEST)
        work[first:last, :] = done
        if last < 256:
            work[last:, :] -= contract(done[:, last:256], done, ((0,), (0,)), HIGHEST)
    r_factor[...] = jnp.where(rows <= lanes, work[:, :256], 0.0) * shrink
    inverse[...] = jnp.where(rows >= lanes, work[:, 256:], 0.0)

def factor(core, mine, other, shrink, size=64, group=4):
    full = jax.ShapeDtypeStruct((256, 256), F32)
    return pl.pallas_call(
        lambda *refs: factor_kernel(shrink, size, group, *refs),
        out_shape=[full, full],
        in_specs=[pl.BlockSpec(memory_space=pltpu.SMEM), pl.BlockSpec(memory_space=pltpu.VMEM), pl.BlockSpec(memory_space=pltpu.VMEM)],
        out_specs=[pl.BlockSpec(memory_space=pltpu.VMEM)] * 2,
        scratch_shapes=[pltpu.VMEM((256, 512), F32)],
        cost_estimate=pl.CostEstimate(flops=8000000000, bytes_accessed=0, transcendentals=0),
        compiler_params=pltpu.CompilerParams(vmem_limit_bytes=16 << 20),
    )(core, mine, other)

def blocks_of(pieces, block):
    return [
        (n, row, offset, low + row)
        for n, (count, offset, low) in enumerate(pieces)
        for row in range(0, count, block)
    ]


def rows_at(column, offset, low, chunk, block):
    return pl.ds(pl.multiple_of(lax.rem(column + offset, 4) * chunk + low, block), block)


def update_kernel(shrink, blocks, block, chunk, place, mine, other, inverse, *refs):
    *pieces, trailing, updated, r_cross, result, weights, sems = refs
    first = place[1] == 0
    top = jnp.where(first, mine[...], other[...])
    bottom = jnp.where(first, other[...], mine[...])
    coupling = contract(inverse[...], jnp.concatenate([top, bottom], axis=0), ((1,), (0,)), HIGHEST)
    r_cross[...] = coupling * shrink
    high, low = split(contract(inverse[...], coupling, ((0,), (0,)), HIGHEST))
    weights[:256, :] = high
    weights[256:512, :] = high
    weights[512:, :] = low
    stores = []
    for n, (piece, row, offset, low_row) in enumerate(blocks):
        rows = rows_at(place[0], offset, low_row, chunk, block)
        high, low = split(pieces[piece][row : row + block, :])
        product = contract(jnp.concatenate([high, low, high], axis=1), weights[...], ((1,), (0,)))
        here = pl.ds(n * block, block)
        result[here, :] = trailing[rows, :] - product
        store = pltpu.make_async_copy(result.at[here], updated.at[rows], sems.at[n])
        store.start()
        stores.append(store)
    for store in stores:
        store.wait()


def update(mine, other, inverse, pieces, spots, trailing, place, shrink, block):
    blocks = blocks_of(spots, block)
    vmem, anywhere = pl.BlockSpec(memory_space=pltpu.VMEM), pl.BlockSpec(memory_space=pl.ANY)
    total = trailing.shape[0]
    return pl.pallas_call(
        lambda *refs: update_kernel(shrink, blocks, block, total // 4, *refs),
        out_shape=[jax.ShapeDtypeStruct(trailing.shape, F32), jax.ShapeDtypeStruct((256, 256), F32)],
        in_specs=[pl.BlockSpec(memory_space=pltpu.SMEM), *[vmem] * (len(pieces) + 4)],
        out_specs=[anywhere, vmem],
        scratch_shapes=[
            pltpu.VMEM((total, 256), F32),
            pltpu.VMEM((768, 256), BF16),
            pltpu.SemaphoreType.DMA((len(blocks),)),
        ],
        compiler_params=pltpu.CompilerParams(vmem_limit_bytes=UPDATE_VMEM),
    )(place, mine, other, inverse, *pieces, trailing)


def cross_kernel(initial, halves, blocks, block, chunk, place, *refs):
    refs = list(refs)
    total = refs.pop(0)[...] if initial else None
    count = 2 if halves else 1
    *pieces, trailing = refs[:-count]
    outs = refs[-count:]
    for piece, row, offset, low in blocks:
        left = split(pieces[piece][row : row + block, :])
        right = split(trailing[rows_at(place[0], offset, low, chunk, block), :])
        product = contract(
            jnp.concatenate([left[0], left[1], left[0]], axis=0),
            jnp.concatenate([right[0], right[0], right[1]], axis=0),
            ((0,), (0,)),
        )
        total = product if total is None else total + product
    if halves:
        first = place[1] == 0
        outs[0][...] = jnp.where(first, total[:128, :], total[128:, :])
        outs[1][...] = jnp.where(first, total[128:, :], total[:128, :])
    else:
        outs[0][...] = total


def cross_part(place, initial, pieces, spots, trailing, halves, block):
    blocks = blocks_of(spots, block)
    vmem = pl.BlockSpec(memory_space=pltpu.VMEM)
    given = [] if initial is None else [initial]
    shapes = [(128, 256)] * 2 if halves else [(256, 256)]
    return pl.pallas_call(
        lambda *refs: cross_kernel(bool(given), halves, blocks, block, trailing.shape[0] // 4, *refs),
        out_shape=[jax.ShapeDtypeStruct(shape, F32) for shape in shapes],
        in_specs=[pl.BlockSpec(memory_space=pltpu.SMEM), *[vmem] * (len(given) + len(pieces) + 1)],
        out_specs=[vmem] * len(shapes),
        compiler_params=pltpu.CompilerParams(vmem_limit_bytes=CROSS_VMEM),
    )(place, *given, *pieces, trailing)


def gram_kernel(place, panel, keep, send):
    @pl.when(pl.program_id(0) == 0)
    def _():
        keep[...] = jnp.zeros_like(keep)
        send[...] = jnp.zeros_like(send)
    part = contract(panel[...], panel[...], ((0,), (0,)), HIGHEST)
    @pl.when(place[1] == 0)
    def _():
        keep[...] += part[:128, :]
        send[...] += part[128:, :]
    @pl.when(place[1] != 0)
    def _():
        keep[...] += part[128:, :]
        send[...] += part[:128, :]

def gram_part(place, panel, block=1024):
    half = pl.BlockSpec((128, 256), lambda i, place: (0, 0))
    return pl.pallas_call(
        gram_kernel,
        out_shape=[jax.ShapeDtypeStruct((128, 256), F32)] * 2,
        grid_spec=pltpu.PrefetchScalarGridSpec(
            num_scalar_prefetch=1, grid=(panel.shape[0] // block,),
            in_specs=[pl.BlockSpec((block, 256), lambda i, place: (i, 0))],
            out_specs=[half, half]),
        compiler_params=pltpu.CompilerParams(vmem_limit_bytes=32 << 20),
    )(place, panel)


def over_rows(move):
    pairs = []
    for z in range(4):
        for x in range(4):
            for core in range(2):
                z2, x2, core2 = move(z, x, core)
                pairs.append(((z * 4 + x) * 2 + core, (z2 % 4 * 4 + x2 % 4) * 2 + core2))
    return pairs


ORDER = (1, 3, 2)


PARTNER = over_rows(lambda z, x, core: (z, x, 1 - core))
FIRST = [over_rows(lambda z, x, core, k=k: (z, x + k, core) if core == 0 else (z + k, x, core)) for k in ORDER]
SECOND = [over_rows(lambda z, x, core, k=k: (z + k, x, core) if core == 0 else (z, x + k, core)) for k in ORDER]


def around(k):
    return [(i, (i + k) % 4) for i in range(4)]


def move(name, part, axis, pairs):
    with jax.named_scope(name):
        return lax.ppermute(part, axis, pairs)


def exchange_sum(name, part, axis, moves):
    others = [move(name, part, axis, pairs) for pairs in moves]
    return (part + others[2]) + (others[0] + others[1])


def partner(name, part):
    return move(name, part, "rows", PARTNER)


def local(panel_cols, trailing):
    rows_total = trailing.shape[0] * lax.axis_size("rows")
    shrink = 1.0 / math.sqrt(rows_total)
    core = lax.axis_index("rows") % 2
    place = jnp.stack([lax.axis_index("cols"), core]).astype(jnp.int32)
    size = panel_cols.shape[0]
    half = size // 2
    barrier = lax.optimization_barrier
    left = move("left", panel_cols, "cols", around(1))
    right = move("right", panel_cols, "cols", around(-1))

    keep, send = gram_part(place, panel_cols)
    gram = keep + partner("gram_halves", send)
    gram = exchange_sum("gram_first", gram, "rows", FIRST)
    gram = exchange_sum("gram_second", gram, "rows", SECOND)
    left, _ = barrier((left, gram))
    right, _ = barrier((right, gram))
    far1 = move("far1", left[:half], "cols", around(1))
    far2 = move("far2", right[half:], "cols", around(-1))
    gram = exchange_sum("gram_cols", gram, "cols", [around(k) for k in ORDER])
    r_factor, inverse = factor(place[1:], gram, partner("gram_join", gram), shrink, 64, 8)

    (cross,) = cross_part(place, None, (panel_cols, left, right), ((size, 0, 0), (size, 3, 0), (size, 1, 0)), trailing, False, BLOCK)
    inverse, far1, far2, cross = barrier((inverse, far1, far2, cross))
    keep, send = cross_part(place, cross, (far1, far2), ((half, 2, 0), (half, 2, half)), trailing, True, BLOCK)
    cross = keep + partner("cross_halves", send)
    cross = exchange_sum("cross_first", cross, "rows", FIRST)
    cross = exchange_sum("cross_second", cross, "rows", SECOND)
    pieces = (panel_cols, left, right, far1, far2)
    spots = ((size, 0, 0), (size, 3, 0), (size, 1, 0), (half, 2, 0), (half, 2, half))
    updated, r_cross = update(cross, partner("cross_join", cross), inverse, pieces, spots, trailing, place, shrink, BLOCK)
    return (r_factor, r_cross, updated)


def solution(mesh):
    in_specs = (P(("rows", "cols"), None), P("rows", "cols"))
    out_specs = (P(), P(None, "cols"), P("rows", "cols"))
    return jax.shard_map(local, mesh=mesh, in_specs=in_specs, out_specs=out_specs, check_vma=False)
```

time: 447 us -> 117 us (0.26)
  waiting for transfers between devices: 327 us -> 43.2 us
  other arithmetic: 55.4 us -> 0.29 us
  matrix products: 41.2 us -> 0 us
  starting transfers between devices: 0.3 us -> 41.5 us
  Pallas kernels: 0 us -> 28.2 us
  between operations: 15.2 us -> 0.92 us
  local copies, waits for them, and re-layouts: 7.51 us -> 3 us
    psum x2 -> x0, waiting for transfers between devices: 247 us -> none  [the longest x1 145 us: local(): gram_sum = lax.psum(matmul(panel_cols.T, panel_cols), ('rows', 'cols'))]
    all_gather x1 -> x0, waiting for transfers between devices: 80.6 us -> none  [local(): orthonormal = lax.all_gather(basis_part, 'cols', axis=0, tiled=True)]
    another operation x9 -> x1, other arithmetic: 53.7 us -> 0.07 us  [local(): place = jnp.stack([lax.axis_index('cols'), core]).astype(jnp.int32)]
    ppermute x0 -> x23, waiting for transfers between devices: none -> 43.2 us  [move(): return lax.ppermute(part, axis, pairs)]
    ppermute x0 -> x23, starting transfers between devices: none -> 41.5 us  [move(): return lax.ppermute(part, axis, pairs)]
    dot_general x4 -> x0, matrix products: 39.9 us -> none  [matmul(): return jnp.dot(left, right, precision=lax.Precision.HIGHEST)]
    pallas_call x0 -> x5, Pallas kernels: none -> 28.2 us  [the longest x1 10.2 us: factor(): pl.pallas_call(lambda *refs: factor_kernel(shrink, size, group, *refs), o...]
  transfers between devices with their start and end apart: 3 -> 23, of which waited for: 3 -> 17; matrix products, arithmetic and copies ran while one was open for 0% -> 1% of each run, Pallas kernels for 0% -> 15%
where the time goes in v2:
time: 117 us
  waiting for transfers between devices  43.2 us (37%)
  starting transfers between devices  41.5 us (35%)
  Pallas kernels  28.2 us (24%)
  local copies, waits for them, and re-layouts  3 us (3%)
    ppermute x23, waiting for transfers between devices, move(): return lax.ppermute(part, axis, pairs)  43.2 us
    ppermute x23, starting transfers between devices, move(): return lax.ppermute(part, axis, pairs)  41.5 us
    pallas_call x1, Pallas kernels, factor(): pl.pallas_call(lambda *refs: factor_kernel(shrink, size, group, *refs), o...  10.2 us
    pallas_call x1, Pallas kernels, update(): pl.pallas_call(lambda *refs: update_kernel(shrink, blocks, block, total /...  8.58 us
    pallas_call x2, Pallas kernels, cross_part(): pl.pallas_call(lambda *refs: cross_kernel(bool(given), halves, blocks, bl...  6.33 us
    pallas_call x1, Pallas kernels, gram_part(): pl.pallas_call(gram_kernel, out_shape=[jax.ShapeDtypeStruct((128, 256), F...  3.05 us
  transfers between devices with their start and end apart: 23, of which 17 were waited for; matrix products, arithmetic and copies ran while one was open for 1% of the time, Pallas kernels for 15%

profile of v2, /device:TPU:1, one launch (start us, length us, event | category | flops | bytes accessed | tf_op | source)
XLA Modules:
  0.0 117.0 jit_solution(7598927549612178741)
XLA Ops:
  0.6 3.6 %collective-permute-start.13 = (f32[2048,256]{1,0:T(8,128)}, f32[2048,256]{1,0:T(8,128)S(1)}, u32[]{:S(2)}, u32[]{:S(2)}) collective-permute-start(f32[2048,256]{1,0:T(8,128)} %refs_4_.5), channel_id=1, source_target_pairs={{0,3},{1,0},{2,1},{3,2},{4,7},{5,4},{6,5},{7,6},{8,11},{9,8},{10,9... | collective-permute-start | bytes 6291464 | tf_op jit(solution)/shard_map/right/ppermute | solution.py:229
  4.3 1.6 %copy-done = f32[2048,256]{1,0:T(8,128)S(1)} copy-done((f32[2048,256]{1,0:T(8,128)S(1)}, f32[2048,256]{1,0:T(8,128)}, u32[]{:S(2)}) %copy-start) | copy-done | bytes 2097176
  6.0 3.0 %shard_map.49 = (f32[128,256]{1,0:T(8,128)S(1)}, f32[128,256]{1,0:T(8,128)S(1)}) custom-call(s32[2]{0:T(128)S(1)} %pad_add_fusion.place.refs_0_, f32[2048,256]{1,0:T(8,128)S(1)} %copy-done), custom_call_target="tpu_custom_call" | custom-call | tf_op jit(solution)/shard_map/pallas_call | solution.py:194
  9.0 1.0 collective-permute-start
  10.1 1.0 collective-permute-done
  11.1 3.8 %collective-permute-start.3 = (f32[128,256]{1,0:T(8,128)S(1)}, f32[128,256]{1,0:T(8,128)S(1)}, u32[]{:S(2)}, u32[]{:S(2)}) collective-permute-start(f32[128,256]{1,0:T(8,128)S(1)} %add.56), channel_id=1, source_target_pairs={{0,24},{4,100},{8,0},{12,108},{16,8},{20,116},{24,16},{28,124},{32... | collective-permute-start | bytes 393224 | tf_op jit(solution)/shard_map/gram_first/ppermute | solution.py:229
  14.9 1.3 %collective-permute-start.1 = (f32[128,256]{1,0:T(8,128)S(1)}, f32[128,256]{1,0:T(8,128)S(1)}, u32[]{:S(2)}, u32[]{:S(2)}) collective-permute-start(f32[128,256]{1,0:T(8,128)S(1)} %add.56), channel_id=1, source_target_pairs={{0,16},{4,68},{8,24},{12,76},{16,0},{20,84},{24,8},{28,92},{32,48}... | collective-permute-start | bytes 393224 | tf_op jit(solution)/shard_map/gram_first/ppermute | solution.py:229
  16.8 4.9 %collective-permute-done.2 = f32[128,256]{1,0:T(8,128)S(1)} collective-permute-done((f32[128,256]{1,0:T(8,128)S(1)}, f32[128,256]{1,0:T(8,128)S(1)}, u32[]{:S(2)}, u32[]{:S(2)}) %collective-permute-start.2) | collective-permute-done | bytes 131104 | tf_op jit(solution)/shard_map/gram_first/ppermute | solution.py:229
  21.8 2.5 %collective-permute-start.6 = (f32[128,256]{1,0:T(8,128)S(1)}, f32[128,256]{1,0:T(8,128)S(1)}, u32[]{:S(2)}, u32[]{:S(2)}) collective-permute-start(f32[128,256]{1,0:T(8,128)S(1)} %add_add_fusion.4), channel_id=1, source_target_pairs={{0,96},{4,28},{8,104},{12,4},{16,112},{20,12},{24,120},{28,20},{32... | collective-permute-start | bytes 393224 | tf_op jit(solution)/shard_map/gram_second/ppermute | solution.py:229
  24.3 1.7 %collective-permute-start.4 = (f32[128,256]{1,0:T(8,128)S(1)}, f32[128,256]{1,0:T(8,128)S(1)}, u32[]{:S(2)}, u32[]{:S(2)}) collective-permute-start(f32[128,256]{1,0:T(8,128)S(1)} %add_add_fusion.4), channel_id=1, source_target_pairs={{0,64},{4,20},{8,72},{12,28},{16,80},{20,4},{24,88},{28,12},{32,96... | collective-permute-start | bytes 393224 | tf_op jit(solution)/shard_map/gram_second/ppermute | solution.py:229
  26.3 4.9 %collective-permute-done.5 = f32[128,256]{1,0:T(8,128)S(1)} collective-permute-done((f32[128,256]{1,0:T(8,128)S(1)}, f32[128,256]{1,0:T(8,128)S(1)}, u32[]{:S(2)}, u32[]{:S(2)}) %collective-permute-start.5) | collective-permute-done | bytes 131104 | tf_op jit(solution)/shard_map/gram_second/ppermute | solution.py:229
  31.2 2.8 %collective-permute-start.9 = (f32[128,256]{1,0:T(8,128)S(1)}, f32[128,256]{1,0:T(8,128)S(1)}, u32[]{:S(2)}, u32[]{:S(2)}) collective-permute-start(f32[128,256]{1,0:T(8,128)S(1)} %add_add_fusion.3), channel_id=1, source_target_pairs={{0,3},{1,0},{2,1},{3,2},{4,7},{5,4},{6,5},{7,6},{8,11},{9,8},{10,9... | collective-permute-start | bytes 393224 | tf_op jit(solution)/shard_map/gram_cols/ppermute | solution.py:229
  34.0 1.3 %collective-permute-start.7 = (f32[128,256]{1,0:T(8,128)S(1)}, f32[128,256]{1,0:T(8,128)S(1)}, u32[]{:S(2)}, u32[]{:S(2)}) collective-permute-start(f32[128,256]{1,0:T(8,128)S(1)} %add_add_fusion.3), channel_id=1, source_target_pairs={{0,2},{1,3},{2,0},{3,1},{4,6},{5,7},{6,4},{7,5},{8,10},{9,11},{10,... | collective-permute-start | bytes 393224 | tf_op jit(solution)/shard_map/gram_cols/ppermute | solution.py:229
  35.2 13.6 %collective-permute-done.13.refs_3_.refs_6_ = f32[2048,256]{1,0:T(8,128)S(1)} collective-permute-done((f32[2048,256]{1,0:T(8,128)}, f32[2048,256]{1,0:T(8,128)S(1)}, u32[]{:S(2)}, u32[]{:S(2)}) %collective-permute-start.13) | collective-permute-done | bytes 2097184 | tf_op jit(solution)/shard_map/right/ppermute | solution.py:229
  48.9 3.4 %collective-permute-start.14 = (f32[1024,256]{1,0:T(8,128)S(1)}, f32[1024,256]{1,0:T(8,128)S(1)}, u32[]{:S(2)}, u32[]{:S(2)}) collective-permute-start(f32[1024,256]{1,0:T(8,128)S(1)} %slice.7), channel_id=1, source_target_pairs={{0,3},{1,0},{2,1},{3,2},{4,7},{5,4},{6,5},{7,6},{8,11},{9,8},{10,9... | collective-permute-start | bytes 3145736 | tf_op jit(solution)/shard_map/far2/ppermute | solution.py:229
  52.3 1.3 %slice.6 = f32[1024,256]{1,0:T(8,128)S(1)} slice(f32[2048,256]{1,0:T(8,128)} %collective-permute-done.11.refs_2_.refs_5_), slice={[0:1024], [0:256]} | slice | bytes 2097152 | tf_op jit(solution)/shard_map/slice | solution.py:258
  53.7 2.1 %collective-permute-done.8 = f32[128,256]{1,0:T(8,128)S(1)} collective-permute-done((f32[128,256]{1,0:T(8,128)S(1)}, f32[128,256]{1,0:T(8,128)S(1)}, u32[]{:S(2)}, u32[]{:S(2)}) %collective-permute-start.8) | collective-permute-done | bytes 131104 | tf_op jit(solution)/shard_map/gram_cols/ppermute | solution.py:229
  56.2 3.7 %collective-permute-start.10 = (f32[128,256]{1,0:T(8,128)S(1)}, f32[128,256]{1,0:T(8,128)S(1)}, u32[]{:S(2)}, u32[]{:S(2)}) collective-permute-start(f32[128,256]{1,0:T(8,128)S(1)} %add_add_fusion.2.refs_1_), channel_id=1, source_target_pairs={{0,4},{4,0},{8,12},{12,8},{16,20},{20,16},{24,28},{28,24},{32,36},... | collective-permute-start | bytes 393224 | tf_op jit(solution)/shard_map/gram_join/ppermute | solution.py:229
  60.9 10.2 %shard_map.50 = (f32[256,256]{1,0:T(8,128)}, f32[256,256]{1,0:T(8,128)S(1)}) custom-call(s32[1]{0:T(128)} %bitcast.refs_0_, f32[128,256]{1,0:T(8,128)S(1)} %add_add_fusion.2.refs_1_, f32[128,256]{1,0:T(8,128)S(1)} %collective-permute-done.10.refs_2_), custom_call_target="tpu_custom_call" | custom-call | flops 8000000000 | tf_op jit(solution)/shard_map/pallas_call | solution.py:75
  71.1 4.6 %shard_map.51.refs_1_ = f32[256,256]{1,0:T(8,128)S(1)} custom-call(s32[2]{0:T(128)S(1)} %pad_add_fusion.place.refs_0_, f32[2048,256]{1,0:T(8,128)S(1)} %copy-done, f32[2048,256]{1,0:T(8,128)} %collective-permute-done.11.refs_2_.refs_5_, f32[2048,256]{1,0:T(8,128)S(1)} %collective-permute-done.13.refs_3_.refs_6_, f32[8192,256]{1,0:T(8,128)S(1)} %bitcast.3), custom_call_target="tpu_custom_call" | custom-call | tf_op jit(solution)/shard_map/pallas_call | solution.py:168
  76.3 1.8 %collective-permute-done.12.refs_2_.refs_7_ = f32[1024,256]{1,0:T(8,128)S(1)} collective-permute-done((f32[1024,256]{1,0:T(8,128)S(1)}, f32[1024,256]{1,0:T(8,128)S(1)}, u32[]{:S(2)}, u32[]{:S(2)}) %collective-permute-start.12) | collective-permute-done | bytes 1048608 | tf_op jit(solution)/shard_map/far1/ppermute | solution.py:229
  78.0 1.7 %shard_map.52 = (f32[128,256]{1,0:T(8,128)S(1)}, f32[128,256]{1,0:T(8,128)S(1)}) custom-call(s32[2]{0:T(128)S(1)} %pad_add_fusion.place.refs_0_, f32[256,256]{1,0:T(8,128)S(1)} %shard_map.51.refs_1_, f32[1024,256]{1,0:T(8,128)S(1)} %collective-permute-done.12.refs_2_.refs_7_, f32[1024,256]{1,0:T(8,128)S(1)} %collective-permute-done.14.refs_3_.refs_8_, ...), custom_call_target="tpu_custom_call" | custom-call | tf_op jit(solution)/shard_map/pallas_call | solution.py:168
  79.7 3.9 %collective-permute-start.15 = (f32[128,256]{1,0:T(8,128)S(1)}, f32[128,256]{1,0:T(8,128)S(1)}, u32[]{:S(2)}, u32[]{:S(2)}) collective-permute-start(f32[128,256]{1,0:T(8,128)S(1)} %get-tuple-element.27), channel_id=1, source_target_pairs={{0,4},{4,0},{8,12},{12,8},{16,20},{20,16},{24,28},{28,24},{32,36},... | collective-permute-start | bytes 393224 | tf_op jit(solution)/shard_map/cross_halves/ppermute | solution.py:229
  84.6 3.8 %collective-permute-start.18 = (f32[128,256]{1,0:T(8,128)S(1)}, f32[128,256]{1,0:T(8,128)S(1)}, u32[]{:S(2)}, u32[]{:S(2)}) collective-permute-start(f32[128,256]{1,0:T(8,128)S(1)} %add.66), channel_id=1, source_target_pairs={{0,24},{4,100},{8,0},{12,108},{16,8},{20,116},{24,16},{28,124},{32... | collective-permute-start | bytes 393224 | tf_op jit(solution)/shard_map/cross_first/ppermute | solution.py:229
  88.4 1.3 %collective-permute-start.16 = (f32[128,256]{1,0:T(8,128)S(1)}, f32[128,256]{1,0:T(8,128)S(1)}, u32[]{:S(2)}, u32[]{:S(2)}) collective-permute-start(f32[128,256]{1,0:T(8,128)S(1)} %add.66), channel_id=1, source_target_pairs={{0,16},{4,68},{8,24},{12,76},{16,0},{20,84},{24,8},{28,92},{32,48}... | collective-permute-start | bytes 393224 | tf_op jit(solution)/shard_map/cross_first/ppermute | solution.py:229
  90.4 4.6 %collective-permute-done.17 = f32[128,256]{1,0:T(8,128)S(1)} collective-permute-done((f32[128,256]{1,0:T(8,128)S(1)}, f32[128,256]{1,0:T(8,128)S(1)}, u32[]{:S(2)}, u32[]{:S(2)}) %collective-permute-start.17) | collective-permute-done | bytes 131104 | tf_op jit(solution)/shard_map/cross_first/ppermute | solution.py:229
  95.0 2.4 %collective-permute-start.21 = (f32[128,256]{1,0:T(8,128)S(1)}, f32[128,256]{1,0:T(8,128)S(1)}, u32[]{:S(2)}, u32[]{:S(2)}) collective-permute-start(f32[128,256]{1,0:T(8,128)S(1)} %add_add_fusion.1), channel_id=1, source_target_pairs={{0,96},{4,28},{8,104},{12,4},{16,112},{20,12},{24,120},{28,20},{32... | collective-permute-start | bytes 393224 | tf_op jit(solution)/shard_map/cross_second/ppermute | solution.py:229
  97.5 1.7 %collective-permute-start.19 = (f32[128,256]{1,0:T(8,128)S(1)}, f32[128,256]{1,0:T(8,128)S(1)}, u32[]{:S(2)}, u32[]{:S(2)}) collective-permute-start(f32[128,256]{1,0:T(8,128)S(1)} %add_add_fusion.1), channel_id=1, source_target_pairs={{0,64},{4,20},{8,72},{12,28},{16,80},{20,4},{24,88},{28,12},{32,96... | collective-permute-start | bytes 393224 | tf_op jit(solution)/shard_map/cross_second/ppermute | solution.py:229
  99.4 4.8 %collective-permute-done.20 = f32[128,256]{1,0:T(8,128)S(1)} collective-permute-done((f32[128,256]{1,0:T(8,128)S(1)}, f32[128,256]{1,0:T(8,128)S(1)}, u32[]{:S(2)}, u32[]{:S(2)}) %collective-permute-start.20) | collective-permute-done | bytes 131104 | tf_op jit(solution)/shard_map/cross_second/ppermute | solution.py:229
  104.2 3.0 %collective-permute-start.22 = (f32[128,256]{1,0:T(8,128)S(1)}, f32[128,256]{1,0:T(8,128)S(1)}, u32[]{:S(2)}, u32[]{:S(2)}) collective-permute-start(f32[128,256]{1,0:T(8,128)S(1)} %add_add_fusion.refs_1_), channel_id=1, source_target_pairs={{0,4},{4,0},{8,12},{12,8},{16,20},{20,16},{24,28},{28,24},{32,36},... | collective-permute-start | bytes 393224 | tf_op jit(solution)/shard_map/cross_join/ppermute | solution.py:229
  107.2 1.0 collective-permute-done.22.refs_2_
  108.2 8.6 %shard_map.53 = (f32[8192,256]{1,0:T(8,128)}, f32[256,256]{1,0:T(8,128)}) custom-call(s32[2]{0:T(128)S(1)} %pad_add_fusion.place.refs_0_, f32[128,256]{1,0:T(8,128)S(1)} %add_add_fusion.refs_1_, f32[128,256]{1,0:T(8,128)S(1)} %collective-permute-done.22.refs_2_, f32[256,256]{1,0:T(8,128)S(1)} %get-tuple-element.28.refs_3_, f32[2048,256]{1,0:T(8,128)S(1)} %copy-done.1, ...), custom_call_target="tpu_custom_call" | custom-call | tf_op jit(solution)/shard_map/pallas_call | solution.py:126
  (38 shorter events, 5.0 us)
Async XLA Ops:
  0.6 48.2 %collective-permute-start.13 = (f32[2048,256]{1,0:T(8,128)}, f32[2048,256]{1,0:T(8,128)S(1)}, u32[]{:S(2)}, u32[]{:S(2)}) collective-permute-start(f32[2048,256]{1,0:T(8,128)} %refs_4_.5), channel_id=1, source_target_pairs={{0,3},{1,0},{2,1},{3,2},{4,7},{5,4},{6,5},{7,6},{8,11},{9,8},{10,9... | collective-permute-start | bytes 6291464 | tf_op jit(solution)/shard_map/right/ppermute | solution.py:229
  4.3 48.1 %collective-permute-start.11 = (f32[2048,256]{1,0:T(8,128)}, f32[2048,256]{1,0:T(8,128)}, u32[]{:S(2)}, u32[]{:S(2)}) collective-permute-start(f32[2048,256]{1,0:T(8,128)} %refs_4_.5), channel_id=1, source_target_pairs={{0,1},{1,2},{2,3},{3,0},{4,5},{5,6},{6,7},{7,4},{8,9},{9,10},{10,1... | collective-permute-start | bytes 6291464 | tf_op jit(solution)/shard_map/left/ppermute | solution.py:229
  4.3 1.6 %copy-start = (f32[2048,256]{1,0:T(8,128)S(1)}, f32[2048,256]{1,0:T(8,128)}, u32[]{:S(2)}) copy-start(f32[2048,256]{1,0:T(8,128)} %refs_4_.5) | copy-start | bytes 6291460
  9.0 2.0 %collective-permute-start = (f32[128,256]{1,0:T(8,128)S(1)}, f32[128,256]{1,0:T(8,128)S(1)}, u32[]{:S(2)}, u32[]{:S(2)}) collective-permute-start(f32[128,256]{1,0:T(8,128)S(1)} %get-tuple-element.18), channel_id=1, source_target_pairs={{0,4},{4,0},{8,12},{12,8},{16,20},{20,16},{24,28},{28,24},{32,36},... | collective-permute-start | bytes 393224 | tf_op jit(solution)/shard_map/gram_halves/ppermute | solution.py:229
  11.1 5.8 %collective-permute-start.3 = (f32[128,256]{1,0:T(8,128)S(1)}, f32[128,256]{1,0:T(8,128)S(1)}, u32[]{:S(2)}, u32[]{:S(2)}) collective-permute-start(f32[128,256]{1,0:T(8,128)S(1)} %add.56), channel_id=1, source_target_pairs={{0,24},{4,100},{8,0},{12,108},{16,8},{20,116},{24,16},{28,124},{32... | collective-permute-start | bytes 393224 | tf_op jit(solution)/shard_map/gram_first/ppermute | solution.py:229
  14.9 6.8 %collective-permute-start.2 = (f32[128,256]{1,0:T(8,128)S(1)}, f32[128,256]{1,0:T(8,128)S(1)}, u32[]{:S(2)}, u32[]{:S(2)}) collective-permute-start(f32[128,256]{1,0:T(8,128)S(1)} %add.56), channel_id=1, source_target_pairs={{0,8},{4,36},{8,16},{12,44},{16,24},{20,52},{24,0},{28,60},{32,40}... | collective-permute-start | bytes 393224 | tf_op jit(solution)/shard_map/gram_first/ppermute | solution.py:229
  14.9 6.8 %collective-permute-start.1 = (f32[128,256]{1,0:T(8,128)S(1)}, f32[128,256]{1,0:T(8,128)S(1)}, u32[]{:S(2)}, u32[]{:S(2)}) collective-permute-start(f32[128,256]{1,0:T(8,128)S(1)} %add.56), channel_id=1, source_target_pairs={{0,16},{4,68},{8,24},{12,76},{16,0},{20,84},{24,8},{28,92},{32,48}... | collective-permute-start | bytes 393224 | tf_op jit(solution)/shard_map/gram_first/ppermute | solution.py:229
  21.8 4.5 %collective-permute-start.6 = (f32[128,256]{1,0:T(8,128)S(1)}, f32[128,256]{1,0:T(8,128)S(1)}, u32[]{:S(2)}, u32[]{:S(2)}) collective-permute-start(f32[128,256]{1,0:T(8,128)S(1)} %add_add_fusion.4), channel_id=1, source_target_pairs={{0,96},{4,28},{8,104},{12,4},{16,112},{20,12},{24,120},{28,20},{32... | collective-permute-start | bytes 393224 | tf_op jit(solution)/shard_map/gram_second/ppermute | solution.py:229
  24.3 6.8 %collective-permute-start.5 = (f32[128,256]{1,0:T(8,128)S(1)}, f32[128,256]{1,0:T(8,128)S(1)}, u32[]{:S(2)}, u32[]{:S(2)}) collective-permute-start(f32[128,256]{1,0:T(8,128)S(1)} %add_add_fusion.4), channel_id=1, source_target_pairs={{0,32},{4,12},{8,40},{12,20},{16,48},{20,28},{24,56},{28,4},{32,64... | collective-permute-start | bytes 393224 | tf_op jit(solution)/shard_map/gram_second/ppermute | solution.py:229
  24.3 6.8 %collective-permute-start.4 = (f32[128,256]{1,0:T(8,128)S(1)}, f32[128,256]{1,0:T(8,128)S(1)}, u32[]{:S(2)}, u32[]{:S(2)}) collective-permute-start(f32[128,256]{1,0:T(8,128)S(1)} %add_add_fusion.4), channel_id=1, source_target_pairs={{0,64},{4,20},{8,72},{12,28},{16,80},{20,4},{24,88},{28,12},{32,96... | collective-permute-start | bytes 393224 | tf_op jit(solution)/shard_map/gram_second/ppermute | solution.py:229
  31.2 22.5 %collective-permute-start.9 = (f32[128,256]{1,0:T(8,128)S(1)}, f32[128,256]{1,0:T(8,128)S(1)}, u32[]{:S(2)}, u32[]{:S(2)}) collective-permute-start(f32[128,256]{1,0:T(8,128)S(1)} %add_add_fusion.3), channel_id=1, source_target_pairs={{0,3},{1,0},{2,1},{3,2},{4,7},{5,4},{6,5},{7,6},{8,11},{9,8},{10,9... | collective-permute-start | bytes 393224 | tf_op jit(solution)/shard_map/gram_cols/ppermute | solution.py:229
  34.0 21.8 %collective-permute-start.8 = (f32[128,256]{1,0:T(8,128)S(1)}, f32[128,256]{1,0:T(8,128)S(1)}, u32[]{:S(2)}, u32[]{:S(2)}) collective-permute-start(f32[128,256]{1,0:T(8,128)S(1)} %add_add_fusion.3), channel_id=1, source_target_pairs={{0,1},{1,2},{2,3},{3,0},{4,5},{5,6},{6,7},{7,4},{8,9},{9,10},{10,1... | collective-permute-start | bytes 393224 | tf_op jit(solution)/shard_map/gram_cols/ppermute | solution.py:229
  34.0 22.2 %collective-permute-start.7 = (f32[128,256]{1,0:T(8,128)S(1)}, f32[128,256]{1,0:T(8,128)S(1)}, u32[]{:S(2)}, u32[]{:S(2)}) collective-permute-start(f32[128,256]{1,0:T(8,128)S(1)} %add_add_fusion.3), channel_id=1, source_target_pairs={{0,2},{1,3},{2,0},{3,1},{4,6},{5,7},{6,4},{7,5},{8,10},{9,11},{10,... | collective-permute-start | bytes 393224 | tf_op jit(solution)/shard_map/gram_cols/ppermute | solution.py:229
  48.9 27.3 %collective-permute-start.14 = (f32[1024,256]{1,0:T(8,128)S(1)}, f32[1024,256]{1,0:T(8,128)S(1)}, u32[]{:S(2)}, u32[]{:S(2)}) collective-permute-start(f32[1024,256]{1,0:T(8,128)S(1)} %slice.7), channel_id=1, source_target_pairs={{0,3},{1,0},{2,1},{3,2},{4,7},{5,4},{6,5},{7,6},{8,11},{9,8},{10,9... | collective-permute-start | bytes 3145736 | tf_op jit(solution)/shard_map/far2/ppermute | solution.py:229
  53.6 24.4 %collective-permute-start.12 = (f32[1024,256]{1,0:T(8,128)S(1)}, f32[1024,256]{1,0:T(8,128)S(1)}, u32[]{:S(2)}, u32[]{:S(2)}) collective-permute-start(f32[1024,256]{1,0:T(8,128)S(1)} %slice.6), channel_id=1, source_target_pairs={{0,1},{1,2},{2,3},{3,0},{4,5},{5,6},{6,7},{7,4},{8,9},{9,10},{10,1... | collective-permute-start | bytes 3145736 | tf_op jit(solution)/shard_map/far1/ppermute | solution.py:229
  56.2 15.0 %slice-start = ((s8[8388608]{0:T(1024)(128)(4,1)}), s8[4194304]{0:T(1024)(128)(4,1)S(1)}, s32[]{:S(2)}) async-start(s8[8388608]{0:T(1024)(128)(4,1)} %bitcast.2), calls=%async_computation | async-start | bytes 8388608
  56.2 14.9 %slice-start.1 = ((s8[8388608]{0:T(1024)(128)(4,1)}), s8[4194304]{0:T(1024)(128)(4,1)S(1)}, s32[]{:S(2)}) async-start(s8[8388608]{0:T(1024)(128)(4,1)} %bitcast.2), calls=%async_computation.1 | async-start | bytes 8388608
  56.2 4.7 %collective-permute-start.10 = (f32[128,256]{1,0:T(8,128)S(1)}, f32[128,256]{1,0:T(8,128)S(1)}, u32[]{:S(2)}, u32[]{:S(2)}) collective-permute-start(f32[128,256]{1,0:T(8,128)S(1)} %add_add_fusion.2.refs_1_), channel_id=1, source_target_pairs={{0,4},{4,0},{8,12},{12,8},{16,20},{20,16},{24,28},{28,24},{32,36},... | collective-permute-start | bytes 393224 | tf_op jit(solution)/shard_map/gram_join/ppermute | solution.py:229
  78.0 30.2 %copy-start.1 = (f32[2048,256]{1,0:T(8,128)S(1)}, f32[2048,256]{1,0:T(8,128)}, u32[]{:S(2)}) copy-start(f32[2048,256]{1,0:T(8,128)} %refs_4_.5) | copy-start | bytes 6291460
  79.7 4.9 %collective-permute-start.15 = (f32[128,256]{1,0:T(8,128)S(1)}, f32[128,256]{1,0:T(8,128)S(1)}, u32[]{:S(2)}, u32[]{:S(2)}) collective-permute-start(f32[128,256]{1,0:T(8,128)S(1)} %get-tuple-element.27), channel_id=1, source_target_pairs={{0,4},{4,0},{8,12},{12,8},{16,20},{20,16},{24,28},{28,24},{32,36},... | collective-permute-start | bytes 393224 | tf_op jit(solution)/shard_map/cross_halves/ppermute | solution.py:229
  84.6 5.8 %collective-permute-start.18 = (f32[128,256]{1,0:T(8,128)S(1)}, f32[128,256]{1,0:T(8,128)S(1)}, u32[]{:S(2)}, u32[]{:S(2)}) collective-permute-start(f32[128,256]{1,0:T(8,128)S(1)} %add.66), channel_id=1, source_target_pairs={{0,24},{4,100},{8,0},{12,108},{16,8},{20,116},{24,16},{28,124},{32... | collective-permute-start | bytes 393224 | tf_op jit(solution)/shard_map/cross_first/ppermute | solution.py:229
  88.4 6.5 %collective-permute-start.17 = (f32[128,256]{1,0:T(8,128)S(1)}, f32[128,256]{1,0:T(8,128)S(1)}, u32[]{:S(2)}, u32[]{:S(2)}) collective-permute-start(f32[128,256]{1,0:T(8,128)S(1)} %add.66), channel_id=1, source_target_pairs={{0,8},{4,36},{8,16},{12,44},{16,24},{20,52},{24,0},{28,60},{32,40}... | collective-permute-start | bytes 393224 | tf_op jit(solution)/shard_map/cross_first/ppermute | solution.py:229
  88.4 6.5 %collective-permute-start.16 = (f32[128,256]{1,0:T(8,128)S(1)}, f32[128,256]{1,0:T(8,128)S(1)}, u32[]{:S(2)}, u32[]{:S(2)}) collective-permute-start(f32[128,256]{1,0:T(8,128)S(1)} %add.66), channel_id=1, source_target_pairs={{0,16},{4,68},{8,24},{12,76},{16,0},{20,84},{24,8},{28,92},{32,48}... | collective-permute-start | bytes 393224 | tf_op jit(solution)/shard_map/cross_first/ppermute | solution.py:229
  95.0 4.4 %collective-permute-start.21 = (f32[128,256]{1,0:T(8,128)S(1)}, f32[128,256]{1,0:T(8,128)S(1)}, u32[]{:S(2)}, u32[]{:S(2)}) collective-permute-start(f32[128,256]{1,0:T(8,128)S(1)} %add_add_fusion.1), channel_id=1, source_target_pairs={{0,96},{4,28},{8,104},{12,4},{16,112},{20,12},{24,120},{28,20},{32... | collective-permute-start | bytes 393224 | tf_op jit(solution)/shard_map/cross_second/ppermute | solution.py:229
  97.5 6.7 %collective-permute-start.20 = (f32[128,256]{1,0:T(8,128)S(1)}, f32[128,256]{1,0:T(8,128)S(1)}, u32[]{:S(2)}, u32[]{:S(2)}) collective-permute-start(f32[128,256]{1,0:T(8,128)S(1)} %add_add_fusion.1), channel_id=1, source_target_pairs={{0,32},{4,12},{8,40},{12,20},{16,48},{20,28},{24,56},{28,4},{32,64... | collective-permute-start | bytes 393224 | tf_op jit(solution)/shard_map/cross_second/ppermute | solution.py:229
  97.5 6.7 %collective-permute-start.19 = (f32[128,256]{1,0:T(8,128)S(1)}, f32[128,256]{1,0:T(8,128)S(1)}, u32[]{:S(2)}, u32[]{:S(2)}) collective-permute-start(f32[128,256]{1,0:T(8,128)S(1)} %add_add_fusion.1), channel_id=1, source_target_pairs={{0,64},{4,20},{8,72},{12,28},{16,80},{20,4},{24,88},{28,12},{32,96... | collective-permute-start | bytes 393224 | tf_op jit(solution)/shard_map/cross_second/ppermute | solution.py:229
  104.2 4.0 %collective-permute-start.22 = (f32[128,256]{1,0:T(8,128)S(1)}, f32[128,256]{1,0:T(8,128)S(1)}, u32[]{:S(2)}, u32[]{:S(2)}) collective-permute-start(f32[128,256]{1,0:T(8,128)S(1)} %add_add_fusion.refs_1_), channel_id=1, source_target_pairs={{0,4},{4,0},{8,12},{12,8},{16,20},{20,16},{24,28},{28,24},{32,36},... | collective-permute-start | bytes 393224 | tf_op jit(solution)/shard_map/cross_join/ppermute | solution.py:229

commit v3 on v2

--- a/solution.py
+++ b/solution.py
@@ -10,8 +10,8 @@
 F32, BF16 = jnp.float32, jnp.bfloat16
 HIGHEST = lax.Precision.HIGHEST
 BLOCK = 512
-UPDATE_VMEM = 28 << 20
-CROSS_VMEM = 16 << 20
+UPDATE_VMEM = 14 << 20
+CROSS_VMEM = 8 << 20
 
 def split(value):
     high = value.astype(BF16)
@@ -48,15 +48,15 @@
     wide = wide * lax.rsqrt(diagonal)
     return wide
 
-def factor_kernel(shrink, size, group, core, mine, other, r_factor, inverse, work):
-    @pl.when(core[0] == 0)
-    def _():
-        work[:128, :256] = mine[...]
-        work[128:, :256] = other[...]
-    @pl.when(core[0] != 0)
-    def _():
-        work[:128, :256] = other[...]
-        work[128:, :256] = mine[...]
+def factor_kernel(shrink, size, group, mine, other, r_factor, inverse, work):
+    _, first = whereabouts()
+    one = jnp.where(first, mine[...], other[...])
+    two = jnp.where(first, other[...], mine[...])
+    work[:128, :128] = one[:128, :]
+    work[:64, 128:256] = one[128:, :]
+    work[64:128, 128:256] = two[128:, :]
+    work[128:, :128] = jnp.zeros((128, 128), F32)
+    work[128:, 128:256] = two[:128, :]
     rows = lax.broadcasted_iota(jnp.int32, (256, 256), 0)
     lanes = lax.broadcasted_iota(jnp.int32, (256, 256), 1)
     work[:, 256:] = (rows == lanes).astype(F32)
@@ -70,17 +70,21 @@
     r_factor[...] = jnp.where(rows <= lanes, work[:, :256], 0.0) * shrink
     inverse[...] = jnp.where(rows >= lanes, work[:, 256:], 0.0)
 
-def factor(core, mine, other, shrink, size=64, group=4):
+def factor(mine, other, shrink, size=64, group=4):
     full = jax.ShapeDtypeStruct((256, 256), F32)
     return pl.pallas_call(
         lambda *refs: factor_kernel(shrink, size, group, *refs),
         out_shape=[full, full],
-        in_specs=[pl.BlockSpec(memory_space=pltpu.SMEM), pl.BlockSpec(memory_space=pltpu.VMEM), pl.BlockSpec(memory_space=pltpu.VMEM)],
+        in_specs=[pl.BlockSpec(memory_space=pltpu.VMEM)] * 2,
         out_specs=[pl.BlockSpec(memory_space=pltpu.VMEM)] * 2,
         scratch_shapes=[pltpu.VMEM((256, 512), F32)],
         cost_estimate=pl.CostEstimate(flops=8000000000, bytes_accessed=0, transcendentals=0),
         compiler_params=pltpu.CompilerParams(vmem_limit_bytes=16 << 20),
-    )(core, mine, other)
+    )(mine, other)
+
+def whereabouts():
+    return lax.axis_index("cols"), lax.rem(lax.axis_index("rows"), 2) == 0
+
 
 def blocks_of(pieces, block):
     return [
@@ -94,9 +98,9 @@
     return pl.ds(pl.multiple_of(lax.rem(column + offset, 4) * chunk + low, block), block)
 
 
-def update_kernel(shrink, blocks, block, chunk, place, mine, other, inverse, *refs):
+def update_kernel(shrink, blocks, block, chunk, mine, other, inverse, *refs):
     *pieces, trailing, updated, r_cross, result, weights, sems = refs
-    first = place[1] == 0
+    column, first = whereabouts()
     top = jnp.where(first, mine[...], other[...])
     bottom = jnp.where(first, other[...], mine[...])
     coupling = contract(inverse[...], jnp.concatenate([top, bottom], axis=0), ((1,), (0,)), HIGHEST)
@@ -107,7 +111,7 @@
     weights[512:, :] = low
     stores = []
     for n, (piece, row, offset, low_row) in enumerate(blocks):
-        rows = rows_at(place[0], offset, low_row, chunk, block)
+        rows = rows_at(column, offset, low_row, chunk, block)
         high, low = split(pieces[piece][row : row + block, :])
         product = contract(jnp.concatenate([high, low, high], axis=1), weights[...], ((1,), (0,)))
         here = pl.ds(n * block, block)
@@ -119,14 +123,14 @@
         store.wait()
 
 
-def update(mine, other, inverse, pieces, spots, trailing, place, shrink, block):
+def update(mine, other, inverse, pieces, spots, trailing, shrink, block):
     blocks = blocks_of(spots, block)
     vmem, anywhere = pl.BlockSpec(memory_space=pltpu.VMEM), pl.BlockSpec(memory_space=pl.ANY)
     total = trailing.shape[0]
     return pl.pallas_call(
         lambda *refs: update_kernel(shrink, blocks, block, total // 4, *refs),
         out_shape=[jax.ShapeDtypeStruct(trailing.shape, F32), jax.ShapeDtypeStruct((256, 256), F32)],
-        in_specs=[pl.BlockSpec(memory_space=pltpu.SMEM), *[vmem] * (len(pieces) + 4)],
+        in_specs=[vmem] * (len(pieces) + 4),
         out_specs=[anywhere, vmem],
         scratch_shapes=[
             pltpu.VMEM((total, 256), F32),
@@ -134,18 +138,19 @@
             pltpu.SemaphoreType.DMA((len(blocks),)),
         ],
         compiler_params=pltpu.CompilerParams(vmem_limit_bytes=UPDATE_VMEM),
-    )(place, mine, other, inverse, *pieces, trailing)
-
-
-def cross_kernel(initial, halves, blocks, block, chunk, place, *refs):
+    )(mine, other, inverse, *pieces, trailing)
+
+
+def cross_kernel(initial, halves, blocks, block, chunk, *refs):
     refs = list(refs)
+    column, first = whereabouts()
     total = refs.pop(0)[...] if initial else None
     count = 2 if halves else 1
     *pieces, trailing = refs[:-count]
     outs = refs[-count:]
     for piece, row, offset, low in blocks:
         left = split(pieces[piece][row : row + block, :])
-        right = split(trailing[rows_at(place[0], offset, low, chunk, block), :])
+        right = split(trailing[rows_at(column, offset, low, chunk, block), :])
         product = contract(
             jnp.concatenate([left[0], left[1], left[0]], axis=0),
             jnp.concatenate([right[0], right[0], right[1]], axis=0),
@@ -153,14 +158,13 @@
         )
         total = product if total is None else total + product
     if halves:
-        first = place[1] == 0
         outs[0][...] = jnp.where(first, total[:128, :], total[128:, :])
         outs[1][...] = jnp.where(first, total[128:, :], total[:128, :])
     else:
         outs[0][...] = total
 
 
-def cross_part(place, initial, pieces, spots, trailing, halves, block):
+def cross_part(initial, pieces, spots, trailing, halves, block):
     blocks = blocks_of(spots, block)
     vmem = pl.BlockSpec(memory_space=pltpu.VMEM)
     given = [] if initial is None else [initial]
@@ -168,38 +172,30 @@
     return pl.pallas_call(
         lambda *refs: cross_kernel(bool(given), halves, blocks, block, trailing.shape[0] // 4, *refs),
         out_shape=[jax.ShapeDtypeStruct(shape, F32) for shape in shapes],
-        in_specs=[pl.BlockSpec(memory_space=pltpu.SMEM), *[vmem] * (len(given) + len(pieces) + 1)],
+        in_specs=[vmem] * (len(given) + len(pieces) + 1),
         out_specs=[vmem] * len(shapes),
         compiler_params=pltpu.CompilerParams(vmem_limit_bytes=CROSS_VMEM),
-    )(place, *given, *pieces, trailing)
-
-
-def gram_kernel(place, panel, keep, send):
-    @pl.when(pl.program_id(0) == 0)
-    def _():
-        keep[...] = jnp.zeros_like(keep)
-        send[...] = jnp.zeros_like(send)
-    part = contract(panel[...], panel[...], ((0,), (0,)), HIGHEST)
-    @pl.when(place[1] == 0)
-    def _():
-        keep[...] += part[:128, :]
-        send[...] += part[128:, :]
-    @pl.when(place[1] != 0)
-    def _():
-        keep[...] += part[128:, :]
-        send[...] += part[:128, :]
-
-def gram_part(place, panel, block=1024):
-    half = pl.BlockSpec((128, 256), lambda i, place: (0, 0))
+    )(*given, *pieces, trailing)
+
+
+def gram_kernel(panel, keep, send):
+    gram = contract(panel[...], panel[...], ((0,), (0,)), HIGHEST)
+    one = jnp.concatenate([gram[:128, :128], gram[:64, 128:]], axis=0)
+    two = jnp.concatenate([gram[128:, 128:], gram[64:128, 128:]], axis=0)
+    _, first = whereabouts()
+    keep[...] = jnp.where(first, one, two)
+    send[...] = jnp.where(first, two, one)
+
+
+def gram_part(panel):
+    vmem = pl.BlockSpec(memory_space=pltpu.VMEM)
     return pl.pallas_call(
         gram_kernel,
-        out_shape=[jax.ShapeDtypeStruct((128, 256), F32)] * 2,
-        grid_spec=pltpu.PrefetchScalarGridSpec(
-            num_scalar_prefetch=1, grid=(panel.shape[0] // block,),
-            in_specs=[pl.BlockSpec((block, 256), lambda i, place: (i, 0))],
-            out_specs=[half, half]),
-        compiler_params=pltpu.CompilerParams(vmem_limit_bytes=32 << 20),
-    )(place, panel)
+        out_shape=[jax.ShapeDtypeStruct((192, 128), F32)] * 2,
+        in_specs=[vmem],
+        out_specs=[vmem, vmem],
+        compiler_params=pltpu.CompilerParams(vmem_limit_bytes=16 << 20),
+    )(panel)
 
 
 def over_rows(move):
@@ -231,7 +227,7 @@
 
 def exchange_sum(name, part, axis, moves):
     others = [move(name, part, axis, pairs) for pairs in moves]
-    return (part + others[2]) + (others[0] + others[1])
+    return (others[0] + others[1]) + (part + others[2])
 
 
 def partner(name, part):
@@ -241,15 +237,13 @@
 def local(panel_cols, trailing):
     rows_total = trailing.shape[0] * lax.axis_size("rows")
     shrink = 1.0 / math.sqrt(rows_total)
-    core = lax.axis_index("rows") % 2
-    place = jnp.stack([lax.axis_index("cols"), core]).astype(jnp.int32)
     size = panel_cols.shape[0]
     half = size // 2
     barrier = lax.optimization_barrier
     left = move("left", panel_cols, "cols", around(1))
     right = move("right", panel_cols, "cols", around(-1))
 
-    keep, send = gram_part(place, panel_cols)
+    keep, send = gram_part(panel_cols)
     gram = keep + partner("gram_halves", send)
     gram = exchange_sum("gram_first", gram, "rows", FIRST)
     gram = exchange_sum("gram_second", gram, "rows", SECOND)
@@ -258,17 +252,18 @@
     far1 = move("far1", left[:half], "cols", around(1))
     far2 = move("far2", right[half:], "cols", around(-1))
     gram = exchange_sum("gram_cols", gram, "cols", [around(k) for k in ORDER])
-    r_factor, inverse = factor(place[1:], gram, partner("gram_join", gram), shrink, 64, 8)
-
-    (cross,) = cross_part(place, None, (panel_cols, left, right), ((size, 0, 0), (size, 3, 0), (size, 1, 0)), trailing, False, BLOCK)
-    inverse, far1, far2, cross = barrier((inverse, far1, far2, cross))
-    keep, send = cross_part(place, cross, (far1, far2), ((half, 2, 0), (half, 2, half)), trailing, True, BLOCK)
+    r_factor, inverse = factor(gram, partner("gram_join", gram), shrink, 64, 8)
+
+    (cross,) = cross_part(None, (panel_cols, left, right), ((size, 0, 0), (size, 3, 0), (size, 1, 0)), trailing, False, BLOCK)
+    (cross,) = cross_part(cross, (far2,), ((half, 2, half),), trailing, False, BLOCK)
+    inverse, far1, cross = barrier((inverse, far1, cross))
+    keep, send = cross_part(cross, (far1,), ((half, 2, 0),), trailing, True, BLOCK)
     cross = keep + partner("cross_halves", send)
     cross = exchange_sum("cross_first", cross, "rows", FIRST)
     cross = exchange_sum("cross_second", cross, "rows", SECOND)
     pieces = (panel_cols, left, right, far1, far2)
     spots = ((size, 0, 0), (size, 3, 0), (size, 1, 0), (half, 2, 0), (half, 2, half))
-    updated, r_cross = update(cross, partner("cross_join", cross), inverse, pieces, spots, trailing, place, shrink, BLOCK)
+    updated, r_cross = update(cross, partner("cross_join", cross), inverse, pieces, spots, trailing, shrink, BLOCK)
     return (r_factor, r_cross, updated)
 
 

time: 117 us -> 112 us (0.957)
  Pallas kernels: 28.2 us -> 22.8 us
  waiting for transfers between devices: 43.2 us -> 45.1 us
  local copies, waits for them, and re-layouts: 3 us -> 1.81 us
    pallas_call x2 -> x3, Pallas kernels: 6.33 us -> 3.9 us  [cross_part(): pl.pallas_call(lambda *refs: cross_kernel(bool(given), halves, blocks, bl...]
    ppermute x23, waiting for transfers between devices: 43.2 us -> 45.1 us  [move(): return lax.ppermute(part, axis, pairs)]
    pallas_call x1, Pallas kernels: 8.58 us -> 6.73 us  [update(): pl.pallas_call(lambda *refs: update_kernel(shrink, blocks, block, total /...]
    slice x1, local copies, waits for them, and re-layouts: 1.29 us -> 0.07 us  [local(): far1 = move('far1', left[:half], 'cols', around(1))]
  transfers between devices with their start and end apart: 23 -> 23, of which waited for: 17 -> 20; matrix products, arithmetic and copies ran while one was open for 1% -> 0% of each run, Pallas kernels for 15% -> 14%
where the time goes in v3:
time: 112 us
  waiting for transfers between devices  45.1 us (40%)
  starting transfers between devices  41.2 us (37%)
  Pallas kernels  22.8 us (20%)
  local copies, waits for them, and re-layouts  1.81 us (2%)
    ppermute x23, waiting for transfers between devices, move(): return lax.ppermute(part, axis, pairs)  45.1 us
    ppermute x23, starting transfers between devices, move(): return lax.ppermute(part, axis, pairs)  41.2 us
    pallas_call x1, Pallas kernels, factor(): pl.pallas_call(lambda *refs: factor_kernel(shrink, size, group, *refs), o...  10 us
    pallas_call x1, Pallas kernels, update(): pl.pallas_call(lambda *refs: update_kernel(shrink, blocks, block, total /...  6.73 us
    pallas_call x3, Pallas kernels, cross_part(): pl.pallas_call(lambda *refs: cross_kernel(bool(given), halves, blocks, bl...  3.9 us
  transfers between devices with their start and end apart: 23, of which 20 were waited for; matrix products, arithmetic and copies ran while one was open for 0% of the time, Pallas kernels for 14%

profile of v3, /device:TPU:1, one launch (start us, length us, event | category | flops | bytes accessed | tf_op | source)
XLA Modules:
  0.0 112.0 jit_solution(7413220531861960987)
XLA Ops:
  0.6 3.6 %collective-permute-start.13 = (f32[2048,256]{1,0:T(8,128)}, f32[2048,256]{1,0:T(8,128)S(1)}, u32[]{:S(2)}, u32[]{:S(2)}) collective-permute-start(f32[2048,256]{1,0:T(8,128)} %refs_3_.3), channel_id=1, source_target_pairs={{0,3},{1,0},{2,1},{3,2},{4,7},{5,4},{6,5},{7,6},{8,11},{9,8},{10,9... | collective-permute-start | bytes 6291464 | tf_op jit(solution)/shard_map/right/ppermute | solution.py:225
  4.3 1.7 %copy-done = f32[2048,256]{1,0:T(8,128)S(1)} copy-done((f32[2048,256]{1,0:T(8,128)S(1)}, f32[2048,256]{1,0:T(8,128)}, u32[]{:S(2)}) %copy-start) | copy-done | bytes 2097176
  5.9 2.1 %shard_map.49 = (f32[192,128]{1,0:T(8,128)S(1)}, f32[192,128]{1,0:T(8,128)S(1)}) custom-call(f32[2048,256]{1,0:T(8,128)S(1)} %copy-done), custom_call_target="tpu_custom_call" | custom-call | tf_op jit(solution)/shard_map/pallas_call | solution.py:192
  8.0 1.0 collective-permute-start
  10.0 3.7 %collective-permute-start.3 = (f32[192,128]{1,0:T(8,128)S(1)}, f32[192,128]{1,0:T(8,128)S(1)}, u32[]{:S(2)}, u32[]{:S(2)}) collective-permute-start(f32[192,128]{1,0:T(8,128)S(1)} %add.51), channel_id=1, source_target_pairs={{0,16},{4,68},{8,24},{12,76},{16,0},{20,84},{24,8},{28,92},{32,48}... | collective-permute-start | bytes 294920 | tf_op jit(solution)/shard_map/gram_first/ppermute | solution.py:225
  14.1 1.0 collective-permute-start.1
  16.0 1.8 %collective-permute-done.2 = f32[192,128]{1,0:T(8,128)S(1)} collective-permute-done((f32[192,128]{1,0:T(8,128)S(1)}, f32[192,128]{1,0:T(8,128)S(1)}, u32[]{:S(2)}, u32[]{:S(2)}) %collective-permute-start.2) | collective-permute-done | bytes 98336 | tf_op jit(solution)/shard_map/gram_first/ppermute | solution.py:225
  17.8 1.3 %collective-permute-done.1 = f32[192,128]{1,0:T(8,128)S(1)} collective-permute-done((f32[192,128]{1,0:T(8,128)S(1)}, f32[192,128]{1,0:T(8,128)S(1)}, u32[]{:S(2)}, u32[]{:S(2)}) %collective-permute-start.1) | collective-permute-done | bytes 98336 | tf_op jit(solution)/shard_map/gram_first/ppermute | solution.py:225
  19.1 2.8 %collective-permute-start.6 = (f32[192,128]{1,0:T(8,128)S(1)}, f32[192,128]{1,0:T(8,128)S(1)}, u32[]{:S(2)}, u32[]{:S(2)}) collective-permute-start(f32[192,128]{1,0:T(8,128)S(1)} %add_add_fusion.4), channel_id=1, source_target_pairs={{0,64},{4,20},{8,72},{12,28},{16,80},{20,4},{24,88},{28,12},{32,96... | collective-permute-start | bytes 294920 | tf_op jit(solution)/shard_map/gram_second/ppermute | solution.py:225
  24.2 1.5 %collective-permute-done.5 = f32[192,128]{1,0:T(8,128)S(1)} collective-permute-done((f32[192,128]{1,0:T(8,128)S(1)}, f32[192,128]{1,0:T(8,128)S(1)}, u32[]{:S(2)}, u32[]{:S(2)}) %collective-permute-start.5) | collective-permute-done | bytes 98336 | tf_op jit(solution)/shard_map/gram_second/ppermute | solution.py:225
  25.7 2.1 %collective-permute-done.4 = f32[192,128]{1,0:T(8,128)S(1)} collective-permute-done((f32[192,128]{1,0:T(8,128)S(1)}, f32[192,128]{1,0:T(8,128)S(1)}, u32[]{:S(2)}, u32[]{:S(2)}) %collective-permute-start.4) | collective-permute-done | bytes 98336 | tf_op jit(solution)/shard_map/gram_second/ppermute | solution.py:225
  27.8 1.4 %collective-permute-start.9 = (f32[192,128]{1,0:T(8,128)S(1)}, f32[192,128]{1,0:T(8,128)S(1)}, u32[]{:S(2)}, u32[]{:S(2)}) collective-permute-start(f32[192,128]{1,0:T(8,128)S(1)} %add_add_fusion.3), channel_id=1, source_target_pairs={{0,2},{1,3},{2,0},{3,1},{4,6},{5,7},{6,4},{7,5},{8,10},{9,11},{10,... | collective-permute-start | bytes 294920 | tf_op jit(solution)/shard_map/gram_cols/ppermute | solution.py:225
  29.2 1.7 %collective-permute-start.8 = (f32[192,128]{1,0:T(8,128)S(1)}, f32[192,128]{1,0:T(8,128)S(1)}, u32[]{:S(2)}, u32[]{:S(2)}) collective-permute-start(f32[192,128]{1,0:T(8,128)S(1)} %add_add_fusion.3), channel_id=1, source_target_pairs={{0,3},{1,0},{2,1},{3,2},{4,7},{5,4},{6,5},{7,6},{8,11},{9,8},{10,9... | collective-permute-start | bytes 294920 | tf_op jit(solution)/shard_map/gram_cols/ppermute | solution.py:225
  31.4 18.4 %collective-permute-done.13.refs_2_.refs_5_ = f32[2048,256]{1,0:T(8,128)S(1)} collective-permute-done((f32[2048,256]{1,0:T(8,128)}, f32[2048,256]{1,0:T(8,128)S(1)}, u32[]{:S(2)}, u32[]{:S(2)}) %collective-permute-start.13) | collective-permute-done | bytes 2097184 | tf_op jit(solution)/shard_map/right/ppermute | solution.py:225
  49.9 3.9 %collective-permute-start.14 = (f32[1024,256]{1,0:T(8,128)S(1)}, f32[1024,256]{1,0:T(8,128)S(1)}, u32[]{:S(2)}, u32[]{:S(2)}) collective-permute-start(f32[1024,256]{1,0:T(8,128)S(1)} %slice.7), channel_id=1, source_target_pairs={{0,3},{1,0},{2,1},{3,2},{4,7},{5,4},{6,5},{7,6},{8,11},{9,8},{10,9... | collective-permute-start | bytes 3145736 | tf_op jit(solution)/shard_map/far2/ppermute | solution.py:225
  53.9 2.2 %collective-permute-done.7 = f32[192,128]{1,0:T(8,128)S(1)} collective-permute-done((f32[192,128]{1,0:T(8,128)S(1)}, f32[192,128]{1,0:T(8,128)S(1)}, u32[]{:S(2)}, u32[]{:S(2)}) %collective-permute-start.7) | collective-permute-done | bytes 98336 | tf_op jit(solution)/shard_map/gram_cols/ppermute | solution.py:225
  56.1 2.1 %collective-permute-start.10 = (f32[192,128]{1,0:T(8,128)S(1)}, f32[192,128]{1,0:T(8,128)S(1)}, u32[]{:S(2)}, u32[]{:S(2)}) collective-permute-start(f32[192,128]{1,0:T(8,128)S(1)} %add_add_fusion.2.refs_0_), channel_id=1, source_target_pairs={{0,4},{4,0},{8,12},{12,8},{16,20},{20,16},{24,28},{28,24},{32,36},... | collective-permute-start | bytes 294920 | tf_op jit(solution)/shard_map/gram_join/ppermute | solution.py:225
  59.2 10.0 %shard_map.50 = (f32[256,256]{1,0:T(8,128)}, f32[256,256]{1,0:T(8,128)S(1)}) custom-call(f32[192,128]{1,0:T(8,128)S(1)} %add_add_fusion.2.refs_0_, f32[192,128]{1,0:T(8,128)S(1)} %collective-permute-done.10.refs_1_), custom_call_target="tpu_custom_call" | custom-call | flops 8000000000 | tf_op jit(solution)/shard_map/pallas_call | solution.py:75
  69.2 2.7 %shard_map.51.refs_0_ = f32[256,256]{1,0:T(8,128)S(1)} custom-call(f32[2048,256]{1,0:T(8,128)S(1)} %copy-done.1, f32[2048,256]{1,0:T(8,128)S(1)} %collective-permute-done.11.refs_1_.refs_4_, f32[2048,256]{1,0:T(8,128)S(1)} %collective-permute-done.13.refs_2_.refs_5_, f32[8192,256]{1,0:T(8,128)S(1)} %bitcast.1), custom_call_target="tpu_custom_call" | custom-call | tf_op jit(solution)/shard_map/pallas_call | solution.py:172
  73.5 2.7 %collective-permute-done.12.refs_1_.refs_6_ = f32[1024,256]{1,0:T(8,128)S(1)} collective-permute-done((f32[1024,256]{1,0:T(8,128)S(1)}, f32[1024,256]{1,0:T(8,128)S(1)}, u32[]{:S(2)}, u32[]{:S(2)}) %collective-permute-start.12) | collective-permute-done | bytes 1048608 | tf_op jit(solution)/shard_map/far1/ppermute | solution.py:225
  76.8 4.6 %collective-permute-start.15 = (f32[128,256]{1,0:T(8,128)S(1)}, f32[128,256]{1,0:T(8,128)S(1)}, u32[]{:S(2)}, u32[]{:S(2)}) collective-permute-start(f32[128,256]{1,0:T(8,128)S(1)} %get-tuple-element.25), channel_id=1, source_target_pairs={{0,4},{4,0},{8,12},{12,8},{16,20},{20,16},{24,28},{28,24},{32,36},... | collective-permute-start | bytes 393224 | tf_op jit(solution)/shard_map/cross_halves/ppermute | solution.py:225
  82.4 3.6 %collective-permute-start.18 = (f32[128,256]{1,0:T(8,128)S(1)}, f32[128,256]{1,0:T(8,128)S(1)}, u32[]{:S(2)}, u32[]{:S(2)}) collective-permute-start(f32[128,256]{1,0:T(8,128)S(1)} %add.61), channel_id=1, source_target_pairs={{0,16},{4,68},{8,24},{12,76},{16,0},{20,84},{24,8},{28,92},{32,48}... | collective-permute-start | bytes 393224 | tf_op jit(solution)/shard_map/cross_first/ppermute | solution.py:225
  86.4 1.0 collective-permute-start.16
  87.5 1.2 %collective-permute-done.18 = f32[128,256]{1,0:T(8,128)S(1)} collective-permute-done((f32[128,256]{1,0:T(8,128)S(1)}, f32[128,256]{1,0:T(8,128)S(1)}, u32[]{:S(2)}, u32[]{:S(2)}) %collective-permute-start.18) | collective-permute-done | bytes 131104 | tf_op jit(solution)/shard_map/cross_first/ppermute | solution.py:225
  88.6 1.9 %collective-permute-done.17 = f32[128,256]{1,0:T(8,128)S(1)} collective-permute-done((f32[128,256]{1,0:T(8,128)S(1)}, f32[128,256]{1,0:T(8,128)S(1)}, u32[]{:S(2)}, u32[]{:S(2)}) %collective-permute-start.17) | collective-permute-done | bytes 131104 | tf_op jit(solution)/shard_map/cross_first/ppermute | solution.py:225
  90.5 1.2 %collective-permute-done.16 = f32[128,256]{1,0:T(8,128)S(1)} collective-permute-done((f32[128,256]{1,0:T(8,128)S(1)}, f32[128,256]{1,0:T(8,128)S(1)}, u32[]{:S(2)}, u32[]{:S(2)}) %collective-permute-start.16) | collective-permute-done | bytes 131104 | tf_op jit(solution)/shard_map/cross_first/ppermute | solution.py:225
  91.8 2.5 %collective-permute-start.21 = (f32[128,256]{1,0:T(8,128)S(1)}, f32[128,256]{1,0:T(8,128)S(1)}, u32[]{:S(2)}, u32[]{:S(2)}) collective-permute-start(f32[128,256]{1,0:T(8,128)S(1)} %add_add_fusion.1), channel_id=1, source_target_pairs={{0,64},{4,20},{8,72},{12,28},{16,80},{20,4},{24,88},{28,12},{32,96... | collective-permute-start | bytes 393224 | tf_op jit(solution)/shard_map/cross_second/ppermute | solution.py:225
  95.8 1.4 %collective-permute-done.21 = f32[128,256]{1,0:T(8,128)S(1)} collective-permute-done((f32[128,256]{1,0:T(8,128)S(1)}, f32[128,256]{1,0:T(8,128)S(1)}, u32[]{:S(2)}, u32[]{:S(2)}) %collective-permute-start.21) | collective-permute-done | bytes 131104 | tf_op jit(solution)/shard_map/cross_second/ppermute | solution.py:225
  97.2 1.5 %collective-permute-done.20 = f32[128,256]{1,0:T(8,128)S(1)} collective-permute-done((f32[128,256]{1,0:T(8,128)S(1)}, f32[128,256]{1,0:T(8,128)S(1)}, u32[]{:S(2)}, u32[]{:S(2)}) %collective-permute-start.20) | collective-permute-done | bytes 131104 | tf_op jit(solution)/shard_map/cross_second/ppermute | solution.py:225
  98.7 1.5 %collective-permute-done.19 = f32[128,256]{1,0:T(8,128)S(1)} collective-permute-done((f32[128,256]{1,0:T(8,128)S(1)}, f32[128,256]{1,0:T(8,128)S(1)}, u32[]{:S(2)}, u32[]{:S(2)}) %collective-permute-start.19) | collective-permute-done | bytes 131104 | tf_op jit(solution)/shard_map/cross_second/ppermute | solution.py:225
  100.2 3.9 %collective-permute-start.22 = (f32[128,256]{1,0:T(8,128)S(1)}, f32[128,256]{1,0:T(8,128)S(1)}, u32[]{:S(2)}, u32[]{:S(2)}) collective-permute-start(f32[128,256]{1,0:T(8,128)S(1)} %add_add_fusion.refs_0_), channel_id=1, source_target_pairs={{0,4},{4,0},{8,12},{12,8},{16,20},{20,16},{24,28},{28,24},{32,36},... | collective-permute-start | bytes 393224 | tf_op jit(solution)/shard_map/cross_join/ppermute | solution.py:225
  105.1 6.7 %shard_map.54 = (f32[8192,256]{1,0:T(8,128)}, f32[256,256]{1,0:T(8,128)}) custom-call(f32[128,256]{1,0:T(8,128)S(1)} %add_add_fusion.refs_0_, f32[128,256]{1,0:T(8,128)S(1)} %collective-permute-done.22.refs_1_, f32[256,256]{1,0:T(8,128)S(1)} %get-tuple-element.26.refs_2_, f32[2048,256]{1,0:T(8,128)S(1)} %copy-done.1, ...), custom_call_target="tpu_custom_call" | custom-call | tf_op jit(solution)/shard_map/pallas_call | solution.py:130
  (38 shorter events, 12.4 us)
Async XLA Ops:
  0.6 49.2 %collective-permute-start.13 = (f32[2048,256]{1,0:T(8,128)}, f32[2048,256]{1,0:T(8,128)S(1)}, u32[]{:S(2)}, u32[]{:S(2)}) collective-permute-start(f32[2048,256]{1,0:T(8,128)} %refs_3_.3), channel_id=1, source_target_pairs={{0,3},{1,0},{2,1},{3,2},{4,7},{5,4},{6,5},{7,6},{8,11},{9,8},{10,9... | collective-permute-start | bytes 6291464 | tf_op jit(solution)/shard_map/right/ppermute | solution.py:225
  4.3 49.5 %collective-permute-start.11 = (f32[2048,256]{1,0:T(8,128)}, f32[2048,256]{1,0:T(8,128)S(1)}, u32[]{:S(2)}, u32[]{:S(2)}) collective-permute-start(f32[2048,256]{1,0:T(8,128)} %refs_3_.3), channel_id=1, source_target_pairs={{0,1},{1,2},{2,3},{3,0},{4,5},{5,6},{6,7},{7,4},{8,9},{9,10},{10,1... | collective-permute-start | bytes 6291464 | tf_op jit(solution)/shard_map/left/ppermute | solution.py:225
  4.3 1.7 %copy-start = (f32[2048,256]{1,0:T(8,128)S(1)}, f32[2048,256]{1,0:T(8,128)}, u32[]{:S(2)}) copy-start(f32[2048,256]{1,0:T(8,128)} %refs_3_.3) | copy-start | bytes 6291460
  8.0 2.0 %collective-permute-start = (f32[192,128]{1,0:T(8,128)S(1)}, f32[192,128]{1,0:T(8,128)S(1)}, u32[]{:S(2)}, u32[]{:S(2)}) collective-permute-start(f32[192,128]{1,0:T(8,128)S(1)} %get-tuple-element.17), channel_id=1, source_target_pairs={{0,4},{4,0},{8,12},{12,8},{16,20},{20,16},{24,28},{28,24},{32,36},... | collective-permute-start | bytes 294920 | tf_op jit(solution)/shard_map/gram_halves/ppermute | solution.py:225
  10.0 6.0 %collective-permute-start.3 = (f32[192,128]{1,0:T(8,128)S(1)}, f32[192,128]{1,0:T(8,128)S(1)}, u32[]{:S(2)}, u32[]{:S(2)}) collective-permute-start(f32[192,128]{1,0:T(8,128)S(1)} %add.51), channel_id=1, source_target_pairs={{0,16},{4,68},{8,24},{12,76},{16,0},{20,84},{24,8},{28,92},{32,48}... | collective-permute-start | bytes 294920 | tf_op jit(solution)/shard_map/gram_first/ppermute | solution.py:225
  13.7 4.1 %collective-permute-start.2 = (f32[192,128]{1,0:T(8,128)S(1)}, f32[192,128]{1,0:T(8,128)S(1)}, u32[]{:S(2)}, u32[]{:S(2)}) collective-permute-start(f32[192,128]{1,0:T(8,128)S(1)} %add.51), channel_id=1, source_target_pairs={{0,24},{4,100},{8,0},{12,108},{16,8},{20,116},{24,16},{28,124},{32... | collective-permute-start | bytes 294920 | tf_op jit(solution)/shard_map/gram_first/ppermute | solution.py:225
  14.1 5.0 %collective-permute-start.1 = (f32[192,128]{1,0:T(8,128)S(1)}, f32[192,128]{1,0:T(8,128)S(1)}, u32[]{:S(2)}, u32[]{:S(2)}) collective-permute-start(f32[192,128]{1,0:T(8,128)S(1)} %add.51), channel_id=1, source_target_pairs={{0,8},{4,36},{8,16},{12,44},{16,24},{20,52},{24,0},{28,60},{32,40}... | collective-permute-start | bytes 294920 | tf_op jit(solution)/shard_map/gram_first/ppermute | solution.py:225
  19.1 5.1 %collective-permute-start.6 = (f32[192,128]{1,0:T(8,128)S(1)}, f32[192,128]{1,0:T(8,128)S(1)}, u32[]{:S(2)}, u32[]{:S(2)}) collective-permute-start(f32[192,128]{1,0:T(8,128)S(1)} %add_add_fusion.4), channel_id=1, source_target_pairs={{0,64},{4,20},{8,72},{12,28},{16,80},{20,4},{24,88},{28,12},{32,96... | collective-permute-start | bytes 294920 | tf_op jit(solution)/shard_map/gram_second/ppermute | solution.py:225
  22.0 3.8 %collective-permute-start.5 = (f32[192,128]{1,0:T(8,128)S(1)}, f32[192,128]{1,0:T(8,128)S(1)}, u32[]{:S(2)}, u32[]{:S(2)}) collective-permute-start(f32[192,128]{1,0:T(8,128)S(1)} %add_add_fusion.4), channel_id=1, source_target_pairs={{0,96},{4,28},{8,104},{12,4},{16,112},{20,12},{24,120},{28,20},{32... | collective-permute-start | bytes 294920 | tf_op jit(solution)/shard_map/gram_second/ppermute | solution.py:225
  22.8 5.0 %collective-permute-start.4 = (f32[192,128]{1,0:T(8,128)S(1)}, f32[192,128]{1,0:T(8,128)S(1)}, u32[]{:S(2)}, u32[]{:S(2)}) collective-permute-start(f32[192,128]{1,0:T(8,128)S(1)} %add_add_fusion.4), channel_id=1, source_target_pairs={{0,32},{4,12},{8,40},{12,20},{16,48},{20,28},{24,56},{28,4},{32,64... | collective-permute-start | bytes 294920 | tf_op jit(solution)/shard_map/gram_second/ppermute | solution.py:225
  27.8 26.1 %collective-permute-start.9 = (f32[192,128]{1,0:T(8,128)S(1)}, f32[192,128]{1,0:T(8,128)S(1)}, u32[]{:S(2)}, u32[]{:S(2)}) collective-permute-start(f32[192,128]{1,0:T(8,128)S(1)} %add_add_fusion.3), channel_id=1, source_target_pairs={{0,2},{1,3},{2,0},{3,1},{4,6},{5,7},{6,4},{7,5},{8,10},{9,11},{10,... | collective-permute-start | bytes 294920 | tf_op jit(solution)/shard_map/gram_cols/ppermute | solution.py:225
  29.2 24.7 %collective-permute-start.8 = (f32[192,128]{1,0:T(8,128)S(1)}, f32[192,128]{1,0:T(8,128)S(1)}, u32[]{:S(2)}, u32[]{:S(2)}) collective-permute-start(f32[192,128]{1,0:T(8,128)S(1)} %add_add_fusion.3), channel_id=1, source_target_pairs={{0,3},{1,0},{2,1},{3,2},{4,7},{5,4},{6,5},{7,6},{8,11},{9,8},{10,9... | collective-permute-start | bytes 294920 | tf_op jit(solution)/shard_map/gram_cols/ppermute | solution.py:225
  30.9 25.2 %collective-permute-start.7 = (f32[192,128]{1,0:T(8,128)S(1)}, f32[192,128]{1,0:T(8,128)S(1)}, u32[]{:S(2)}, u32[]{:S(2)}) collective-permute-start(f32[192,128]{1,0:T(8,128)S(1)} %add_add_fusion.3), channel_id=1, source_target_pairs={{0,1},{1,2},{2,3},{3,0},{4,5},{5,6},{6,7},{7,4},{8,9},{9,10},{10,1... | collective-permute-start | bytes 294920 | tf_op jit(solution)/shard_map/gram_cols/ppermute | solution.py:225
  49.9 23.0 %collective-permute-start.14 = (f32[1024,256]{1,0:T(8,128)S(1)}, f32[1024,256]{1,0:T(8,128)S(1)}, u32[]{:S(2)}, u32[]{:S(2)}) collective-permute-start(f32[1024,256]{1,0:T(8,128)S(1)} %slice.7), channel_id=1, source_target_pairs={{0,3},{1,0},{2,1},{3,2},{4,7},{5,4},{6,5},{7,6},{8,11},{9,8},{10,9... | collective-permute-start | bytes 3145736 | tf_op jit(solution)/shard_map/far2/ppermute | solution.py:225
  53.8 22.4 %collective-permute-start.12 = (f32[1024,256]{1,0:T(8,128)S(1)}, f32[1024,256]{1,0:T(8,128)S(1)}, u32[]{:S(2)}, u32[]{:S(2)}) collective-permute-start(f32[1024,256]{1,0:T(8,128)S(1)} %slice.6), channel_id=1, source_target_pairs={{0,1},{1,2},{2,3},{3,0},{4,5},{5,6},{6,7},{7,4},{8,9},{9,10},{10,1... | collective-permute-start | bytes 3145736 | tf_op jit(solution)/shard_map/far1/ppermute | solution.py:225
  56.1 13.2 %slice-start = ((s8[8388608]{0:T(1024)(128)(4,1)}), s8[4194304]{0:T(1024)(128)(4,1)S(1)}, s32[]{:S(2)}) async-start(s8[8388608]{0:T(1024)(128)(4,1)} %bitcast), calls=%async_computation | async-start | bytes 8388608
  56.1 13.1 %slice-start.1 = ((s8[8388608]{0:T(1024)(128)(4,1)}), s8[4194304]{0:T(1024)(128)(4,1)S(1)}, s32[]{:S(2)}) async-start(s8[8388608]{0:T(1024)(128)(4,1)} %bitcast), calls=%async_computation.1 | async-start | bytes 8388608
  56.1 13.1 %copy-start.1 = (f32[2048,256]{1,0:T(8,128)S(1)}, f32[2048,256]{1,0:T(8,128)}, u32[]{:S(2)}) copy-start(f32[2048,256]{1,0:T(8,128)} %refs_3_.3) | copy-start | bytes 6291460
  56.1 3.1 %collective-permute-start.10 = (f32[192,128]{1,0:T(8,128)S(1)}, f32[192,128]{1,0:T(8,128)S(1)}, u32[]{:S(2)}, u32[]{:S(2)}) collective-permute-start(f32[192,128]{1,0:T(8,128)S(1)} %add_add_fusion.2.refs_0_), channel_id=1, source_target_pairs={{0,4},{4,0},{8,12},{12,8},{16,20},{20,16},{24,28},{28,24},{32,36},... | collective-permute-start | bytes 294920 | tf_op jit(solution)/shard_map/gram_join/ppermute | solution.py:225
  76.8 5.6 %collective-permute-start.15 = (f32[128,256]{1,0:T(8,128)S(1)}, f32[128,256]{1,0:T(8,128)S(1)}, u32[]{:S(2)}, u32[]{:S(2)}) collective-permute-start(f32[128,256]{1,0:T(8,128)S(1)} %get-tuple-element.25), channel_id=1, source_target_pairs={{0,4},{4,0},{8,12},{12,8},{16,20},{20,16},{24,28},{28,24},{32,36},... | collective-permute-start | bytes 393224 | tf_op jit(solution)/shard_map/cross_halves/ppermute | solution.py:225
  82.4 6.3 %collective-permute-start.18 = (f32[128,256]{1,0:T(8,128)S(1)}, f32[128,256]{1,0:T(8,128)S(1)}, u32[]{:S(2)}, u32[]{:S(2)}) collective-permute-start(f32[128,256]{1,0:T(8,128)S(1)} %add.61), channel_id=1, source_target_pairs={{0,16},{4,68},{8,24},{12,76},{16,0},{20,84},{24,8},{28,92},{32,48}... | collective-permute-start | bytes 393224 | tf_op jit(solution)/shard_map/cross_first/ppermute | solution.py:225
  86.0 4.5 %collective-permute-start.17 = (f32[128,256]{1,0:T(8,128)S(1)}, f32[128,256]{1,0:T(8,128)S(1)}, u32[]{:S(2)}, u32[]{:S(2)}) collective-permute-start(f32[128,256]{1,0:T(8,128)S(1)} %add.61), channel_id=1, source_target_pairs={{0,24},{4,100},{8,0},{12,108},{16,8},{20,116},{24,16},{28,124},{32... | collective-permute-start | bytes 393224 | tf_op jit(solution)/shard_map/cross_first/ppermute | solution.py:225
  86.4 5.3 %collective-permute-start.16 = (f32[128,256]{1,0:T(8,128)S(1)}, f32[128,256]{1,0:T(8,128)S(1)}, u32[]{:S(2)}, u32[]{:S(2)}) collective-permute-start(f32[128,256]{1,0:T(8,128)S(1)} %add.61), channel_id=1, source_target_pairs={{0,8},{4,36},{8,16},{12,44},{16,24},{20,52},{24,0},{28,60},{32,40}... | collective-permute-start | bytes 393224 | tf_op jit(solution)/shard_map/cross_first/ppermute | solution.py:225
  91.8 5.4 %collective-permute-start.21 = (f32[128,256]{1,0:T(8,128)S(1)}, f32[128,256]{1,0:T(8,128)S(1)}, u32[]{:S(2)}, u32[]{:S(2)}) collective-permute-start(f32[128,256]{1,0:T(8,128)S(1)} %add_add_fusion.1), channel_id=1, source_target_pairs={{0,64},{4,20},{8,72},{12,28},{16,80},{20,4},{24,88},{28,12},{32,96... | collective-permute-start | bytes 393224 | tf_op jit(solution)/shard_map/cross_second/ppermute | solution.py:225
  94.3 4.4 %collective-permute-start.20 = (f32[128,256]{1,0:T(8,128)S(1)}, f32[128,256]{1,0:T(8,128)S(1)}, u32[]{:S(2)}, u32[]{:S(2)}) collective-permute-start(f32[128,256]{1,0:T(8,128)S(1)} %add_add_fusion.1), channel_id=1, source_target_pairs={{0,96},{4,28},{8,104},{12,4},{16,112},{20,12},{24,120},{28,20},{32... | collective-permute-start | bytes 393224 | tf_op jit(solution)/shard_map/cross_second/ppermute | solution.py:225
  95.2 5.0 %collective-permute-start.19 = (f32[128,256]{1,0:T(8,128)S(1)}, f32[128,256]{1,0:T(8,128)S(1)}, u32[]{:S(2)}, u32[]{:S(2)}) collective-permute-start(f32[128,256]{1,0:T(8,128)S(1)} %add_add_fusion.1), channel_id=1, source_target_pairs={{0,32},{4,12},{8,40},{12,20},{16,48},{20,28},{24,56},{28,4},{32,64... | collective-permute-start | bytes 393224 | tf_op jit(solution)/shard_map/cross_second/ppermute | solution.py:225
  100.2 4.8 %collective-permute-start.22 = (f32[128,256]{1,0:T(8,128)S(1)}, f32[128,256]{1,0:T(8,128)S(1)}, u32[]{:S(2)}, u32[]{:S(2)}) collective-permute-start(f32[128,256]{1,0:T(8,128)S(1)} %add_add_fusion.refs_0_), channel_id=1, source_target_pairs={{0,4},{4,0},{8,12},{12,8},{16,20},{20,16},{24,28},{28,24},{32,36},... | collective-permute-start | bytes 393224 | tf_op jit(solution)/shard_map/cross_join/ppermute | solution.py:225

commit v4 on v3

--- a/solution.py
+++ b/solution.py
@@ -48,7 +48,7 @@
     wide = wide * lax.rsqrt(diagonal)
     return wide
 
-def factor_kernel(shrink, size, group, mine, other, r_factor, inverse, work):
+def factor_kernel(shrink, size, group, mine, other, r_factor, inverse, gram_inverse, work):
     _, first = whereabouts()
     one = jnp.where(first, mine[...], other[...])
     two = jnp.where(first, other[...], mine[...])
@@ -68,15 +68,17 @@
         if last < 256:
             work[last:, :] -= contract(done[:, last:256], done, ((0,), (0,)), HIGHEST)
     r_factor[...] = jnp.where(rows <= lanes, work[:, :256], 0.0) * shrink
-    inverse[...] = jnp.where(rows >= lanes, work[:, 256:], 0.0)
+    lower = jnp.where(rows >= lanes, work[:, 256:], 0.0)
+    inverse[...] = lower
+    gram_inverse[...] = contract(lower, lower, ((0,), (0,)), HIGHEST)
 
 def factor(mine, other, shrink, size=64, group=4):
     full = jax.ShapeDtypeStruct((256, 256), F32)
     return pl.pallas_call(
         lambda *refs: factor_kernel(shrink, size, group, *refs),
-        out_shape=[full, full],
+        out_shape=[full, full, full],
         in_specs=[pl.BlockSpec(memory_space=pltpu.VMEM)] * 2,
-        out_specs=[pl.BlockSpec(memory_space=pltpu.VMEM)] * 2,
+        out_specs=[pl.BlockSpec(memory_space=pltpu.VMEM)] * 3,
         scratch_shapes=[pltpu.VMEM((256, 512), F32)],
         cost_estimate=pl.CostEstimate(flops=8000000000, bytes_accessed=0, transcendentals=0),
         compiler_params=pltpu.CompilerParams(vmem_limit_bytes=16 << 20),
@@ -98,47 +100,46 @@
     return pl.ds(pl.multiple_of(lax.rem(column + offset, 4) * chunk + low, block), block)
 
 
-def update_kernel(shrink, blocks, block, chunk, mine, other, inverse, *refs):
+def update_kernel(shrink, blocks, block, chunk, mine, other, inverse, gram_inverse, *refs):
     *pieces, trailing, updated, r_cross, result, weights, sems = refs
     column, first = whereabouts()
     top = jnp.where(first, mine[...], other[...])
     bottom = jnp.where(first, other[...], mine[...])
-    coupling = contract(inverse[...], jnp.concatenate([top, bottom], axis=0), ((1,), (0,)), HIGHEST)
-    r_cross[...] = coupling * shrink
-    high, low = split(contract(inverse[...], coupling, ((0,), (0,)), HIGHEST))
-    weights[:256, :] = high
-    weights[256:512, :] = high
-    weights[512:, :] = low
+    cross = jnp.concatenate([top, bottom], axis=0)
+    weights[:256, :], weights[256:, :] = split(contract(gram_inverse[...], cross, ((1,), (0,)), HIGHEST))
     stores = []
     for n, (piece, row, offset, low_row) in enumerate(blocks):
         rows = rows_at(column, offset, low_row, chunk, block)
         high, low = split(pieces[piece][row : row + block, :])
-        product = contract(jnp.concatenate([high, low, high], axis=1), weights[...], ((1,), (0,)))
+        product = contract(high, weights[:256, :], ((1,), (0,)))
+        product += contract(low, weights[:256, :], ((1,), (0,)))
+        product += contract(high, weights[256:, :], ((1,), (0,)))
         here = pl.ds(n * block, block)
         result[here, :] = trailing[rows, :] - product
         store = pltpu.make_async_copy(result.at[here], updated.at[rows], sems.at[n])
         store.start()
         stores.append(store)
+    r_cross[...] = contract(inverse[...], cross, ((1,), (0,)), HIGHEST) * shrink
     for store in stores:
         store.wait()
 
 
-def update(mine, other, inverse, pieces, spots, trailing, shrink, block):
+def update(mine, other, inverse, gram_inverse, pieces, spots, trailing, shrink, block):
     blocks = blocks_of(spots, block)
     vmem, anywhere = pl.BlockSpec(memory_space=pltpu.VMEM), pl.BlockSpec(memory_space=pl.ANY)
     total = trailing.shape[0]
     return pl.pallas_call(
         lambda *refs: update_kernel(shrink, blocks, block, total // 4, *refs),
         out_shape=[jax.ShapeDtypeStruct(trailing.shape, F32), jax.ShapeDtypeStruct((256, 256), F32)],
-        in_specs=[vmem] * (len(pieces) + 4),
+        in_specs=[vmem] * (len(pieces) + 5),
         out_specs=[anywhere, vmem],
         scratch_shapes=[
             pltpu.VMEM((total, 256), F32),
-            pltpu.VMEM((768, 256), BF16),
+            pltpu.VMEM((512, 256), BF16),
             pltpu.SemaphoreType.DMA((len(blocks),)),
         ],
         compiler_params=pltpu.CompilerParams(vmem_limit_bytes=UPDATE_VMEM),
-    )(mine, other, inverse, *pieces, trailing)
+    )(mine, other, inverse, gram_inverse, *pieces, trailing)
 
 
 def cross_kernel(initial, halves, blocks, block, chunk, *refs):
@@ -212,8 +213,8 @@
 
 
 PARTNER = over_rows(lambda z, x, core: (z, x, 1 - core))
-FIRST = [over_rows(lambda z, x, core, k=k: (z, x + k, core) if core == 0 else (z + k, x, core)) for k in ORDER]
-SECOND = [over_rows(lambda z, x, core, k=k: (z + k, x, core) if core == 0 else (z, x + k, core)) for k in ORDER]
+FIRST = [over_rows(lambda z, x, core, k=k: (z, x ^ k, core) if core == 0 else (z ^ k, x, core)) for k in ORDER]
+SECOND = [over_rows(lambda z, x, core, k=k: (z ^ k, x, core) if core == 0 else (z, x ^ k, core)) for k in ORDER]
 
 
 def around(k):
@@ -252,7 +253,7 @@
     far1 = move("far1", left[:half], "cols", around(1))
     far2 = move("far2", right[half:], "cols", around(-1))
     gram = exchange_sum("gram_cols", gram, "cols", [around(k) for k in ORDER])
-    r_factor, inverse = factor(gram, partner("gram_join", gram), shrink, 64, 8)
+    r_factor, inverse, gram_inverse = factor(gram, partner("gram_join", gram), shrink, 64, 8)
 
     (cross,) = cross_part(None, (panel_cols, left, right), ((size, 0, 0), (size, 3, 0), (size, 1, 0)), trailing, False, BLOCK)
     (cross,) = cross_part(cross, (far2,), ((half, 2, half),), trailing, False, BLOCK)
@@ -263,7 +264,7 @@
     cross = exchange_sum("cross_second", cross, "rows", SECOND)
     pieces = (panel_cols, left, right, far1, far2)
     spots = ((size, 0, 0), (size, 3, 0), (size, 1, 0), (half, 2, 0), (half, 2, half))
-    updated, r_cross = update(cross, partner("cross_join", cross), inverse, pieces, spots, trailing, shrink, BLOCK)
+    updated, r_cross = update(cross, partner("cross_join", cross), inverse, gram_inverse, pieces, spots, trailing, shrink, 256)
     return (r_factor, r_cross, updated)
 
 

time: 112 us -> 110 us (0.982)
  starting transfers between devices: 41.2 us -> 38 us
  waiting for transfers between devices: 45.1 us -> 46.5 us
    ppermute x23, starting transfers between devices: 41.2 us -> 38 us  [move(): return lax.ppermute(part, axis, pairs)]
    ppermute x23, waiting for transfers between devices: 45.1 us -> 46.5 us  [move(): return lax.ppermute(part, axis, pairs)]
  transfers between devices with their start and end apart: 23 -> 23, of which waited for: 20 -> 16; matrix products, arithmetic and copies ran while one was open for 0% -> 0% of each run, Pallas kernels for 14% -> 14%
where the time goes in v4:
time: 110 us
  waiting for transfers between devices  46.5 us (42%)
  starting transfers between devices  38 us (35%)
  Pallas kernels  22.3 us (20%)
  local copies, waits for them, and re-layouts  1.81 us (2%)
    ppermute x23, waiting for transfers between devices, move(): return lax.ppermute(part, axis, pairs)  46.5 us
    ppermute x23, starting transfers between devices, move(): return lax.ppermute(part, axis, pairs)  38 us
    pallas_call x1, Pallas kernels, factor(): pl.pallas_call(lambda *refs: factor_kernel(shrink, size, group, *refs), o...  9.99 us
    pallas_call x1, Pallas kernels, update(): pl.pallas_call(lambda *refs: update_kernel(shrink, blocks, block, total /...  6.27 us
    pallas_call x3, Pallas kernels, cross_part(): pl.pallas_call(lambda *refs: cross_kernel(bool(given), halves, blocks, bl...  3.9 us
  transfers between devices with their start and end apart: 23, of which 16 were waited for; matrix products, arithmetic and copies ran while one was open for 0% of the time, Pallas kernels for 14%

profile of v4, /device:TPU:1, one launch (start us, length us, event | category | flops | bytes accessed | tf_op | source)
XLA Modules:
  0.0 109.7 jit_solution(15794472941199205130)
XLA Ops:
  0.6 3.6 %collective-permute-start.13 = (f32[2048,256]{1,0:T(8,128)}, f32[2048,256]{1,0:T(8,128)S(1)}, u32[]{:S(2)}, u32[]{:S(2)}) collective-permute-start(f32[2048,256]{1,0:T(8,128)} %refs_4_.1), channel_id=1, source_target_pairs={{0,3},{1,0},{2,1},{3,2},{4,7},{5,4},{6,5},{7,6},{8,11},{9,8},{10,9... | collective-permute-start | bytes 6291464 | tf_op jit(solution)/shard_map/right/ppermute | solution.py:226
  4.3 1.7 %copy-done = f32[2048,256]{1,0:T(8,128)S(1)} copy-done((f32[2048,256]{1,0:T(8,128)S(1)}, f32[2048,256]{1,0:T(8,128)}, u32[]{:S(2)}) %copy-start) | copy-done | bytes 2097176
  5.9 2.1 %shard_map.49 = (f32[192,128]{1,0:T(8,128)S(1)}, f32[192,128]{1,0:T(8,128)S(1)}) custom-call(f32[2048,256]{1,0:T(8,128)S(1)} %copy-done), custom_call_target="tpu_custom_call" | custom-call | tf_op jit(solution)/shard_map/pallas_call | solution.py:193
  8.0 1.0 collective-permute-start
  10.0 3.7 %collective-permute-start.3 = (f32[192,128]{1,0:T(8,128)S(1)}, f32[192,128]{1,0:T(8,128)S(1)}, u32[]{:S(2)}, u32[]{:S(2)}) collective-permute-start(f32[192,128]{1,0:T(8,128)S(1)} %add.51), channel_id=1, source_target_pairs={{0,16},{4,68},{8,24},{12,76},{16,0},{20,84},{24,8},{28,92},{32,48}... | collective-permute-start | bytes 294920 | tf_op jit(solution)/shard_map/gram_first/ppermute | solution.py:226
  14.4 1.6 %collective-permute-done.3 = f32[192,128]{1,0:T(8,128)S(1)} collective-permute-done((f32[192,128]{1,0:T(8,128)S(1)}, f32[192,128]{1,0:T(8,128)S(1)}, u32[]{:S(2)}, u32[]{:S(2)}) %collective-permute-start.3) | collective-permute-done | bytes 98336 | tf_op jit(solution)/shard_map/gram_first/ppermute | solution.py:226
  16.0 2.7 %collective-permute-done.2 = f32[192,128]{1,0:T(8,128)S(1)} collective-permute-done((f32[192,128]{1,0:T(8,128)S(1)}, f32[192,128]{1,0:T(8,128)S(1)}, u32[]{:S(2)}, u32[]{:S(2)}) %collective-permute-start.2) | collective-permute-done | bytes 98336 | tf_op jit(solution)/shard_map/gram_first/ppermute | solution.py:226
  18.7 2.8 %collective-permute-start.6 = (f32[192,128]{1,0:T(8,128)S(1)}, f32[192,128]{1,0:T(8,128)S(1)}, u32[]{:S(2)}, u32[]{:S(2)}) collective-permute-start(f32[192,128]{1,0:T(8,128)S(1)} %add_add_fusion.4), channel_id=1, source_target_pairs={{0,64},{4,20},{8,72},{12,28},{16,80},{20,4},{24,88},{28,12},{32,96... | collective-permute-start | bytes 294920 | tf_op jit(solution)/shard_map/gram_second/ppermute | solution.py:226
  22.4 1.4 %collective-permute-done.6 = f32[192,128]{1,0:T(8,128)S(1)} collective-permute-done((f32[192,128]{1,0:T(8,128)S(1)}, f32[192,128]{1,0:T(8,128)S(1)}, u32[]{:S(2)}, u32[]{:S(2)}) %collective-permute-start.6) | collective-permute-done | bytes 98336 | tf_op jit(solution)/shard_map/gram_second/ppermute | solution.py:226
  23.8 2.7 %collective-permute-done.5 = f32[192,128]{1,0:T(8,128)S(1)} collective-permute-done((f32[192,128]{1,0:T(8,128)S(1)}, f32[192,128]{1,0:T(8,128)S(1)}, u32[]{:S(2)}, u32[]{:S(2)}) %collective-permute-start.5) | collective-permute-done | bytes 98336 | tf_op jit(solution)/shard_map/gram_second/ppermute | solution.py:226
  26.5 1.4 %collective-permute-start.9 = (f32[192,128]{1,0:T(8,128)S(1)}, f32[192,128]{1,0:T(8,128)S(1)}, u32[]{:S(2)}, u32[]{:S(2)}) collective-permute-start(f32[192,128]{1,0:T(8,128)S(1)} %add_add_fusion.3), channel_id=1, source_target_pairs={{0,2},{1,3},{2,0},{3,1},{4,6},{5,7},{6,4},{7,5},{8,10},{9,11},{10,... | collective-permute-start | bytes 294920 | tf_op jit(solution)/shard_map/gram_cols/ppermute | solution.py:226
  27.9 1.7 %collective-permute-start.8 = (f32[192,128]{1,0:T(8,128)S(1)}, f32[192,128]{1,0:T(8,128)S(1)}, u32[]{:S(2)}, u32[]{:S(2)}) collective-permute-start(f32[192,128]{1,0:T(8,128)S(1)} %add_add_fusion.3), channel_id=1, source_target_pairs={{0,3},{1,0},{2,1},{3,2},{4,7},{5,4},{6,5},{7,6},{8,11},{9,8},{10,9... | collective-permute-start | bytes 294920 | tf_op jit(solution)/shard_map/gram_cols/ppermute | solution.py:226
  30.1 19.7 %collective-permute-done.13.refs_2_.refs_6_ = f32[2048,256]{1,0:T(8,128)S(1)} collective-permute-done((f32[2048,256]{1,0:T(8,128)}, f32[2048,256]{1,0:T(8,128)S(1)}, u32[]{:S(2)}, u32[]{:S(2)}) %collective-permute-start.13) | collective-permute-done | bytes 2097184 | tf_op jit(solution)/shard_map/right/ppermute | solution.py:226
  49.9 3.9 %collective-permute-start.14 = (f32[1024,256]{1,0:T(8,128)S(1)}, f32[1024,256]{1,0:T(8,128)S(1)}, u32[]{:S(2)}, u32[]{:S(2)}) collective-permute-start(f32[1024,256]{1,0:T(8,128)S(1)} %slice.7), channel_id=1, source_target_pairs={{0,3},{1,0},{2,1},{3,2},{4,7},{5,4},{6,5},{7,6},{8,11},{9,8},{10,9... | collective-permute-start | bytes 3145736 | tf_op jit(solution)/shard_map/far2/ppermute | solution.py:226
  53.9 2.2 %collective-permute-done.7 = f32[192,128]{1,0:T(8,128)S(1)} collective-permute-done((f32[192,128]{1,0:T(8,128)S(1)}, f32[192,128]{1,0:T(8,128)S(1)}, u32[]{:S(2)}, u32[]{:S(2)}) %collective-permute-start.7) | collective-permute-done | bytes 98336 | tf_op jit(solution)/shard_map/gram_cols/ppermute | solution.py:226
  56.1 2.1 %collective-permute-start.10 = (f32[192,128]{1,0:T(8,128)S(1)}, f32[192,128]{1,0:T(8,128)S(1)}, u32[]{:S(2)}, u32[]{:S(2)}) collective-permute-start(f32[192,128]{1,0:T(8,128)S(1)} %add_add_fusion.2.refs_0_), channel_id=1, source_target_pairs={{0,4},{4,0},{8,12},{12,8},{16,20},{20,16},{24,28},{28,24},{32,36},... | collective-permute-start | bytes 294920 | tf_op jit(solution)/shard_map/gram_join/ppermute | solution.py:226
  58.3 0.9 collective-permute-done.10.refs_1_
  59.2 10.0 %shard_map.50 = (f32[256,256]{1,0:T(8,128)}, f32[256,256]{1,0:T(8,128)S(1)}, f32[256,256]{1,0:T(8,128)S(1)}) custom-call(f32[192,128]{1,0:T(8,128)S(1)} %add_add_fusion.2.refs_0_, f32[192,128]{1,0:T(8,128)S(1)} %collective-permute-done.10.refs_1_), custom_call_target="tpu_custom_call" | custom-call | flops 8000000000 | tf_op jit(solution)/shard_map/pallas_call | solution.py:77
  69.2 2.7 %shard_map.51.refs_0_ = f32[256,256]{1,0:T(8,128)S(1)} custom-call(f32[2048,256]{1,0:T(8,128)S(1)} %copy-done.1, f32[2048,256]{1,0:T(8,128)S(1)} %collective-permute-done.11.refs_1_.refs_5_, f32[2048,256]{1,0:T(8,128)S(1)} %collective-permute-done.13.refs_2_.refs_6_, f32[8192,256]{1,0:T(8,128)S(1)} %bitcast.1), custom_call_target="tpu_custom_call" | custom-call | tf_op jit(solution)/shard_map/pallas_call | solution.py:173
  71.9 1.0 collective-permute-done.14.refs_1_.refs_8_
  73.5 2.7 %collective-permute-done.12.refs_1_.refs_7_ = f32[1024,256]{1,0:T(8,128)S(1)} collective-permute-done((f32[1024,256]{1,0:T(8,128)S(1)}, f32[1024,256]{1,0:T(8,128)S(1)}, u32[]{:S(2)}, u32[]{:S(2)}) %collective-permute-start.12) | collective-permute-done | bytes 1048608 | tf_op jit(solution)/shard_map/far1/ppermute | solution.py:226
  76.8 4.6 %collective-permute-start.15 = (f32[128,256]{1,0:T(8,128)S(1)}, f32[128,256]{1,0:T(8,128)S(1)}, u32[]{:S(2)}, u32[]{:S(2)}) collective-permute-start(f32[128,256]{1,0:T(8,128)S(1)} %get-tuple-element.26), channel_id=1, source_target_pairs={{0,4},{4,0},{8,12},{12,8},{16,20},{20,16},{24,28},{28,24},{32,36},... | collective-permute-start | bytes 393224 | tf_op jit(solution)/shard_map/cross_halves/ppermute | solution.py:226
  81.4 1.0 collective-permute-done.15
  82.4 3.6 %collective-permute-start.18 = (f32[128,256]{1,0:T(8,128)S(1)}, f32[128,256]{1,0:T(8,128)S(1)}, u32[]{:S(2)}, u32[]{:S(2)}) collective-permute-start(f32[128,256]{1,0:T(8,128)S(1)} %add.61), channel_id=1, source_target_pairs={{0,16},{4,68},{8,24},{12,76},{16,0},{20,84},{24,8},{28,92},{32,48}... | collective-permute-start | bytes 393224 | tf_op jit(solution)/shard_map/cross_first/ppermute | solution.py:226
  86.7 1.9 %collective-permute-done.18 = f32[128,256]{1,0:T(8,128)S(1)} collective-permute-done((f32[128,256]{1,0:T(8,128)S(1)}, f32[128,256]{1,0:T(8,128)S(1)}, u32[]{:S(2)}, u32[]{:S(2)}) %collective-permute-start.18) | collective-permute-done | bytes 131104 | tf_op jit(solution)/shard_map/cross_first/ppermute | solution.py:226
  88.6 2.7 %collective-permute-done.17 = f32[128,256]{1,0:T(8,128)S(1)} collective-permute-done((f32[128,256]{1,0:T(8,128)S(1)}, f32[128,256]{1,0:T(8,128)S(1)}, u32[]{:S(2)}, u32[]{:S(2)}) %collective-permute-start.17) | collective-permute-done | bytes 131104 | tf_op jit(solution)/shard_map/cross_first/ppermute | solution.py:226
  91.3 2.5 %collective-permute-start.21 = (f32[128,256]{1,0:T(8,128)S(1)}, f32[128,256]{1,0:T(8,128)S(1)}, u32[]{:S(2)}, u32[]{:S(2)}) collective-permute-start(f32[128,256]{1,0:T(8,128)S(1)} %add_add_fusion.1), channel_id=1, source_target_pairs={{0,64},{4,20},{8,72},{12,28},{16,80},{20,4},{24,88},{28,12},{32,96... | collective-permute-start | bytes 393224 | tf_op jit(solution)/shard_map/cross_second/ppermute | solution.py:226
  94.7 2.0 %collective-permute-done.21 = f32[128,256]{1,0:T(8,128)S(1)} collective-permute-done((f32[128,256]{1,0:T(8,128)S(1)}, f32[128,256]{1,0:T(8,128)S(1)}, u32[]{:S(2)}, u32[]{:S(2)}) %collective-permute-start.21) | collective-permute-done | bytes 131104 | tf_op jit(solution)/shard_map/cross_second/ppermute | solution.py:226
  96.8 2.2 %collective-permute-done.20 = f32[128,256]{1,0:T(8,128)S(1)} collective-permute-done((f32[128,256]{1,0:T(8,128)S(1)}, f32[128,256]{1,0:T(8,128)S(1)}, u32[]{:S(2)}, u32[]{:S(2)}) %collective-permute-start.20) | collective-permute-done | bytes 131104 | tf_op jit(solution)/shard_map/cross_second/ppermute | solution.py:226
  99.0 3.3 %collective-permute-start.22 = (f32[128,256]{1,0:T(8,128)S(1)}, f32[128,256]{1,0:T(8,128)S(1)}, u32[]{:S(2)}, u32[]{:S(2)}) collective-permute-start(f32[128,256]{1,0:T(8,128)S(1)} %add_add_fusion.refs_0_), channel_id=1, source_target_pairs={{0,4},{4,0},{8,12},{12,8},{16,20},{20,16},{24,28},{28,24},{32,36},... | collective-permute-start | bytes 393224 | tf_op jit(solution)/shard_map/cross_join/ppermute | solution.py:226
  102.3 1.0 collective-permute-done.22.refs_1_
  103.2 6.3 %shard_map.54 = (f32[8192,256]{1,0:T(8,128)}, f32[256,256]{1,0:T(8,128)}) custom-call(f32[128,256]{1,0:T(8,128)S(1)} %add_add_fusion.refs_0_, f32[128,256]{1,0:T(8,128)S(1)} %collective-permute-done.22.refs_1_, f32[256,256]{1,0:T(8,128)S(1)} %get-tuple-element.27.refs_2_, f32[256,256]{1,0:T(8,128)S(1)} %get-tuple-element.28.refs_3_, ...), custom_call_target="tpu_custom_call" | custom-call | tf_op jit(solution)/shard_map/pallas_call | solution.py:131
  (38 shorter events, 6.3 us)
Async XLA Ops:
  0.6 49.2 %collective-permute-start.13 = (f32[2048,256]{1,0:T(8,128)}, f32[2048,256]{1,0:T(8,128)S(1)}, u32[]{:S(2)}, u32[]{:S(2)}) collective-permute-start(f32[2048,256]{1,0:T(8,128)} %refs_4_.1), channel_id=1, source_target_pairs={{0,3},{1,0},{2,1},{3,2},{4,7},{5,4},{6,5},{7,6},{8,11},{9,8},{10,9... | collective-permute-start | bytes 6291464 | tf_op jit(solution)/shard_map/right/ppermute | solution.py:226
  4.3 49.5 %collective-permute-start.11 = (f32[2048,256]{1,0:T(8,128)}, f32[2048,256]{1,0:T(8,128)S(1)}, u32[]{:S(2)}, u32[]{:S(2)}) collective-permute-start(f32[2048,256]{1,0:T(8,128)} %refs_4_.1), channel_id=1, source_target_pairs={{0,1},{1,2},{2,3},{3,0},{4,5},{5,6},{6,7},{7,4},{8,9},{9,10},{10,1... | collective-permute-start | bytes 6291464 | tf_op jit(solution)/shard_map/left/ppermute | solution.py:226
  4.3 1.7 %copy-start = (f32[2048,256]{1,0:T(8,128)S(1)}, f32[2048,256]{1,0:T(8,128)}, u32[]{:S(2)}) copy-start(f32[2048,256]{1,0:T(8,128)} %refs_4_.1) | copy-start | bytes 6291460
  8.0 2.0 %collective-permute-start = (f32[192,128]{1,0:T(8,128)S(1)}, f32[192,128]{1,0:T(8,128)S(1)}, u32[]{:S(2)}, u32[]{:S(2)}) collective-permute-start(f32[192,128]{1,0:T(8,128)S(1)} %get-tuple-element.18), channel_id=1, source_target_pairs={{0,4},{4,0},{8,12},{12,8},{16,20},{20,16},{24,28},{28,24},{32,36},... | collective-permute-start | bytes 294920 | tf_op jit(solution)/shard_map/gram_halves/ppermute | solution.py:226
  10.0 6.0 %collective-permute-start.3 = (f32[192,128]{1,0:T(8,128)S(1)}, f32[192,128]{1,0:T(8,128)S(1)}, u32[]{:S(2)}, u32[]{:S(2)}) collective-permute-start(f32[192,128]{1,0:T(8,128)S(1)} %add.51), channel_id=1, source_target_pairs={{0,16},{4,68},{8,24},{12,76},{16,0},{20,84},{24,8},{28,92},{32,48}... | collective-permute-start | bytes 294920 | tf_op jit(solution)/shard_map/gram_first/ppermute | solution.py:226
  13.7 5.0 %collective-permute-start.2 = (f32[192,128]{1,0:T(8,128)S(1)}, f32[192,128]{1,0:T(8,128)S(1)}, u32[]{:S(2)}, u32[]{:S(2)}) collective-permute-start(f32[192,128]{1,0:T(8,128)S(1)} %add.51), channel_id=1, source_target_pairs={{0,24},{4,100},{8,16},{12,108},{16,8},{20,116},{24,0},{28,124},{32... | collective-permute-start | bytes 294920 | tf_op jit(solution)/shard_map/gram_first/ppermute | solution.py:226
  14.1 4.5 %collective-permute-start.1 = (f32[192,128]{1,0:T(8,128)S(1)}, f32[192,128]{1,0:T(8,128)S(1)}, u32[]{:S(2)}, u32[]{:S(2)}) collective-permute-start(f32[192,128]{1,0:T(8,128)S(1)} %add.51), channel_id=1, source_target_pairs={{0,8},{4,36},{8,0},{12,44},{16,24},{20,52},{24,16},{28,60},{32,40}... | collective-permute-start | bytes 294920 | tf_op jit(solution)/shard_map/gram_first/ppermute | solution.py:226
  18.7 5.1 %collective-permute-start.6 = (f32[192,128]{1,0:T(8,128)S(1)}, f32[192,128]{1,0:T(8,128)S(1)}, u32[]{:S(2)}, u32[]{:S(2)}) collective-permute-start(f32[192,128]{1,0:T(8,128)S(1)} %add_add_fusion.4), channel_id=1, source_target_pairs={{0,64},{4,20},{8,72},{12,28},{16,80},{20,4},{24,88},{28,12},{32,96... | collective-permute-start | bytes 294920 | tf_op jit(solution)/shard_map/gram_second/ppermute | solution.py:226
  21.5 5.0 %collective-permute-start.5 = (f32[192,128]{1,0:T(8,128)S(1)}, f32[192,128]{1,0:T(8,128)S(1)}, u32[]{:S(2)}, u32[]{:S(2)}) collective-permute-start(f32[192,128]{1,0:T(8,128)S(1)} %add_add_fusion.4), channel_id=1, source_target_pairs={{0,96},{4,28},{8,104},{12,20},{16,112},{20,12},{24,120},{28,4},{32... | collective-permute-start | bytes 294920 | tf_op jit(solution)/shard_map/gram_second/ppermute | solution.py:226
  22.4 4.1 %collective-permute-start.4 = (f32[192,128]{1,0:T(8,128)S(1)}, f32[192,128]{1,0:T(8,128)S(1)}, u32[]{:S(2)}, u32[]{:S(2)}) collective-permute-start(f32[192,128]{1,0:T(8,128)S(1)} %add_add_fusion.4), channel_id=1, source_target_pairs={{0,32},{4,12},{8,40},{12,4},{16,48},{20,28},{24,56},{28,20},{32,0}... | collective-permute-start | bytes 294920 | tf_op jit(solution)/shard_map/gram_second/ppermute | solution.py:226
  26.5 27.4 %collective-permute-start.9 = (f32[192,128]{1,0:T(8,128)S(1)}, f32[192,128]{1,0:T(8,128)S(1)}, u32[]{:S(2)}, u32[]{:S(2)}) collective-permute-start(f32[192,128]{1,0:T(8,128)S(1)} %add_add_fusion.3), channel_id=1, source_target_pairs={{0,2},{1,3},{2,0},{3,1},{4,6},{5,7},{6,4},{7,5},{8,10},{9,11},{10,... | collective-permute-start | bytes 294920 | tf_op jit(solution)/shard_map/gram_cols/ppermute | solution.py:226
  27.9 26.0 %collective-permute-start.8 = (f32[192,128]{1,0:T(8,128)S(1)}, f32[192,128]{1,0:T(8,128)S(1)}, u32[]{:S(2)}, u32[]{:S(2)}) collective-permute-start(f32[192,128]{1,0:T(8,128)S(1)} %add_add_fusion.3), channel_id=1, source_target_pairs={{0,3},{1,0},{2,1},{3,2},{4,7},{5,4},{6,5},{7,6},{8,11},{9,8},{10,9... | collective-permute-start | bytes 294920 | tf_op jit(solution)/shard_map/gram_cols/ppermute | solution.py:226
  29.6 26.5 %collective-permute-start.7 = (f32[192,128]{1,0:T(8,128)S(1)}, f32[192,128]{1,0:T(8,128)S(1)}, u32[]{:S(2)}, u32[]{:S(2)}) collective-permute-start(f32[192,128]{1,0:T(8,128)S(1)} %add_add_fusion.3), channel_id=1, source_target_pairs={{0,1},{1,2},{2,3},{3,0},{4,5},{5,6},{6,7},{7,4},{8,9},{9,10},{10,1... | collective-permute-start | bytes 294920 | tf_op jit(solution)/shard_map/gram_cols/ppermute | solution.py:226
  49.9 23.0 %collective-permute-start.14 = (f32[1024,256]{1,0:T(8,128)S(1)}, f32[1024,256]{1,0:T(8,128)S(1)}, u32[]{:S(2)}, u32[]{:S(2)}) collective-permute-start(f32[1024,256]{1,0:T(8,128)S(1)} %slice.7), channel_id=1, source_target_pairs={{0,3},{1,0},{2,1},{3,2},{4,7},{5,4},{6,5},{7,6},{8,11},{9,8},{10,9... | collective-permute-start | bytes 3145736 | tf_op jit(solution)/shard_map/far2/ppermute | solution.py:226
  53.8 22.4 %collective-permute-start.12 = (f32[1024,256]{1,0:T(8,128)S(1)}, f32[1024,256]{1,0:T(8,128)S(1)}, u32[]{:S(2)}, u32[]{:S(2)}) collective-permute-start(f32[1024,256]{1,0:T(8,128)S(1)} %slice.6), channel_id=1, source_target_pairs={{0,1},{1,2},{2,3},{3,0},{4,5},{5,6},{6,7},{7,4},{8,9},{9,10},{10,1... | collective-permute-start | bytes 3145736 | tf_op jit(solution)/shard_map/far1/ppermute | solution.py:226
  56.1 13.1 %slice-start = ((s8[8388608]{0:T(1024)(128)(4,1)}), s8[4194304]{0:T(1024)(128)(4,1)S(1)}, s32[]{:S(2)}) async-start(s8[8388608]{0:T(1024)(128)(4,1)} %bitcast), calls=%async_computation | async-start | bytes 8388608
  56.1 13.1 %slice-start.1 = ((s8[8388608]{0:T(1024)(128)(4,1)}), s8[4194304]{0:T(1024)(128)(4,1)S(1)}, s32[]{:S(2)}) async-start(s8[8388608]{0:T(1024)(128)(4,1)} %bitcast), calls=%async_computation.1 | async-start | bytes 8388608
  56.1 13.1 %copy-start.1 = (f32[2048,256]{1,0:T(8,128)S(1)}, f32[2048,256]{1,0:T(8,128)}, u32[]{:S(2)}) copy-start(f32[2048,256]{1,0:T(8,128)} %refs_4_.1) | copy-start | bytes 6291460
  56.1 3.1 %collective-permute-start.10 = (f32[192,128]{1,0:T(8,128)S(1)}, f32[192,128]{1,0:T(8,128)S(1)}, u32[]{:S(2)}, u32[]{:S(2)}) collective-permute-start(f32[192,128]{1,0:T(8,128)S(1)} %add_add_fusion.2.refs_0_), channel_id=1, source_target_pairs={{0,4},{4,0},{8,12},{12,8},{16,20},{20,16},{24,28},{28,24},{32,36},... | collective-permute-start | bytes 294920 | tf_op jit(solution)/shard_map/gram_join/ppermute | solution.py:226
  76.8 5.6 %collective-permute-start.15 = (f32[128,256]{1,0:T(8,128)S(1)}, f32[128,256]{1,0:T(8,128)S(1)}, u32[]{:S(2)}, u32[]{:S(2)}) collective-permute-start(f32[128,256]{1,0:T(8,128)S(1)} %get-tuple-element.26), channel_id=1, source_target_pairs={{0,4},{4,0},{8,12},{12,8},{16,20},{20,16},{24,28},{28,24},{32,36},... | collective-permute-start | bytes 393224 | tf_op jit(solution)/shard_map/cross_halves/ppermute | solution.py:226
  82.4 6.3 %collective-permute-start.18 = (f32[128,256]{1,0:T(8,128)S(1)}, f32[128,256]{1,0:T(8,128)S(1)}, u32[]{:S(2)}, u32[]{:S(2)}) collective-permute-start(f32[128,256]{1,0:T(8,128)S(1)} %add.61), channel_id=1, source_target_pairs={{0,16},{4,68},{8,24},{12,76},{16,0},{20,84},{24,8},{28,92},{32,48}... | collective-permute-start | bytes 393224 | tf_op jit(solution)/shard_map/cross_first/ppermute | solution.py:226
  86.0 5.3 %collective-permute-start.17 = (f32[128,256]{1,0:T(8,128)S(1)}, f32[128,256]{1,0:T(8,128)S(1)}, u32[]{:S(2)}, u32[]{:S(2)}) collective-permute-start(f32[128,256]{1,0:T(8,128)S(1)} %add.61), channel_id=1, source_target_pairs={{0,24},{4,100},{8,16},{12,108},{16,8},{20,116},{24,0},{28,124},{32... | collective-permute-start | bytes 393224 | tf_op jit(solution)/shard_map/cross_first/ppermute | solution.py:226
  86.4 4.9 %collective-permute-start.16 = (f32[128,256]{1,0:T(8,128)S(1)}, f32[128,256]{1,0:T(8,128)S(1)}, u32[]{:S(2)}, u32[]{:S(2)}) collective-permute-start(f32[128,256]{1,0:T(8,128)S(1)} %add.61), channel_id=1, source_target_pairs={{0,8},{4,36},{8,0},{12,44},{16,24},{20,52},{24,16},{28,60},{32,40}... | collective-permute-start | bytes 393224 | tf_op jit(solution)/shard_map/cross_first/ppermute | solution.py:226
  91.3 5.4 %collective-permute-start.21 = (f32[128,256]{1,0:T(8,128)S(1)}, f32[128,256]{1,0:T(8,128)S(1)}, u32[]{:S(2)}, u32[]{:S(2)}) collective-permute-start(f32[128,256]{1,0:T(8,128)S(1)} %add_add_fusion.1), channel_id=1, source_target_pairs={{0,64},{4,20},{8,72},{12,28},{16,80},{20,4},{24,88},{28,12},{32,96... | collective-permute-start | bytes 393224 | tf_op jit(solution)/shard_map/cross_second/ppermute | solution.py:226
  93.9 5.0 %collective-permute-start.20 = (f32[128,256]{1,0:T(8,128)S(1)}, f32[128,256]{1,0:T(8,128)S(1)}, u32[]{:S(2)}, u32[]{:S(2)}) collective-permute-start(f32[128,256]{1,0:T(8,128)S(1)} %add_add_fusion.1), channel_id=1, source_target_pairs={{0,96},{4,28},{8,104},{12,20},{16,112},{20,12},{24,120},{28,4},{32... | collective-permute-start | bytes 393224 | tf_op jit(solution)/shard_map/cross_second/ppermute | solution.py:226
  94.7 4.2 %collective-permute-start.19 = (f32[128,256]{1,0:T(8,128)S(1)}, f32[128,256]{1,0:T(8,128)S(1)}, u32[]{:S(2)}, u32[]{:S(2)}) collective-permute-start(f32[128,256]{1,0:T(8,128)S(1)} %add_add_fusion.1), channel_id=1, source_target_pairs={{0,32},{4,12},{8,40},{12,4},{16,48},{20,28},{24,56},{28,20},{32,0}... | collective-permute-start | bytes 393224 | tf_op jit(solution)/shard_map/cross_second/ppermute | solution.py:226
  99.0 4.3 %collective-permute-start.22 = (f32[128,256]{1,0:T(8,128)S(1)}, f32[128,256]{1,0:T(8,128)S(1)}, u32[]{:S(2)}, u32[]{:S(2)}) collective-permute-start(f32[128,256]{1,0:T(8,128)S(1)} %add_add_fusion.refs_0_), channel_id=1, source_target_pairs={{0,4},{4,0},{8,12},{12,8},{16,20},{20,16},{24,28},{28,24},{32,36},... | collective-permute-start | bytes 393224 | tf_op jit(solution)/shard_map/cross_join/ppermute | solution.py:226

commit v5 on v4

--- a/solution.py
+++ b/solution.py
@@ -10,6 +10,7 @@
 F32, BF16 = jnp.float32, jnp.bfloat16
 HIGHEST = lax.Precision.HIGHEST
 BLOCK = 512
+FEWER = 64
 UPDATE_VMEM = 14 << 20
 CROSS_VMEM = 8 << 20
 
@@ -90,31 +91,32 @@
 
 def blocks_of(pieces, block):
     return [
-        (n, row, offset, low + row)
+        (n, row, offset, low + row, min(block, count - row))
         for n, (count, offset, low) in enumerate(pieces)
         for row in range(0, count, block)
     ]
 
 
-def rows_at(column, offset, low, chunk, block):
-    return pl.ds(pl.multiple_of(lax.rem(column + offset, 4) * chunk + low, block), block)
-
-
-def update_kernel(shrink, blocks, block, chunk, mine, other, inverse, gram_inverse, *refs):
+def rows_at(column, offset, low, chunk, count):
+    return pl.ds(pl.multiple_of(lax.rem(column + offset, 4) * chunk + low, 64), count)
+
+
+def update_kernel(shrink, blocks, chunk, mine, other, inverse, gram_inverse, *refs):
     *pieces, trailing, updated, r_cross, result, weights, sems = refs
     column, first = whereabouts()
     top = jnp.where(first, mine[...], other[...])
     bottom = jnp.where(first, other[...], mine[...])
     cross = jnp.concatenate([top, bottom], axis=0)
     weights[:256, :], weights[256:, :] = split(contract(gram_inverse[...], cross, ((1,), (0,)), HIGHEST))
-    stores = []
-    for n, (piece, row, offset, low_row) in enumerate(blocks):
-        rows = rows_at(column, offset, low_row, chunk, block)
-        high, low = split(pieces[piece][row : row + block, :])
+    stores, done = [], 0
+    for n, (piece, row, offset, low_row, count) in enumerate(blocks):
+        rows = rows_at(column, offset, low_row, chunk, count)
+        high, low = split(pieces[piece][row : row + count, :])
         product = contract(high, weights[:256, :], ((1,), (0,)))
         product += contract(low, weights[:256, :], ((1,), (0,)))
         product += contract(high, weights[256:, :], ((1,), (0,)))
-        here = pl.ds(n * block, block)
+        here = pl.ds(done, count)
+        done += count
         result[here, :] = trailing[rows, :] - product
         store = pltpu.make_async_copy(result.at[here], updated.at[rows], sems.at[n])
         store.start()
@@ -129,7 +131,7 @@
     vmem, anywhere = pl.BlockSpec(memory_space=pltpu.VMEM), pl.BlockSpec(memory_space=pl.ANY)
     total = trailing.shape[0]
     return pl.pallas_call(
-        lambda *refs: update_kernel(shrink, blocks, block, total // 4, *refs),
+        lambda *refs: update_kernel(shrink, blocks, total // 4, *refs),
         out_shape=[jax.ShapeDtypeStruct(trailing.shape, F32), jax.ShapeDtypeStruct((256, 256), F32)],
         in_specs=[vmem] * (len(pieces) + 5),
         out_specs=[anywhere, vmem],
@@ -142,16 +144,16 @@
     )(mine, other, inverse, gram_inverse, *pieces, trailing)
 
 
-def cross_kernel(initial, halves, blocks, block, chunk, *refs):
+def cross_kernel(initial, halves, blocks, chunk, *refs):
     refs = list(refs)
     column, first = whereabouts()
     total = refs.pop(0)[...] if initial else None
     count = 2 if halves else 1
     *pieces, trailing = refs[:-count]
     outs = refs[-count:]
-    for piece, row, offset, low in blocks:
-        left = split(pieces[piece][row : row + block, :])
-        right = split(trailing[rows_at(column, offset, low, chunk, block), :])
+    for piece, row, offset, low, size in blocks:
+        left = split(pieces[piece][row : row + size, :])
+        right = split(trailing[rows_at(column, offset, low, chunk, size), :])
         product = contract(
             jnp.concatenate([left[0], left[1], left[0]], axis=0),
             jnp.concatenate([right[0], right[0], right[1]], axis=0),
@@ -171,7 +173,7 @@
     given = [] if initial is None else [initial]
     shapes = [(128, 256)] * 2 if halves else [(256, 256)]
     return pl.pallas_call(
-        lambda *refs: cross_kernel(bool(given), halves, blocks, block, trailing.shape[0] // 4, *refs),
+        lambda *refs: cross_kernel(bool(given), halves, blocks, trailing.shape[0] // 4, *refs),
         out_shape=[jax.ShapeDtypeStruct(shape, F32) for shape in shapes],
         in_specs=[vmem] * (len(given) + len(pieces) + 1),
         out_specs=[vmem] * len(shapes),
@@ -240,6 +242,7 @@
     shrink = 1.0 / math.sqrt(rows_total)
     size = panel_cols.shape[0]
     half = size // 2
+    fewer = half - FEWER
     barrier = lax.optimization_barrier
     left = move("left", panel_cols, "cols", around(1))
     right = move("right", panel_cols, "cols", around(-1))
@@ -250,20 +253,20 @@
     gram = exchange_sum("gram_second", gram, "rows", SECOND)
     left, _ = barrier((left, gram))
     right, _ = barrier((right, gram))
-    far1 = move("far1", left[:half], "cols", around(1))
-    far2 = move("far2", right[half:], "cols", around(-1))
+    far1 = move("far1", left[:fewer], "cols", around(1))
+    far2 = move("far2", right[fewer:], "cols", around(-1))
     gram = exchange_sum("gram_cols", gram, "cols", [around(k) for k in ORDER])
     r_factor, inverse, gram_inverse = factor(gram, partner("gram_join", gram), shrink, 64, 8)
 
     (cross,) = cross_part(None, (panel_cols, left, right), ((size, 0, 0), (size, 3, 0), (size, 1, 0)), trailing, False, BLOCK)
-    (cross,) = cross_part(cross, (far2,), ((half, 2, half),), trailing, False, BLOCK)
+    (cross,) = cross_part(cross, (far2,), ((size - fewer, 2, fewer),), trailing, False, BLOCK)
     inverse, far1, cross = barrier((inverse, far1, cross))
-    keep, send = cross_part(cross, (far1,), ((half, 2, 0),), trailing, True, BLOCK)
+    keep, send = cross_part(cross, (far1,), ((fewer, 2, 0),), trailing, True, BLOCK)
     cross = keep + partner("cross_halves", send)
     cross = exchange_sum("cross_first", cross, "rows", FIRST)
     cross = exchange_sum("cross_second", cross, "rows", SECOND)
     pieces = (panel_cols, left, right, far1, far2)
-    spots = ((size, 0, 0), (size, 3, 0), (size, 1, 0), (half, 2, 0), (half, 2, half))
+    spots = ((size, 0, 0), (size, 3, 0), (size, 1, 0), (fewer, 2, 0), (size - fewer, 2, fewer))
     updated, r_cross = update(cross, partner("cross_join", cross), inverse, gram_inverse, pieces, spots, trailing, shrink, 256)
     return (r_factor, r_cross, updated)
 

time: 110 us -> 109 us (level)
  waiting for transfers between devices: 46.5 us -> 45.2 us
    ppermute x23, waiting for transfers between devices: 46.5 us -> 45.2 us  [move(): return lax.ppermute(part, axis, pairs)]
  transfers between devices with their start and end apart: 23 -> 23, of which waited for: 16 -> 15; matrix products, arithmetic and copies ran while one was open for 0% -> 0% of each run, Pallas kernels for 14% -> 14%
where the time goes in v5:
time: 109 us
  waiting for transfers between devices  45.2 us (41%)
  starting transfers between devices  38.1 us (35%)
  Pallas kernels  22.3 us (20%)
  local copies, waits for them, and re-layouts  1.81 us (2%)
    ppermute x23, waiting for transfers between devices, move(): return lax.ppermute(part, axis, pairs)  45.2 us
    ppermute x23, starting transfers between devices, move(): return lax.ppermute(part, axis, pairs)  38.1 us
    pallas_call x1, Pallas kernels, factor(): pl.pallas_call(lambda *refs: factor_kernel(shrink, size, group, *refs), o...  9.99 us
    pallas_call x1, Pallas kernels, update(): pl.pallas_call(lambda *refs: update_kernel(shrink, blocks, total // 4, *r...  6.29 us
    pallas_call x3, Pallas kernels, cross_part(): pl.pallas_call(lambda *refs: cross_kernel(bool(given), halves, blocks, tr...  3.94 us
  transfers between devices with their start and end apart: 23, of which 15 were waited for; matrix products, arithmetic and copies ran while one was open for 0% of the time, Pallas kernels for 14%

profile of v5, /device:TPU:1, one launch (start us, length us, event | category | flops | bytes accessed | tf_op | source)
XLA Modules:
  0.0 108.5 jit_solution(5483939904194894872)
XLA Ops:
  0.6 3.6 %collective-permute-start.13 = (f32[2048,256]{1,0:T(8,128)}, f32[2048,256]{1,0:T(8,128)S(1)}, u32[]{:S(2)}, u32[]{:S(2)}) collective-permute-start(f32[2048,256]{1,0:T(8,128)} %refs_4_.1), channel_id=1, source_target_pairs={{0,3},{1,0},{2,1},{3,2},{4,7},{5,4},{6,5},{7,6},{8,11},{9,8},{10,9... | collective-permute-start | bytes 6291464 | tf_op jit(solution)/shard_map/right/ppermute | solution.py:228
  4.3 1.7 %copy-done = f32[2048,256]{1,0:T(8,128)S(1)} copy-done((f32[2048,256]{1,0:T(8,128)S(1)}, f32[2048,256]{1,0:T(8,128)}, u32[]{:S(2)}) %copy-start) | copy-done | bytes 2097176
  5.9 2.1 %shard_map.49 = (f32[192,128]{1,0:T(8,128)S(1)}, f32[192,128]{1,0:T(8,128)S(1)}) custom-call(f32[2048,256]{1,0:T(8,128)S(1)} %copy-done), custom_call_target="tpu_custom_call" | custom-call | tf_op jit(solution)/shard_map/pallas_call | solution.py:195
  8.0 1.0 collective-permute-start
  9.1 0.9 collective-permute-done
  10.0 3.7 %collective-permute-start.3 = (f32[192,128]{1,0:T(8,128)S(1)}, f32[192,128]{1,0:T(8,128)S(1)}, u32[]{:S(2)}, u32[]{:S(2)}) collective-permute-start(f32[192,128]{1,0:T(8,128)S(1)} %add.51), channel_id=1, source_target_pairs={{0,16},{4,68},{8,24},{12,76},{16,0},{20,84},{24,8},{28,92},{32,48}... | collective-permute-start | bytes 294920 | tf_op jit(solution)/shard_map/gram_first/ppermute | solution.py:228
  14.4 1.6 %collective-permute-done.3 = f32[192,128]{1,0:T(8,128)S(1)} collective-permute-done((f32[192,128]{1,0:T(8,128)S(1)}, f32[192,128]{1,0:T(8,128)S(1)}, u32[]{:S(2)}, u32[]{:S(2)}) %collective-permute-start.3) | collective-permute-done | bytes 98336 | tf_op jit(solution)/shard_map/gram_first/ppermute | solution.py:228
  16.0 2.7 %collective-permute-done.2 = f32[192,128]{1,0:T(8,128)S(1)} collective-permute-done((f32[192,128]{1,0:T(8,128)S(1)}, f32[192,128]{1,0:T(8,128)S(1)}, u32[]{:S(2)}, u32[]{:S(2)}) %collective-permute-start.2) | collective-permute-done | bytes 98336 | tf_op jit(solution)/shard_map/gram_first/ppermute | solution.py:228
  18.7 2.8 %collective-permute-start.6 = (f32[192,128]{1,0:T(8,128)S(1)}, f32[192,128]{1,0:T(8,128)S(1)}, u32[]{:S(2)}, u32[]{:S(2)}) collective-permute-start(f32[192,128]{1,0:T(8,128)S(1)} %add_add_fusion.4), channel_id=1, source_target_pairs={{0,64},{4,20},{8,72},{12,28},{16,80},{20,4},{24,88},{28,12},{32,96... | collective-permute-start | bytes 294920 | tf_op jit(solution)/shard_map/gram_second/ppermute | solution.py:228
  22.4 1.4 %collective-permute-done.6 = f32[192,128]{1,0:T(8,128)S(1)} collective-permute-done((f32[192,128]{1,0:T(8,128)S(1)}, f32[192,128]{1,0:T(8,128)S(1)}, u32[]{:S(2)}, u32[]{:S(2)}) %collective-permute-start.6) | collective-permute-done | bytes 98336 | tf_op jit(solution)/shard_map/gram_second/ppermute | solution.py:228
  23.8 2.7 %collective-permute-done.5 = f32[192,128]{1,0:T(8,128)S(1)} collective-permute-done((f32[192,128]{1,0:T(8,128)S(1)}, f32[192,128]{1,0:T(8,128)S(1)}, u32[]{:S(2)}, u32[]{:S(2)}) %collective-permute-start.5) | collective-permute-done | bytes 98336 | tf_op jit(solution)/shard_map/gram_second/ppermute | solution.py:228
  26.5 1.4 %collective-permute-start.9 = (f32[192,128]{1,0:T(8,128)S(1)}, f32[192,128]{1,0:T(8,128)S(1)}, u32[]{:S(2)}, u32[]{:S(2)}) collective-permute-start(f32[192,128]{1,0:T(8,128)S(1)} %add_add_fusion.3), channel_id=1, source_target_pairs={{0,2},{1,3},{2,0},{3,1},{4,6},{5,7},{6,4},{7,5},{8,10},{9,11},{10,... | collective-permute-start | bytes 294920 | tf_op jit(solution)/shard_map/gram_cols/ppermute | solution.py:228
  27.9 1.7 %collective-permute-start.8 = (f32[192,128]{1,0:T(8,128)S(1)}, f32[192,128]{1,0:T(8,128)S(1)}, u32[]{:S(2)}, u32[]{:S(2)}) collective-permute-start(f32[192,128]{1,0:T(8,128)S(1)} %add_add_fusion.3), channel_id=1, source_target_pairs={{0,3},{1,0},{2,1},{3,2},{4,7},{5,4},{6,5},{7,6},{8,11},{9,8},{10,9... | collective-permute-start | bytes 294920 | tf_op jit(solution)/shard_map/gram_cols/ppermute | solution.py:228
  30.1 19.7 %collective-permute-done.13.refs_2_.refs_6_ = f32[2048,256]{1,0:T(8,128)S(1)} collective-permute-done((f32[2048,256]{1,0:T(8,128)}, f32[2048,256]{1,0:T(8,128)S(1)}, u32[]{:S(2)}, u32[]{:S(2)}) %collective-permute-start.13) | collective-permute-done | bytes 2097184 | tf_op jit(solution)/shard_map/right/ppermute | solution.py:228
  49.9 3.9 %collective-permute-start.14 = (f32[1088,256]{1,0:T(8,128)S(1)}, f32[1088,256]{1,0:T(8,128)S(1)}, u32[]{:S(2)}, u32[]{:S(2)}) collective-permute-start(f32[1088,256]{1,0:T(8,128)S(1)} %slice.7), channel_id=1, source_target_pairs={{0,3},{1,0},{2,1},{3,2},{4,7},{5,4},{6,5},{7,6},{8,11},{9,8},{10,9... | collective-permute-start | bytes 3342344 | tf_op jit(solution)/shard_map/far2/ppermute | solution.py:228
  53.9 2.2 %collective-permute-done.7 = f32[192,128]{1,0:T(8,128)S(1)} collective-permute-done((f32[192,128]{1,0:T(8,128)S(1)}, f32[192,128]{1,0:T(8,128)S(1)}, u32[]{:S(2)}, u32[]{:S(2)}) %collective-permute-start.7) | collective-permute-done | bytes 98336 | tf_op jit(solution)/shard_map/gram_cols/ppermute | solution.py:228
  56.1 2.1 %collective-permute-start.10 = (f32[192,128]{1,0:T(8,128)S(1)}, f32[192,128]{1,0:T(8,128)S(1)}, u32[]{:S(2)}, u32[]{:S(2)}) collective-permute-start(f32[192,128]{1,0:T(8,128)S(1)} %add_add_fusion.2.refs_0_), channel_id=1, source_target_pairs={{0,4},{4,0},{8,12},{12,8},{16,20},{20,16},{24,28},{28,24},{32,36},... | collective-permute-start | bytes 294920 | tf_op jit(solution)/shard_map/gram_join/ppermute | solution.py:228
  58.3 0.9 collective-permute-done.10.refs_1_
  59.2 10.0 %shard_map.50 = (f32[256,256]{1,0:T(8,128)}, f32[256,256]{1,0:T(8,128)S(1)}, f32[256,256]{1,0:T(8,128)S(1)}) custom-call(f32[192,128]{1,0:T(8,128)S(1)} %add_add_fusion.2.refs_0_, f32[192,128]{1,0:T(8,128)S(1)} %collective-permute-done.10.refs_1_), custom_call_target="tpu_custom_call" | custom-call | flops 8000000000 | tf_op jit(solution)/shard_map/pallas_call | solution.py:78
  69.2 2.7 %shard_map.51.refs_0_ = f32[256,256]{1,0:T(8,128)S(1)} custom-call(f32[2048,256]{1,0:T(8,128)S(1)} %copy-done.1, f32[2048,256]{1,0:T(8,128)S(1)} %collective-permute-done.11.refs_1_.refs_5_, f32[2048,256]{1,0:T(8,128)S(1)} %collective-permute-done.13.refs_2_.refs_6_, f32[8192,256]{1,0:T(8,128)S(1)} %bitcast.1), custom_call_target="tpu_custom_call" | custom-call | tf_op jit(solution)/shard_map/pallas_call | solution.py:175
  71.9 2.4 %collective-permute-done.14.refs_1_.refs_8_ = f32[1088,256]{1,0:T(8,128)S(1)} collective-permute-done((f32[1088,256]{1,0:T(8,128)S(1)}, f32[1088,256]{1,0:T(8,128)S(1)}, u32[]{:S(2)}, u32[]{:S(2)}) %collective-permute-start.14) | collective-permute-done | bytes 1114144 | tf_op jit(solution)/shard_map/far2/ppermute | solution.py:228
  75.6 4.4 %collective-permute-start.15 = (f32[128,256]{1,0:T(8,128)S(1)}, f32[128,256]{1,0:T(8,128)S(1)}, u32[]{:S(2)}, u32[]{:S(2)}) collective-permute-start(f32[128,256]{1,0:T(8,128)S(1)} %get-tuple-element.26), channel_id=1, source_target_pairs={{0,4},{4,0},{8,12},{12,8},{16,20},{20,16},{24,28},{28,24},{32,36},... | collective-permute-start | bytes 393224 | tf_op jit(solution)/shard_map/cross_halves/ppermute | solution.py:228
  80.0 1.0 collective-permute-done.15
  81.0 3.6 %collective-permute-start.18 = (f32[128,256]{1,0:T(8,128)S(1)}, f32[128,256]{1,0:T(8,128)S(1)}, u32[]{:S(2)}, u32[]{:S(2)}) collective-permute-start(f32[128,256]{1,0:T(8,128)S(1)} %add.61), channel_id=1, source_target_pairs={{0,16},{4,68},{8,24},{12,76},{16,0},{20,84},{24,8},{28,92},{32,48}... | collective-permute-start | bytes 393224 | tf_op jit(solution)/shard_map/cross_first/ppermute | solution.py:228
  85.3 1.9 %collective-permute-done.18 = f32[128,256]{1,0:T(8,128)S(1)} collective-permute-done((f32[128,256]{1,0:T(8,128)S(1)}, f32[128,256]{1,0:T(8,128)S(1)}, u32[]{:S(2)}, u32[]{:S(2)}) %collective-permute-start.18) | collective-permute-done | bytes 131104 | tf_op jit(solution)/shard_map/cross_first/ppermute | solution.py:228
  87.2 2.7 %collective-permute-done.17 = f32[128,256]{1,0:T(8,128)S(1)} collective-permute-done((f32[128,256]{1,0:T(8,128)S(1)}, f32[128,256]{1,0:T(8,128)S(1)}, u32[]{:S(2)}, u32[]{:S(2)}) %collective-permute-start.17) | collective-permute-done | bytes 131104 | tf_op jit(solution)/shard_map/cross_first/ppermute | solution.py:228
  89.9 2.8 %collective-permute-start.21 = (f32[128,256]{1,0:T(8,128)S(1)}, f32[128,256]{1,0:T(8,128)S(1)}, u32[]{:S(2)}, u32[]{:S(2)}) collective-permute-start(f32[128,256]{1,0:T(8,128)S(1)} %add_add_fusion.1), channel_id=1, source_target_pairs={{0,64},{4,20},{8,72},{12,28},{16,80},{20,4},{24,88},{28,12},{32,96... | collective-permute-start | bytes 393224 | tf_op jit(solution)/shard_map/cross_second/ppermute | solution.py:228
  93.6 2.0 %collective-permute-done.21 = f32[128,256]{1,0:T(8,128)S(1)} collective-permute-done((f32[128,256]{1,0:T(8,128)S(1)}, f32[128,256]{1,0:T(8,128)S(1)}, u32[]{:S(2)}, u32[]{:S(2)}) %collective-permute-start.21) | collective-permute-done | bytes 131104 | tf_op jit(solution)/shard_map/cross_second/ppermute | solution.py:228
  95.6 2.2 %collective-permute-done.20 = f32[128,256]{1,0:T(8,128)S(1)} collective-permute-done((f32[128,256]{1,0:T(8,128)S(1)}, f32[128,256]{1,0:T(8,128)S(1)}, u32[]{:S(2)}, u32[]{:S(2)}) %collective-permute-start.20) | collective-permute-done | bytes 131104 | tf_op jit(solution)/shard_map/cross_second/ppermute | solution.py:228
  97.8 3.3 %collective-permute-start.22 = (f32[128,256]{1,0:T(8,128)S(1)}, f32[128,256]{1,0:T(8,128)S(1)}, u32[]{:S(2)}, u32[]{:S(2)}) collective-permute-start(f32[128,256]{1,0:T(8,128)S(1)} %add_add_fusion.refs_0_), channel_id=1, source_target_pairs={{0,4},{4,0},{8,12},{12,8},{16,20},{20,16},{24,28},{28,24},{32,36},... | collective-permute-start | bytes 393224 | tf_op jit(solution)/shard_map/cross_join/ppermute | solution.py:228
  101.1 1.0 collective-permute-done.22.refs_1_
  102.1 6.3 %shard_map.54 = (f32[8192,256]{1,0:T(8,128)}, f32[256,256]{1,0:T(8,128)}) custom-call(f32[128,256]{1,0:T(8,128)S(1)} %add_add_fusion.refs_0_, f32[128,256]{1,0:T(8,128)S(1)} %collective-permute-done.22.refs_1_, f32[256,256]{1,0:T(8,128)S(1)} %get-tuple-element.27.refs_2_, f32[256,256]{1,0:T(8,128)S(1)} %get-tuple-element.28.refs_3_, ...), custom_call_target="tpu_custom_call" | custom-call | tf_op jit(solution)/shard_map/pallas_call | solution.py:133
  (38 shorter events, 5.4 us)
Async XLA Ops:
  0.6 49.2 %collective-permute-start.13 = (f32[2048,256]{1,0:T(8,128)}, f32[2048,256]{1,0:T(8,128)S(1)}, u32[]{:S(2)}, u32[]{:S(2)}) collective-permute-start(f32[2048,256]{1,0:T(8,128)} %refs_4_.1), channel_id=1, source_target_pairs={{0,3},{1,0},{2,1},{3,2},{4,7},{5,4},{6,5},{7,6},{8,11},{9,8},{10,9... | collective-permute-start | bytes 6291464 | tf_op jit(solution)/shard_map/right/ppermute | solution.py:228
  4.3 49.5 %collective-permute-start.11 = (f32[2048,256]{1,0:T(8,128)}, f32[2048,256]{1,0:T(8,128)S(1)}, u32[]{:S(2)}, u32[]{:S(2)}) collective-permute-start(f32[2048,256]{1,0:T(8,128)} %refs_4_.1), channel_id=1, source_target_pairs={{0,1},{1,2},{2,3},{3,0},{4,5},{5,6},{6,7},{7,4},{8,9},{9,10},{10,1... | collective-permute-start | bytes 6291464 | tf_op jit(solution)/shard_map/left/ppermute | solution.py:228
  4.3 1.7 %copy-start = (f32[2048,256]{1,0:T(8,128)S(1)}, f32[2048,256]{1,0:T(8,128)}, u32[]{:S(2)}) copy-start(f32[2048,256]{1,0:T(8,128)} %refs_4_.1) | copy-start | bytes 6291460
  8.0 2.0 %collective-permute-start = (f32[192,128]{1,0:T(8,128)S(1)}, f32[192,128]{1,0:T(8,128)S(1)}, u32[]{:S(2)}, u32[]{:S(2)}) collective-permute-start(f32[192,128]{1,0:T(8,128)S(1)} %get-tuple-element.18), channel_id=1, source_target_pairs={{0,4},{4,0},{8,12},{12,8},{16,20},{20,16},{24,28},{28,24},{32,36},... | collective-permute-start | bytes 294920 | tf_op jit(solution)/shard_map/gram_halves/ppermute | solution.py:228
  10.0 6.0 %collective-permute-start.3 = (f32[192,128]{1,0:T(8,128)S(1)}, f32[192,128]{1,0:T(8,128)S(1)}, u32[]{:S(2)}, u32[]{:S(2)}) collective-permute-start(f32[192,128]{1,0:T(8,128)S(1)} %add.51), channel_id=1, source_target_pairs={{0,16},{4,68},{8,24},{12,76},{16,0},{20,84},{24,8},{28,92},{32,48}... | collective-permute-start | bytes 294920 | tf_op jit(solution)/shard_map/gram_first/ppermute | solution.py:228
  13.7 5.0 %collective-permute-start.2 = (f32[192,128]{1,0:T(8,128)S(1)}, f32[192,128]{1,0:T(8,128)S(1)}, u32[]{:S(2)}, u32[]{:S(2)}) collective-permute-start(f32[192,128]{1,0:T(8,128)S(1)} %add.51), channel_id=1, source_target_pairs={{0,24},{4,100},{8,16},{12,108},{16,8},{20,116},{24,0},{28,124},{32... | collective-permute-start | bytes 294920 | tf_op jit(solution)/shard_map/gram_first/ppermute | solution.py:228
  14.1 4.5 %collective-permute-start.1 = (f32[192,128]{1,0:T(8,128)S(1)}, f32[192,128]{1,0:T(8,128)S(1)}, u32[]{:S(2)}, u32[]{:S(2)}) collective-permute-start(f32[192,128]{1,0:T(8,128)S(1)} %add.51), channel_id=1, source_target_pairs={{0,8},{4,36},{8,0},{12,44},{16,24},{20,52},{24,16},{28,60},{32,40}... | collective-permute-start | bytes 294920 | tf_op jit(solution)/shard_map/gram_first/ppermute | solution.py:228
  18.7 5.1 %collective-permute-start.6 = (f32[192,128]{1,0:T(8,128)S(1)}, f32[192,128]{1,0:T(8,128)S(1)}, u32[]{:S(2)}, u32[]{:S(2)}) collective-permute-start(f32[192,128]{1,0:T(8,128)S(1)} %add_add_fusion.4), channel_id=1, source_target_pairs={{0,64},{4,20},{8,72},{12,28},{16,80},{20,4},{24,88},{28,12},{32,96... | collective-permute-start | bytes 294920 | tf_op jit(solution)/shard_map/gram_second/ppermute | solution.py:228
  21.5 5.0 %collective-permute-start.5 = (f32[192,128]{1,0:T(8,128)S(1)}, f32[192,128]{1,0:T(8,128)S(1)}, u32[]{:S(2)}, u32[]{:S(2)}) collective-permute-start(f32[192,128]{1,0:T(8,128)S(1)} %add_add_fusion.4), channel_id=1, source_target_pairs={{0,96},{4,28},{8,104},{12,20},{16,112},{20,12},{24,120},{28,4},{32... | collective-permute-start | bytes 294920 | tf_op jit(solution)/shard_map/gram_second/ppermute | solution.py:228
  22.4 4.1 %collective-permute-start.4 = (f32[192,128]{1,0:T(8,128)S(1)}, f32[192,128]{1,0:T(8,128)S(1)}, u32[]{:S(2)}, u32[]{:S(2)}) collective-permute-start(f32[192,128]{1,0:T(8,128)S(1)} %add_add_fusion.4), channel_id=1, source_target_pairs={{0,32},{4,12},{8,40},{12,4},{16,48},{20,28},{24,56},{28,20},{32,0}... | collective-permute-start | bytes 294920 | tf_op jit(solution)/shard_map/gram_second/ppermute | solution.py:228
  26.5 27.4 %collective-permute-start.9 = (f32[192,128]{1,0:T(8,128)S(1)}, f32[192,128]{1,0:T(8,128)S(1)}, u32[]{:S(2)}, u32[]{:S(2)}) collective-permute-start(f32[192,128]{1,0:T(8,128)S(1)} %add_add_fusion.3), channel_id=1, source_target_pairs={{0,2},{1,3},{2,0},{3,1},{4,6},{5,7},{6,4},{7,5},{8,10},{9,11},{10,... | collective-permute-start | bytes 294920 | tf_op jit(solution)/shard_map/gram_cols/ppermute | solution.py:228
  27.9 26.0 %collective-permute-start.8 = (f32[192,128]{1,0:T(8,128)S(1)}, f32[192,128]{1,0:T(8,128)S(1)}, u32[]{:S(2)}, u32[]{:S(2)}) collective-permute-start(f32[192,128]{1,0:T(8,128)S(1)} %add_add_fusion.3), channel_id=1, source_target_pairs={{0,3},{1,0},{2,1},{3,2},{4,7},{5,4},{6,5},{7,6},{8,11},{9,8},{10,9... | collective-permute-start | bytes 294920 | tf_op jit(solution)/shard_map/gram_cols/ppermute | solution.py:228
  29.6 26.5 %collective-permute-start.7 = (f32[192,128]{1,0:T(8,128)S(1)}, f32[192,128]{1,0:T(8,128)S(1)}, u32[]{:S(2)}, u32[]{:S(2)}) collective-permute-start(f32[192,128]{1,0:T(8,128)S(1)} %add_add_fusion.3), channel_id=1, source_target_pairs={{0,1},{1,2},{2,3},{3,0},{4,5},{5,6},{6,7},{7,4},{8,9},{9,10},{10,1... | collective-permute-start | bytes 294920 | tf_op jit(solution)/shard_map/gram_cols/ppermute | solution.py:228
  49.9 24.4 %collective-permute-start.14 = (f32[1088,256]{1,0:T(8,128)S(1)}, f32[1088,256]{1,0:T(8,128)S(1)}, u32[]{:S(2)}, u32[]{:S(2)}) collective-permute-start(f32[1088,256]{1,0:T(8,128)S(1)} %slice.7), channel_id=1, source_target_pairs={{0,3},{1,0},{2,1},{3,2},{4,7},{5,4},{6,5},{7,6},{8,11},{9,8},{10,9... | collective-permute-start | bytes 3342344 | tf_op jit(solution)/shard_map/far2/ppermute | solution.py:228
  53.8 21.2 %collective-permute-start.12 = (f32[960,256]{1,0:T(8,128)S(1)}, f32[960,256]{1,0:T(8,128)S(1)}, u32[]{:S(2)}, u32[]{:S(2)}) collective-permute-start(f32[960,256]{1,0:T(8,128)S(1)} %slice.6), channel_id=1, source_target_pairs={{0,1},{1,2},{2,3},{3,0},{4,5},{5,6},{6,7},{7,4},{8,9},{9,10},{10,1... | collective-permute-start | bytes 2949128 | tf_op jit(solution)/shard_map/far1/ppermute | solution.py:228
  56.1 13.1 %slice-start = ((s8[8388608]{0:T(1024)(128)(4,1)}), s8[4194304]{0:T(1024)(128)(4,1)S(1)}, s32[]{:S(2)}) async-start(s8[8388608]{0:T(1024)(128)(4,1)} %bitcast), calls=%async_computation | async-start | bytes 8388608
  56.1 13.1 %slice-start.1 = ((s8[8388608]{0:T(1024)(128)(4,1)}), s8[4194304]{0:T(1024)(128)(4,1)S(1)}, s32[]{:S(2)}) async-start(s8[8388608]{0:T(1024)(128)(4,1)} %bitcast), calls=%async_computation.1 | async-start | bytes 8388608
  56.1 13.1 %copy-start.1 = (f32[2048,256]{1,0:T(8,128)S(1)}, f32[2048,256]{1,0:T(8,128)}, u32[]{:S(2)}) copy-start(f32[2048,256]{1,0:T(8,128)} %refs_4_.1) | copy-start | bytes 6291460
  56.1 3.1 %collective-permute-start.10 = (f32[192,128]{1,0:T(8,128)S(1)}, f32[192,128]{1,0:T(8,128)S(1)}, u32[]{:S(2)}, u32[]{:S(2)}) collective-permute-start(f32[192,128]{1,0:T(8,128)S(1)} %add_add_fusion.2.refs_0_), channel_id=1, source_target_pairs={{0,4},{4,0},{8,12},{12,8},{16,20},{20,16},{24,28},{28,24},{32,36},... | collective-permute-start | bytes 294920 | tf_op jit(solution)/shard_map/gram_join/ppermute | solution.py:228
  75.6 5.4 %collective-permute-start.15 = (f32[128,256]{1,0:T(8,128)S(1)}, f32[128,256]{1,0:T(8,128)S(1)}, u32[]{:S(2)}, u32[]{:S(2)}) collective-permute-start(f32[128,256]{1,0:T(8,128)S(1)} %get-tuple-element.26), channel_id=1, source_target_pairs={{0,4},{4,0},{8,12},{12,8},{16,20},{20,16},{24,28},{28,24},{32,36},... | collective-permute-start | bytes 393224 | tf_op jit(solution)/shard_map/cross_halves/ppermute | solution.py:228
  81.0 6.3 %collective-permute-start.18 = (f32[128,256]{1,0:T(8,128)S(1)}, f32[128,256]{1,0:T(8,128)S(1)}, u32[]{:S(2)}, u32[]{:S(2)}) collective-permute-start(f32[128,256]{1,0:T(8,128)S(1)} %add.61), channel_id=1, source_target_pairs={{0,16},{4,68},{8,24},{12,76},{16,0},{20,84},{24,8},{28,92},{32,48}... | collective-permute-start | bytes 393224 | tf_op jit(solution)/shard_map/cross_first/ppermute | solution.py:228
  84.6 5.3 %collective-permute-start.17 = (f32[128,256]{1,0:T(8,128)S(1)}, f32[128,256]{1,0:T(8,128)S(1)}, u32[]{:S(2)}, u32[]{:S(2)}) collective-permute-start(f32[128,256]{1,0:T(8,128)S(1)} %add.61), channel_id=1, source_target_pairs={{0,24},{4,100},{8,16},{12,108},{16,8},{20,116},{24,0},{28,124},{32... | collective-permute-start | bytes 393224 | tf_op jit(solution)/shard_map/cross_first/ppermute | solution.py:228
  85.0 4.9 %collective-permute-start.16 = (f32[128,256]{1,0:T(8,128)S(1)}, f32[128,256]{1,0:T(8,128)S(1)}, u32[]{:S(2)}, u32[]{:S(2)}) collective-permute-start(f32[128,256]{1,0:T(8,128)S(1)} %add.61), channel_id=1, source_target_pairs={{0,8},{4,36},{8,0},{12,44},{16,24},{20,52},{24,16},{28,60},{32,40}... | collective-permute-start | bytes 393224 | tf_op jit(solution)/shard_map/cross_first/ppermute | solution.py:228
  89.9 5.6 %collective-permute-start.21 = (f32[128,256]{1,0:T(8,128)S(1)}, f32[128,256]{1,0:T(8,128)S(1)}, u32[]{:S(2)}, u32[]{:S(2)}) collective-permute-start(f32[128,256]{1,0:T(8,128)S(1)} %add_add_fusion.1), channel_id=1, source_target_pairs={{0,64},{4,20},{8,72},{12,28},{16,80},{20,4},{24,88},{28,12},{32,96... | collective-permute-start | bytes 393224 | tf_op jit(solution)/shard_map/cross_second/ppermute | solution.py:228
  92.7 5.0 %collective-permute-start.20 = (f32[128,256]{1,0:T(8,128)S(1)}, f32[128,256]{1,0:T(8,128)S(1)}, u32[]{:S(2)}, u32[]{:S(2)}) collective-permute-start(f32[128,256]{1,0:T(8,128)S(1)} %add_add_fusion.1), channel_id=1, source_target_pairs={{0,96},{4,28},{8,104},{12,20},{16,112},{20,12},{24,120},{28,4},{32... | collective-permute-start | bytes 393224 | tf_op jit(solution)/shard_map/cross_second/ppermute | solution.py:228
  93.6 4.2 %collective-permute-start.19 = (f32[128,256]{1,0:T(8,128)S(1)}, f32[128,256]{1,0:T(8,128)S(1)}, u32[]{:S(2)}, u32[]{:S(2)}) collective-permute-start(f32[128,256]{1,0:T(8,128)S(1)} %add_add_fusion.1), channel_id=1, source_target_pairs={{0,32},{4,12},{8,40},{12,4},{16,48},{20,28},{24,56},{28,20},{32,0}... | collective-permute-start | bytes 393224 | tf_op jit(solution)/shard_map/cross_second/ppermute | solution.py:228
  97.8 4.3 %collective-permute-start.22 = (f32[128,256]{1,0:T(8,128)S(1)}, f32[128,256]{1,0:T(8,128)S(1)}, u32[]{:S(2)}, u32[]{:S(2)}) collective-permute-start(f32[128,256]{1,0:T(8,128)S(1)} %add_add_fusion.refs_0_), channel_id=1, source_target_pairs={{0,4},{4,0},{8,12},{12,8},{16,20},{20,16},{24,28},{28,24},{32,36},... | collective-permute-start | bytes 393224 | tf_op jit(solution)/shard_map/cross_join/ppermute | solution.py:228

commit v6 on v5

--- a/solution.py
+++ b/solution.py
@@ -101,13 +101,33 @@
     return pl.ds(pl.multiple_of(lax.rem(column + offset, 4) * chunk + low, 64), count)
 
 
-def update_kernel(shrink, blocks, chunk, mine, other, inverse, gram_inverse, *refs):
+def times(square, half, top):
+    columns = jnp.where(top, square[:, :128], square[:, 128:])
+    return contract(columns, half[...], ((1,), (0,)), HIGHEST)
+
+
+def begin_kernel(mine, inverse, gram_inverse, weights_mine, coupling_mine):
+    _, first = whereabouts()
+    weights_mine[...] = times(gram_inverse, mine, first)
+    coupling_mine[...] = times(inverse, mine, first)
+
+
+def begin(mine, inverse, gram_inverse):
+    vmem = pl.BlockSpec(memory_space=pltpu.VMEM)
+    return pl.pallas_call(
+        begin_kernel,
+        out_shape=[jax.ShapeDtypeStruct((256, 256), F32)] * 2,
+        in_specs=[vmem] * 3,
+        out_specs=[vmem] * 2,
+        compiler_params=pltpu.CompilerParams(vmem_limit_bytes=CROSS_VMEM),
+    )(mine, inverse, gram_inverse)
+
+
+def update_kernel(shrink, blocks, chunk, weights_mine, coupling_mine, other, inverse, gram_inverse, *refs):
     *pieces, trailing, updated, r_cross, result, weights, sems = refs
     column, first = whereabouts()
-    top = jnp.where(first, mine[...], other[...])
-    bottom = jnp.where(first, other[...], mine[...])
-    cross = jnp.concatenate([top, bottom], axis=0)
-    weights[:256, :], weights[256:, :] = split(contract(gram_inverse[...], cross, ((1,), (0,)), HIGHEST))
+    full = weights_mine[...] + times(gram_inverse, other, ~first)
+    weights[:256, :], weights[256:, :] = split(full)
     stores, done = [], 0
     for n, (piece, row, offset, low_row, count) in enumerate(blocks):
         rows = rows_at(column, offset, low_row, chunk, count)
@@ -121,19 +141,19 @@
         store = pltpu.make_async_copy(result.at[here], updated.at[rows], sems.at[n])
         store.start()
         stores.append(store)
-    r_cross[...] = contract(inverse[...], cross, ((1,), (0,)), HIGHEST) * shrink
+    r_cross[...] = (coupling_mine[...] + times(inverse, other, ~first)) * shrink
     for store in stores:
         store.wait()
 
 
-def update(mine, other, inverse, gram_inverse, pieces, spots, trailing, shrink, block):
+def update(begun, other, inverse, gram_inverse, pieces, spots, trailing, shrink, block):
     blocks = blocks_of(spots, block)
     vmem, anywhere = pl.BlockSpec(memory_space=pltpu.VMEM), pl.BlockSpec(memory_space=pl.ANY)
     total = trailing.shape[0]
     return pl.pallas_call(
         lambda *refs: update_kernel(shrink, blocks, total // 4, *refs),
         out_shape=[jax.ShapeDtypeStruct(trailing.shape, F32), jax.ShapeDtypeStruct((256, 256), F32)],
-        in_specs=[vmem] * (len(pieces) + 5),
+        in_specs=[vmem] * (len(pieces) + 6),
         out_specs=[anywhere, vmem],
         scratch_shapes=[
             pltpu.VMEM((total, 256), F32),
@@ -141,7 +161,7 @@
             pltpu.SemaphoreType.DMA((len(blocks),)),
         ],
         compiler_params=pltpu.CompilerParams(vmem_limit_bytes=UPDATE_VMEM),
-    )(mine, other, inverse, gram_inverse, *pieces, trailing)
+    )(*begun, other, inverse, gram_inverse, *pieces, trailing)
 
 
 def cross_kernel(initial, halves, blocks, chunk, *refs):
@@ -267,7 +287,7 @@
     cross = exchange_sum("cross_second", cross, "rows", SECOND)
     pieces = (panel_cols, left, right, far1, far2)
     spots = ((size, 0, 0), (size, 3, 0), (size, 1, 0), (fewer, 2, 0), (size - fewer, 2, fewer))
-    updated, r_cross = update(cross, partner("cross_join", cross), inverse, gram_inverse, pieces, spots, trailing, shrink, 256)
+    updated, r_cross = update(begin(cross, inverse, gram_inverse), partner("cross_join", cross), inverse, gram_inverse, pieces, spots, trailing, shrink, 256)
     return (r_factor, r_cross, updated)
 
 

time: 109 us -> 109 us (level)
  transfers between devices with their start and end apart: 23 -> 23, of which waited for: 15 -> 15; matrix products, arithmetic and copies ran while one was open for 0% -> 0% of each run, Pallas kernels for 14% -> 15%
where the time goes in v6:
time: 109 us; the launch traced here: 108 us
  waiting for transfers between devices  44.7 us (41%)
  starting transfers between devices  38.1 us (35%)
  Pallas kernels  22.8 us (21%)
  local copies, waits for them, and re-layouts  1.81 us (2%)
    ppermute x23, waiting for transfers between devices, move(): return lax.ppermute(part, axis, pairs)  44.7 us
    ppermute x23, starting transfers between devices, move(): return lax.ppermute(part, axis, pairs)  38.1 us
    pallas_call x1, Pallas kernels, factor(): pl.pallas_call(lambda *refs: factor_kernel(shrink, size, group, *refs), o...  9.99 us
    pallas_call x1, Pallas kernels, update(): pl.pallas_call(lambda *refs: update_kernel(shrink, blocks, total // 4, *r...  6.23 us
    pallas_call x3, Pallas kernels, cross_part(): pl.pallas_call(lambda *refs: cross_kernel(bool(given), halves, blocks, tr...  3.94 us
  transfers between devices with their start and end apart: 23, of which 15 were waited for; matrix products, arithmetic and copies ran while one was open for 0% of the time, Pallas kernels for 15%

profile of v6, /device:TPU:1, one launch (start us, length us, event | category | flops | bytes accessed | tf_op | source)
XLA Modules:
  0.0 108.5 jit_solution(7179901790889421688)
XLA Ops:
  0.6 3.6 %collective-permute-start.13 = (f32[2048,256]{1,0:T(8,128)}, f32[2048,256]{1,0:T(8,128)S(1)}, u32[]{:S(2)}, u32[]{:S(2)}) collective-permute-start(f32[2048,256]{1,0:T(8,128)} %refs_5_.1), channel_id=1, source_target_pairs={{0,3},{1,0},{2,1},{3,2},{4,7},{5,4},{6,5},{7,6},{8,11},{9,8},{10,9... | collective-permute-start | bytes 6291464 | tf_op jit(solution)/shard_map/right/ppermute | solution.py:248
  4.3 1.7 %copy-done = f32[2048,256]{1,0:T(8,128)S(1)} copy-done((f32[2048,256]{1,0:T(8,128)S(1)}, f32[2048,256]{1,0:T(8,128)}, u32[]{:S(2)}) %copy-start) | copy-done | bytes 2097176
  5.9 2.1 %shard_map.49 = (f32[192,128]{1,0:T(8,128)S(1)}, f32[192,128]{1,0:T(8,128)S(1)}) custom-call(f32[2048,256]{1,0:T(8,128)S(1)} %copy-done), custom_call_target="tpu_custom_call" | custom-call | tf_op jit(solution)/shard_map/pallas_call | solution.py:215
  8.0 1.0 collective-permute-start
  9.1 0.9 collective-permute-done
  10.0 3.7 %collective-permute-start.3 = (f32[192,128]{1,0:T(8,128)S(1)}, f32[192,128]{1,0:T(8,128)S(1)}, u32[]{:S(2)}, u32[]{:S(2)}) collective-permute-start(f32[192,128]{1,0:T(8,128)S(1)} %add.51), channel_id=1, source_target_pairs={{0,16},{4,68},{8,24},{12,76},{16,0},{20,84},{24,8},{28,92},{32,48}... | collective-permute-start | bytes 294920 | tf_op jit(solution)/shard_map/gram_first/ppermute | solution.py:248
  14.4 1.6 %collective-permute-done.3 = f32[192,128]{1,0:T(8,128)S(1)} collective-permute-done((f32[192,128]{1,0:T(8,128)S(1)}, f32[192,128]{1,0:T(8,128)S(1)}, u32[]{:S(2)}, u32[]{:S(2)}) %collective-permute-start.3) | collective-permute-done | bytes 98336 | tf_op jit(solution)/shard_map/gram_first/ppermute | solution.py:248
  16.0 2.7 %collective-permute-done.2 = f32[192,128]{1,0:T(8,128)S(1)} collective-permute-done((f32[192,128]{1,0:T(8,128)S(1)}, f32[192,128]{1,0:T(8,128)S(1)}, u32[]{:S(2)}, u32[]{:S(2)}) %collective-permute-start.2) | collective-permute-done | bytes 98336 | tf_op jit(solution)/shard_map/gram_first/ppermute | solution.py:248
  18.7 2.8 %collective-permute-start.6 = (f32[192,128]{1,0:T(8,128)S(1)}, f32[192,128]{1,0:T(8,128)S(1)}, u32[]{:S(2)}, u32[]{:S(2)}) collective-permute-start(f32[192,128]{1,0:T(8,128)S(1)} %add_add_fusion.4), channel_id=1, source_target_pairs={{0,64},{4,20},{8,72},{12,28},{16,80},{20,4},{24,88},{28,12},{32,96... | collective-permute-start | bytes 294920 | tf_op jit(solution)/shard_map/gram_second/ppermute | solution.py:248
  21.5 0.9 collective-permute-start.5
  22.4 1.4 %collective-permute-done.6 = f32[192,128]{1,0:T(8,128)S(1)} collective-permute-done((f32[192,128]{1,0:T(8,128)S(1)}, f32[192,128]{1,0:T(8,128)S(1)}, u32[]{:S(2)}, u32[]{:S(2)}) %collective-permute-start.6) | collective-permute-done | bytes 98336 | tf_op jit(solution)/shard_map/gram_second/ppermute | solution.py:248
  23.8 2.7 %collective-permute-done.5 = f32[192,128]{1,0:T(8,128)S(1)} collective-permute-done((f32[192,128]{1,0:T(8,128)S(1)}, f32[192,128]{1,0:T(8,128)S(1)}, u32[]{:S(2)}, u32[]{:S(2)}) %collective-permute-start.5) | collective-permute-done | bytes 98336 | tf_op jit(solution)/shard_map/gram_second/ppermute | solution.py:248
  26.5 1.4 %collective-permute-start.9 = (f32[192,128]{1,0:T(8,128)S(1)}, f32[192,128]{1,0:T(8,128)S(1)}, u32[]{:S(2)}, u32[]{:S(2)}) collective-permute-start(f32[192,128]{1,0:T(8,128)S(1)} %add_add_fusion.3), channel_id=1, source_target_pairs={{0,2},{1,3},{2,0},{3,1},{4,6},{5,7},{6,4},{7,5},{8,10},{9,11},{10,... | collective-permute-start | bytes 294920 | tf_op jit(solution)/shard_map/gram_cols/ppermute | solution.py:248
  27.9 1.7 %collective-permute-start.8 = (f32[192,128]{1,0:T(8,128)S(1)}, f32[192,128]{1,0:T(8,128)S(1)}, u32[]{:S(2)}, u32[]{:S(2)}) collective-permute-start(f32[192,128]{1,0:T(8,128)S(1)} %add_add_fusion.3), channel_id=1, source_target_pairs={{0,3},{1,0},{2,1},{3,2},{4,7},{5,4},{6,5},{7,6},{8,11},{9,8},{10,9... | collective-permute-start | bytes 294920 | tf_op jit(solution)/shard_map/gram_cols/ppermute | solution.py:248
  30.1 19.7 %collective-permute-done.13.refs_2_.refs_7_ = f32[2048,256]{1,0:T(8,128)S(1)} collective-permute-done((f32[2048,256]{1,0:T(8,128)}, f32[2048,256]{1,0:T(8,128)S(1)}, u32[]{:S(2)}, u32[]{:S(2)}) %collective-permute-start.13) | collective-permute-done | bytes 2097184 | tf_op jit(solution)/shard_map/right/ppermute | solution.py:248
  49.9 3.9 %collective-permute-start.14 = (f32[1088,256]{1,0:T(8,128)S(1)}, f32[1088,256]{1,0:T(8,128)S(1)}, u32[]{:S(2)}, u32[]{:S(2)}) collective-permute-start(f32[1088,256]{1,0:T(8,128)S(1)} %slice.7), channel_id=1, source_target_pairs={{0,3},{1,0},{2,1},{3,2},{4,7},{5,4},{6,5},{7,6},{8,11},{9,8},{10,9... | collective-permute-start | bytes 3342344 | tf_op jit(solution)/shard_map/far2/ppermute | solution.py:248
  53.9 2.2 %collective-permute-done.7 = f32[192,128]{1,0:T(8,128)S(1)} collective-permute-done((f32[192,128]{1,0:T(8,128)S(1)}, f32[192,128]{1,0:T(8,128)S(1)}, u32[]{:S(2)}, u32[]{:S(2)}) %collective-permute-start.7) | collective-permute-done | bytes 98336 | tf_op jit(solution)/shard_map/gram_cols/ppermute | solution.py:248
  56.1 2.1 %collective-permute-start.10 = (f32[192,128]{1,0:T(8,128)S(1)}, f32[192,128]{1,0:T(8,128)S(1)}, u32[]{:S(2)}, u32[]{:S(2)}) collective-permute-start(f32[192,128]{1,0:T(8,128)S(1)} %add_add_fusion.2.refs_0_), channel_id=1, source_target_pairs={{0,4},{4,0},{8,12},{12,8},{16,20},{20,16},{24,28},{28,24},{32,36},... | collective-permute-start | bytes 294920 | tf_op jit(solution)/shard_map/gram_join/ppermute | solution.py:248
  58.3 0.9 collective-permute-done.10.refs_1_
  59.2 10.0 %shard_map.50 = (f32[256,256]{1,0:T(8,128)}, f32[256,256]{1,0:T(8,128)S(1)}, f32[256,256]{1,0:T(8,128)S(1)}) custom-call(f32[192,128]{1,0:T(8,128)S(1)} %add_add_fusion.2.refs_0_, f32[192,128]{1,0:T(8,128)S(1)} %collective-permute-done.10.refs_1_), custom_call_target="tpu_custom_call" | custom-call | flops 8000000000 | tf_op jit(solution)/shard_map/pallas_call | solution.py:78
  69.2 2.7 %shard_map.51.refs_0_ = f32[256,256]{1,0:T(8,128)S(1)} custom-call(f32[2048,256]{1,0:T(8,128)S(1)} %copy-done.1, f32[2048,256]{1,0:T(8,128)S(1)} %collective-permute-done.11.refs_1_.refs_6_, f32[2048,256]{1,0:T(8,128)S(1)} %collective-permute-done.13.refs_2_.refs_7_, f32[8192,256]{1,0:T(8,128)S(1)} %bitcast.1), custom_call_target="tpu_custom_call" | custom-call | tf_op jit(solution)/shard_map/pallas_call | solution.py:195
  71.9 2.4 %collective-permute-done.14.refs_1_.refs_9_ = f32[1088,256]{1,0:T(8,128)S(1)} collective-permute-done((f32[1088,256]{1,0:T(8,128)S(1)}, f32[1088,256]{1,0:T(8,128)S(1)}, u32[]{:S(2)}, u32[]{:S(2)}) %collective-permute-start.14) | collective-permute-done | bytes 1114144 | tf_op jit(solution)/shard_map/far2/ppermute | solution.py:248
  75.6 4.4 %collective-permute-start.15 = (f32[128,256]{1,0:T(8,128)S(1)}, f32[128,256]{1,0:T(8,128)S(1)}, u32[]{:S(2)}, u32[]{:S(2)}) collective-permute-start(f32[128,256]{1,0:T(8,128)S(1)} %get-tuple-element.28), channel_id=1, source_target_pairs={{0,4},{4,0},{8,12},{12,8},{16,20},{20,16},{24,28},{28,24},{32,36},... | collective-permute-start | bytes 393224 | tf_op jit(solution)/shard_map/cross_halves/ppermute | solution.py:248
  80.0 1.0 collective-permute-done.15
  81.0 3.6 %collective-permute-start.18 = (f32[128,256]{1,0:T(8,128)S(1)}, f32[128,256]{1,0:T(8,128)S(1)}, u32[]{:S(2)}, u32[]{:S(2)}) collective-permute-start(f32[128,256]{1,0:T(8,128)S(1)} %add.61), channel_id=1, source_target_pairs={{0,16},{4,68},{8,24},{12,76},{16,0},{20,84},{24,8},{28,92},{32,48}... | collective-permute-start | bytes 393224 | tf_op jit(solution)/shard_map/cross_first/ppermute | solution.py:248
  85.3 1.9 %collective-permute-done.18 = f32[128,256]{1,0:T(8,128)S(1)} collective-permute-done((f32[128,256]{1,0:T(8,128)S(1)}, f32[128,256]{1,0:T(8,128)S(1)}, u32[]{:S(2)}, u32[]{:S(2)}) %collective-permute-start.18) | collective-permute-done | bytes 131104 | tf_op jit(solution)/shard_map/cross_first/ppermute | solution.py:248
  87.2 2.7 %collective-permute-done.17 = f32[128,256]{1,0:T(8,128)S(1)} collective-permute-done((f32[128,256]{1,0:T(8,128)S(1)}, f32[128,256]{1,0:T(8,128)S(1)}, u32[]{:S(2)}, u32[]{:S(2)}) %collective-permute-start.17) | collective-permute-done | bytes 131104 | tf_op jit(solution)/shard_map/cross_first/ppermute | solution.py:248
  89.9 2.8 %collective-permute-start.21 = (f32[128,256]{1,0:T(8,128)S(1)}, f32[128,256]{1,0:T(8,128)S(1)}, u32[]{:S(2)}, u32[]{:S(2)}) collective-permute-start(f32[128,256]{1,0:T(8,128)S(1)} %add_add_fusion.1), channel_id=1, source_target_pairs={{0,64},{4,20},{8,72},{12,28},{16,80},{20,4},{24,88},{28,12},{32,96... | collective-permute-start | bytes 393224 | tf_op jit(solution)/shard_map/cross_second/ppermute | solution.py:248
  93.6 2.0 %collective-permute-done.21 = f32[128,256]{1,0:T(8,128)S(1)} collective-permute-done((f32[128,256]{1,0:T(8,128)S(1)}, f32[128,256]{1,0:T(8,128)S(1)}, u32[]{:S(2)}, u32[]{:S(2)}) %collective-permute-start.21) | collective-permute-done | bytes 131104 | tf_op jit(solution)/shard_map/cross_second/ppermute | solution.py:248
  95.6 2.2 %collective-permute-done.20 = f32[128,256]{1,0:T(8,128)S(1)} collective-permute-done((f32[128,256]{1,0:T(8,128)S(1)}, f32[128,256]{1,0:T(8,128)S(1)}, u32[]{:S(2)}, u32[]{:S(2)}) %collective-permute-start.20) | collective-permute-done | bytes 131104 | tf_op jit(solution)/shard_map/cross_second/ppermute | solution.py:248
  97.8 3.3 %collective-permute-start.22 = (f32[128,256]{1,0:T(8,128)S(1)}, f32[128,256]{1,0:T(8,128)S(1)}, u32[]{:S(2)}, u32[]{:S(2)}) collective-permute-start(f32[128,256]{1,0:T(8,128)S(1)} %add_add_fusion.mine), channel_id=1, source_target_pairs={{0,4},{4,0},{8,12},{12,8},{16,20},{20,16},{24,28},{28,24},{32,36},... | collective-permute-start | bytes 393224 | tf_op jit(solution)/shard_map/cross_join/ppermute | solution.py:248
  102.1 6.2 %shard_map.55 = (f32[8192,256]{1,0:T(8,128)}, f32[256,256]{1,0:T(8,128)}) custom-call(f32[256,256]{1,0:T(8,128)S(1)} %get-tuple-element.31.refs_0_, f32[256,256]{1,0:T(8,128)S(1)} %get-tuple-element.32.refs_1_, f32[128,256]{1,0:T(8,128)S(1)} %collective-permute-done.22.refs_2_, f32[256,256]{1,0:T(8,128)S(1)} %get-tuple-element.29.inverse.refs_3_, ...), custom_call_target="tpu_custom_call" | custom-call | tf_op jit(solution)/shard_map/pallas_call | solution.py:153
  (39 shorter events, 5.5 us)
Async XLA Ops:
  0.6 49.2 %collective-permute-start.13 = (f32[2048,256]{1,0:T(8,128)}, f32[2048,256]{1,0:T(8,128)S(1)}, u32[]{:S(2)}, u32[]{:S(2)}) collective-permute-start(f32[2048,256]{1,0:T(8,128)} %refs_5_.1), channel_id=1, source_target_pairs={{0,3},{1,0},{2,1},{3,2},{4,7},{5,4},{6,5},{7,6},{8,11},{9,8},{10,9... | collective-permute-start | bytes 6291464 | tf_op jit(solution)/shard_map/right/ppermute | solution.py:248
  4.3 49.5 %collective-permute-start.11 = (f32[2048,256]{1,0:T(8,128)}, f32[2048,256]{1,0:T(8,128)S(1)}, u32[]{:S(2)}, u32[]{:S(2)}) collective-permute-start(f32[2048,256]{1,0:T(8,128)} %refs_5_.1), channel_id=1, source_target_pairs={{0,1},{1,2},{2,3},{3,0},{4,5},{5,6},{6,7},{7,4},{8,9},{9,10},{10,1... | collective-permute-start | bytes 6291464 | tf_op jit(solution)/shard_map/left/ppermute | solution.py:248
  4.3 1.7 %copy-start = (f32[2048,256]{1,0:T(8,128)S(1)}, f32[2048,256]{1,0:T(8,128)}, u32[]{:S(2)}) copy-start(f32[2048,256]{1,0:T(8,128)} %refs_5_.1) | copy-start | bytes 6291460
  8.0 2.0 %collective-permute-start = (f32[192,128]{1,0:T(8,128)S(1)}, f32[192,128]{1,0:T(8,128)S(1)}, u32[]{:S(2)}, u32[]{:S(2)}) collective-permute-start(f32[192,128]{1,0:T(8,128)S(1)} %get-tuple-element.20), channel_id=1, source_target_pairs={{0,4},{4,0},{8,12},{12,8},{16,20},{20,16},{24,28},{28,24},{32,36},... | collective-permute-start | bytes 294920 | tf_op jit(solution)/shard_map/gram_halves/ppermute | solution.py:248
  10.0 6.0 %collective-permute-start.3 = (f32[192,128]{1,0:T(8,128)S(1)}, f32[192,128]{1,0:T(8,128)S(1)}, u32[]{:S(2)}, u32[]{:S(2)}) collective-permute-start(f32[192,128]{1,0:T(8,128)S(1)} %add.51), channel_id=1, source_target_pairs={{0,16},{4,68},{8,24},{12,76},{16,0},{20,84},{24,8},{28,92},{32,48}... | collective-permute-start | bytes 294920 | tf_op jit(solution)/shard_map/gram_first/ppermute | solution.py:248
  13.7 5.0 %collective-permute-start.2 = (f32[192,128]{1,0:T(8,128)S(1)}, f32[192,128]{1,0:T(8,128)S(1)}, u32[]{:S(2)}, u32[]{:S(2)}) collective-permute-start(f32[192,128]{1,0:T(8,128)S(1)} %add.51), channel_id=1, source_target_pairs={{0,24},{4,100},{8,16},{12,108},{16,8},{20,116},{24,0},{28,124},{32... | collective-permute-start | bytes 294920 | tf_op jit(solution)/shard_map/gram_first/ppermute | solution.py:248
  14.1 4.5 %collective-permute-start.1 = (f32[192,128]{1,0:T(8,128)S(1)}, f32[192,128]{1,0:T(8,128)S(1)}, u32[]{:S(2)}, u32[]{:S(2)}) collective-permute-start(f32[192,128]{1,0:T(8,128)S(1)} %add.51), channel_id=1, source_target_pairs={{0,8},{4,36},{8,0},{12,44},{16,24},{20,52},{24,16},{28,60},{32,40}... | collective-permute-start | bytes 294920 | tf_op jit(solution)/shard_map/gram_first/ppermute | solution.py:248
  18.7 5.1 %collective-permute-start.6 = (f32[192,128]{1,0:T(8,128)S(1)}, f32[192,128]{1,0:T(8,128)S(1)}, u32[]{:S(2)}, u32[]{:S(2)}) collective-permute-start(f32[192,128]{1,0:T(8,128)S(1)} %add_add_fusion.4), channel_id=1, source_target_pairs={{0,64},{4,20},{8,72},{12,28},{16,80},{20,4},{24,88},{28,12},{32,96... | collective-permute-start | bytes 294920 | tf_op jit(solution)/shard_map/gram_second/ppermute | solution.py:248
  21.5 5.0 %collective-permute-start.5 = (f32[192,128]{1,0:T(8,128)S(1)}, f32[192,128]{1,0:T(8,128)S(1)}, u32[]{:S(2)}, u32[]{:S(2)}) collective-permute-start(f32[192,128]{1,0:T(8,128)S(1)} %add_add_fusion.4), channel_id=1, source_target_pairs={{0,96},{4,28},{8,104},{12,20},{16,112},{20,12},{24,120},{28,4},{32... | collective-permute-start | bytes 294920 | tf_op jit(solution)/shard_map/gram_second/ppermute | solution.py:248
  22.4 4.1 %collective-permute-start.4 = (f32[192,128]{1,0:T(8,128)S(1)}, f32[192,128]{1,0:T(8,128)S(1)}, u32[]{:S(2)}, u32[]{:S(2)}) collective-permute-start(f32[192,128]{1,0:T(8,128)S(1)} %add_add_fusion.4), channel_id=1, source_target_pairs={{0,32},{4,12},{8,40},{12,4},{16,48},{20,28},{24,56},{28,20},{32,0}... | collective-permute-start | bytes 294920 | tf_op jit(solution)/shard_map/gram_second/ppermute | solution.py:248
  26.5 27.4 %collective-permute-start.9 = (f32[192,128]{1,0:T(8,128)S(1)}, f32[192,128]{1,0:T(8,128)S(1)}, u32[]{:S(2)}, u32[]{:S(2)}) collective-permute-start(f32[192,128]{1,0:T(8,128)S(1)} %add_add_fusion.3), channel_id=1, source_target_pairs={{0,2},{1,3},{2,0},{3,1},{4,6},{5,7},{6,4},{7,5},{8,10},{9,11},{10,... | collective-permute-start | bytes 294920 | tf_op jit(solution)/shard_map/gram_cols/ppermute | solution.py:248
  27.9 26.0 %collective-permute-start.8 = (f32[192,128]{1,0:T(8,128)S(1)}, f32[192,128]{1,0:T(8,128)S(1)}, u32[]{:S(2)}, u32[]{:S(2)}) collective-permute-start(f32[192,128]{1,0:T(8,128)S(1)} %add_add_fusion.3), channel_id=1, source_target_pairs={{0,3},{1,0},{2,1},{3,2},{4,7},{5,4},{6,5},{7,6},{8,11},{9,8},{10,9... | collective-permute-start | bytes 294920 | tf_op jit(solution)/shard_map/gram_cols/ppermute | solution.py:248
  29.6 26.5 %collective-permute-start.7 = (f32[192,128]{1,0:T(8,128)S(1)}, f32[192,128]{1,0:T(8,128)S(1)}, u32[]{:S(2)}, u32[]{:S(2)}) collective-permute-start(f32[192,128]{1,0:T(8,128)S(1)} %add_add_fusion.3), channel_id=1, source_target_pairs={{0,1},{1,2},{2,3},{3,0},{4,5},{5,6},{6,7},{7,4},{8,9},{9,10},{10,1... | collective-permute-start | bytes 294920 | tf_op jit(solution)/shard_map/gram_cols/ppermute | solution.py:248
  49.9 24.4 %collective-permute-start.14 = (f32[1088,256]{1,0:T(8,128)S(1)}, f32[1088,256]{1,0:T(8,128)S(1)}, u32[]{:S(2)}, u32[]{:S(2)}) collective-permute-start(f32[1088,256]{1,0:T(8,128)S(1)} %slice.7), channel_id=1, source_target_pairs={{0,3},{1,0},{2,1},{3,2},{4,7},{5,4},{6,5},{7,6},{8,11},{9,8},{10,9... | collective-permute-start | bytes 3342344 | tf_op jit(solution)/shard_map/far2/ppermute | solution.py:248
  53.8 21.2 %collective-permute-start.12 = (f32[960,256]{1,0:T(8,128)S(1)}, f32[960,256]{1,0:T(8,128)S(1)}, u32[]{:S(2)}, u32[]{:S(2)}) collective-permute-start(f32[960,256]{1,0:T(8,128)S(1)} %slice.6), channel_id=1, source_target_pairs={{0,1},{1,2},{2,3},{3,0},{4,5},{5,6},{6,7},{7,4},{8,9},{9,10},{10,1... | collective-permute-start | bytes 2949128 | tf_op jit(solution)/shard_map/far1/ppermute | solution.py:248
  56.1 13.1 %slice-start = ((s8[8388608]{0:T(1024)(128)(4,1)}), s8[4194304]{0:T(1024)(128)(4,1)S(1)}, s32[]{:S(2)}) async-start(s8[8388608]{0:T(1024)(128)(4,1)} %bitcast), calls=%async_computation | async-start | bytes 8388608
  56.1 13.1 %slice-start.1 = ((s8[8388608]{0:T(1024)(128)(4,1)}), s8[4194304]{0:T(1024)(128)(4,1)S(1)}, s32[]{:S(2)}) async-start(s8[8388608]{0:T(1024)(128)(4,1)} %bitcast), calls=%async_computation.1 | async-start | bytes 8388608
  56.1 13.1 %copy-start.1 = (f32[2048,256]{1,0:T(8,128)S(1)}, f32[2048,256]{1,0:T(8,128)}, u32[]{:S(2)}) copy-start(f32[2048,256]{1,0:T(8,128)} %refs_5_.1) | copy-start | bytes 6291460
  56.1 3.1 %collective-permute-start.10 = (f32[192,128]{1,0:T(8,128)S(1)}, f32[192,128]{1,0:T(8,128)S(1)}, u32[]{:S(2)}, u32[]{:S(2)}) collective-permute-start(f32[192,128]{1,0:T(8,128)S(1)} %add_add_fusion.2.refs_0_), channel_id=1, source_target_pairs={{0,4},{4,0},{8,12},{12,8},{16,20},{20,16},{24,28},{28,24},{32,36},... | collective-permute-start | bytes 294920 | tf_op jit(solution)/shard_map/gram_join/ppermute | solution.py:248
  75.6 5.4 %collective-permute-start.15 = (f32[128,256]{1,0:T(8,128)S(1)}, f32[128,256]{1,0:T(8,128)S(1)}, u32[]{:S(2)}, u32[]{:S(2)}) collective-permute-start(f32[128,256]{1,0:T(8,128)S(1)} %get-tuple-element.28), channel_id=1, source_target_pairs={{0,4},{4,0},{8,12},{12,8},{16,20},{20,16},{24,28},{28,24},{32,36},... | collective-permute-start | bytes 393224 | tf_op jit(solution)/shard_map/cross_halves/ppermute | solution.py:248
  81.0 6.3 %collective-permute-start.18 = (f32[128,256]{1,0:T(8,128)S(1)}, f32[128,256]{1,0:T(8,128)S(1)}, u32[]{:S(2)}, u32[]{:S(2)}) collective-permute-start(f32[128,256]{1,0:T(8,128)S(1)} %add.61), channel_id=1, source_target_pairs={{0,16},{4,68},{8,24},{12,76},{16,0},{20,84},{24,8},{28,92},{32,48}... | collective-permute-start | bytes 393224 | tf_op jit(solution)/shard_map/cross_first/ppermute | solution.py:248
  84.6 5.3 %collective-permute-start.17 = (f32[128,256]{1,0:T(8,128)S(1)}, f32[128,256]{1,0:T(8,128)S(1)}, u32[]{:S(2)}, u32[]{:S(2)}) collective-permute-start(f32[128,256]{1,0:T(8,128)S(1)} %add.61), channel_id=1, source_target_pairs={{0,24},{4,100},{8,16},{12,108},{16,8},{20,116},{24,0},{28,124},{32... | collective-permute-start | bytes 393224 | tf_op jit(solution)/shard_map/cross_first/ppermute | solution.py:248
  85.0 4.9 %collective-permute-start.16 = (f32[128,256]{1,0:T(8,128)S(1)}, f32[128,256]{1,0:T(8,128)S(1)}, u32[]{:S(2)}, u32[]{:S(2)}) collective-permute-start(f32[128,256]{1,0:T(8,128)S(1)} %add.61), channel_id=1, source_target_pairs={{0,8},{4,36},{8,0},{12,44},{16,24},{20,52},{24,16},{28,60},{32,40}... | collective-permute-start | bytes 393224 | tf_op jit(solution)/shard_map/cross_first/ppermute | solution.py:248
  89.9 5.6 %collective-permute-start.21 = (f32[128,256]{1,0:T(8,128)S(1)}, f32[128,256]{1,0:T(8,128)S(1)}, u32[]{:S(2)}, u32[]{:S(2)}) collective-permute-start(f32[128,256]{1,0:T(8,128)S(1)} %add_add_fusion.1), channel_id=1, source_target_pairs={{0,64},{4,20},{8,72},{12,28},{16,80},{20,4},{24,88},{28,12},{32,96... | collective-permute-start | bytes 393224 | tf_op jit(solution)/shard_map/cross_second/ppermute | solution.py:248
  92.7 5.0 %collective-permute-start.20 = (f32[128,256]{1,0:T(8,128)S(1)}, f32[128,256]{1,0:T(8,128)S(1)}, u32[]{:S(2)}, u32[]{:S(2)}) collective-permute-start(f32[128,256]{1,0:T(8,128)S(1)} %add_add_fusion.1), channel_id=1, source_target_pairs={{0,96},{4,28},{8,104},{12,20},{16,112},{20,12},{24,120},{28,4},{32... | collective-permute-start | bytes 393224 | tf_op jit(solution)/shard_map/cross_second/ppermute | solution.py:248
  93.6 4.2 %collective-permute-start.19 = (f32[128,256]{1,0:T(8,128)S(1)}, f32[128,256]{1,0:T(8,128)S(1)}, u32[]{:S(2)}, u32[]{:S(2)}) collective-permute-start(f32[128,256]{1,0:T(8,128)S(1)} %add_add_fusion.1), channel_id=1, source_target_pairs={{0,32},{4,12},{8,40},{12,4},{16,48},{20,28},{24,56},{28,20},{32,0}... | collective-permute-start | bytes 393224 | tf_op jit(solution)/shard_map/cross_second/ppermute | solution.py:248
  97.8 4.3 %collective-permute-start.22 = (f32[128,256]{1,0:T(8,128)S(1)}, f32[128,256]{1,0:T(8,128)S(1)}, u32[]{:S(2)}, u32[]{:S(2)}) collective-permute-start(f32[128,256]{1,0:T(8,128)S(1)} %add_add_fusion.mine), channel_id=1, source_target_pairs={{0,4},{4,0},{8,12},{12,8},{16,20},{20,16},{24,28},{28,24},{32,36},... | collective-permute-start | bytes 393224 | tf_op jit(solution)/shard_map/cross_join/ppermute | solution.py:248
